TPU v7x, 32 devices: a whole 2x2x4 slice. The times are simulated.
32 devices in a mesh: gx: 2 (over x), gy: 4 (over y, core), gz: 4 (over z).
Axes of the slice: x: 2, y: 2, z: 4, core: 2. Of those that a mesh axis runs over, the one named last changes fastest.
Arguments:
- features: bfloat16 [32, 8, 256, 512], P(None, 'gx', 'gy', 'gz'), may hold values from -6 to 6
- conv_weight: bfloat16 [27, 32], replicated, may hold values from -0.21875 to 0.21875
- mask: int32 [8, 256, 512], P('gx', 'gy', 'gz'), may hold values from 0 to 1, as said below
Outputs:
- score: float32 [8, 256, 512], P('gx', 'gy', 'gz')
- depth: float32 [8, 256, 512], P('gx', 'gy', 'gz')
Inputs may be any that keep to these rules, and one draw needn't show every extreme that they name: `mask`: 1 marks a foreground voxel and 0 a background voxel; every draw holds both.
All inputs are finite; a program needn't handle non-finite values.
Results may differ from a plain program's by a relative error of at most 0.0003.
Values may be sent and summed in bfloat16 or wider, within the bound.
No kernel may reach another device: no remote copies, remote signals or barrier semaphores. Data moves between devices by JAX's collectives and lax.ppermute only.
A program may use at most 128 MiB of HBM per device.

v0:
```python
import functools

import jax
import jax.numpy as jnp
from jax import lax
from jax.experimental import pallas as pl
from jax.experimental.pallas import tpu as pltpu
from jax.sharding import PartitionSpec as P

RADIUS = 128
CEILING = float(RADIUS * RADIUS)
HUGE = 1e30
LANES = 128
ROWS = 24
VMEM = pl.BlockSpec(memory_space=pltpu.VMEM)
HBM = pl.BlockSpec(memory_space=pltpu.HBM)


def call(kernel, outs, scratch=(), mib=8, in_specs=None):
    shapes = [jax.ShapeDtypeStruct(s, jnp.float32) for s in outs]

    def run(*args):
        return pl.pallas_call(
            kernel,
            out_shape=shapes,
            in_specs=in_specs or [VMEM] * len(args),
            out_specs=[VMEM] * len(shapes),
            scratch_shapes=list(scratch),
            compiler_params=pltpu.CompilerParams(vmem_limit_bytes=mib * 1024 * 1024),
        )(*args)

    return run


def lane_of(shape):
    return lax.broadcasted_iota(jnp.int32, shape, len(shape) - 1)


def row_of(shape):
    return lax.broadcasted_iota(jnp.int32, shape, len(shape) - 2)


def cost_of(score):
    return CEILING / (1.0 + jnp.exp(-score))


def conv_kernel(planes, f_hbm, w_hbm, mask_hbm, s_ref, m_ref, e_ref, f_vmem, w_vmem, mask_vmem, w_big, acc, sems):
    channels, size_x, size_y, _ = f_vmem.shape
    tiles = size_y // 16
    depth = channels * 16
    weights = pltpu.make_async_copy(w_hbm, w_vmem, sems.at[size_x])
    weights.start()
    copies = [
        pltpu.make_async_copy(f_hbm.at[:, x], f_vmem.at[:, x], sems.at[x]) for x in range(size_x)
    ]
    for copy in copies:
        copy.start()
    masks = pltpu.make_async_copy(mask_hbm, mask_vmem, sems.at[size_x + 1])
    masks.start()

    acc[...] = jnp.zeros_like(acc)
    spread = (
        lax.broadcasted_iota(jnp.int32, (channels, depth), 1) // 16
        == lax.broadcasted_iota(jnp.int32, (channels, depth), 0)
    ).astype(jnp.bfloat16)
    row = lax.broadcasted_iota(jnp.int32, (ROWS, depth), 0)
    y_in = lax.broadcasted_iota(jnp.int32, (ROWS, depth), 1) % 16
    y_out = jnp.where(row <= 16, row, jnp.where(row == ROWS - 1, -1, 64))
    tap = y_in - y_out + 1
    weights.wait()
    wide = jnp.dot(w_vmem[...], spread, preferred_element_type=jnp.float32)
    blocks = []
    for a in range(3):
        for c in range(3):
            block = jnp.zeros((ROWS, depth), jnp.float32)
            for b in range(3):
                k = 9 * a + 3 * b + c
                block = jnp.where(tap == b, wide[k : k + 1, :], block)
            blocks.append(block)
    blocks.append(jnp.zeros((8, depth), jnp.float32))
    w_big[...] = jnp.concatenate(blocks, axis=0).astype(jnp.bfloat16)

    for x in range(size_x):
        copies[x].wait()
        right = jnp.concatenate(
            [f_vmem[:, x, 16 * t : 16 * t + 16, :].reshape(depth, LANES) for t in range(tiles)],
            axis=1,
        )
        got = jnp.dot(w_big[...], right, preferred_element_type=jnp.float32)
        for a in range(3):
            at = x + 2 - a
            for c in range(3):
                first = (3 * a + c) * ROWS
                acc[at, c] = acc[at, c] + got[first : first + ROWS, :]

    shape = (8, LANES)
    row, lane = row_of(shape), lane_of(shape)
    groups = size_y // 8
    masks.wait()
    for p, at in enumerate(planes()):
        fold = None
        for g in range(groups + 1):
            sums = []
            for c in range(3):

                def piece(tile, low, c=c):
                    return acc[at, c, low : low + 8, tile * LANES : tile * LANES + LANES]

                if g == groups:
                    part = jnp.where(row == 0, piece(tiles - 1, 16), 0.0) + jnp.where(
                        row == 7, piece(0, 16), 0.0
                    )
                else:
                    tile, low = g // 2, 8 * (g % 2)
                    part = piece(tile, low)
                    if low == 0 and tile > 0:
                        part = part + jnp.where(row == 0, piece(tile - 1, 16), 0.0)
                    if low == 8 and tile < tiles - 1:
                        part = part + jnp.where(row == 7, piece(tile + 1, 16), 0.0)
                sums.append(part)
            ahead = pltpu.roll(sums[0], 1, 1)
            behind = pltpu.roll(sums[2], LANES - 1, 1)
            inner = (
                sums[1] + jnp.where(lane == 0, 0.0, ahead) + jnp.where(lane == LANES - 1, 0.0, behind)
            )
            outer = jnp.where(lane == 0, ahead, jnp.where(lane == LANES - 1, behind, 0.0))
            if g == groups:
                e_ref[p, 0:8, :] = inner
                e_ref[p, 8:16, :] = jnp.where(row == 7, pltpu.roll(outer, 2 * (groups - 1), 1), outer)
            else:
                span = slice(8 * g, 8 * g + 8)
                if p < size_x:
                    s_ref[p, span, :] = inner
                    inner = jnp.where(mask_vmem[p, span, :] == 1, HUGE, inner)
                m_ref[p, span, :] = inner
                fold = outer if g == 0 else fold + pltpu.roll(outer, 2 * g, 1)
        m_ref[p, size_y : size_y + 8, :] = fold


def y_masks(axis, chip):
    row = row_of((8, LANES))
    index, last = lax.axis_index(axis), lax.axis_size(axis) - 1
    odd = index % 2
    if chip:
        low, high = odd == 1, odd == 0
    else:
        low, high = (odd == 0) & (index > 0), (odd == 1) & (index < last)
    return row == jnp.where(low, 0, -1), row == jnp.where(high, 7, -1)


def edge_rows(masks, part, size_y):
    low, high = masks
    return jnp.concatenate(
        [
            jnp.where(low, part, 0.0),
            jnp.zeros((size_y - 16, LANES), jnp.float32),
            jnp.where(high, part, 0.0),
        ],
        axis=0,
    )


def edge_fold(masks, part):
    low, high = masks
    return jnp.where(low, part, jnp.where(high, part, 0.0))


def turn_kernel(s_ref, own_ref, far_ref, chip_ref, cross_ref, xchip_ref, xcross_ref, score_ref, zm_ref):
    size_x, size_y, _ = s_ref.shape
    rows, fold = slice(0, size_y), slice(size_y, size_y + 8)
    chip, cross = y_masks("gy", True), y_masks("gy", False)
    first = lax.axis_index("gx") == 0
    lane = lane_of((size_y, LANES))
    border = (lane == 0) | (lane == LANES - 1)
    faces_own = {size_x - 1: jnp.where(first, 1.0, 0.0), 0: jnp.where(first, 0.0, 1.0)}
    faces_far = {0: faces_own[size_x - 1], size_x - 1: faces_own[0]}

    def complete(p, base, folded, face_ref, sides, faces):
        if p in faces:
            base = base + faces[p] * face_ref[size_x, rows]
            folded = folded + faces[p] * face_ref[size_x, fold]
        for masks, same, other in sides:
            part, part_h = same[p, 0:8], same[p, 8:16]
            if p in faces:
                part = part + faces[p] * other[size_x, 0:8]
                part_h = part_h + faces[p] * other[size_x, 8:16]
            base = base + edge_rows(masks, part, size_y)
            folded = folded + edge_fold(masks, part_h)
        return base, folded

    costs, turned = [], []
    for far in range(2):
        for p in range(size_x):
            if far:
                sides = ((chip, xchip_ref, chip_ref), (cross, xcross_ref, cross_ref))
                masked, h = complete(p, far_ref[p, rows], far_ref[p, fold], own_ref, sides, faces_far)
            else:
                sides = ((chip, chip_ref, xchip_ref), (cross, cross_ref, xcross_ref))
                full, h = complete(p, s_ref[p], own_ref[p, fold], far_ref, sides, faces_own)
                score_ref[p] = full
                masked = jnp.where(own_ref[p, rows] == HUGE, HUGE, full)
            costs.append(cost_of(masked))
            wide = jnp.concatenate(
                [pltpu.roll(h, (2 - 2 * g) % LANES, 1) for g in range(size_y // 8)], axis=0
            )
            turned.append(jnp.where(border, masked, wide))
    away = jnp.where(first, float(size_x), -float(size_x))
    lines = []
    for i in range(size_x):
        best = costs[i]
        for j in range(size_x):
            if j != i:
                best = jnp.minimum(best, costs[j] + float((i - j) ** 2))
            d = float(j - i) + away
            best = jnp.minimum(best, costs[size_x + j] + d * d)
        lines.append(best)
    zm_ref[0:LANES, :] = jnp.concatenate(lines, axis=0).T
    width = size_x * size_y
    ends = jnp.concatenate(turned, axis=0).T
    zm_ref[LANES : LANES + 8, :] = jnp.concatenate(
        [ends[r : r + 1, k * width : (k + 1) * width] for r in (0, LANES - 1, 1, 2) for k in range(2)],
        axis=0,
    )


Z_FLOOR = -(LANES + 6)


def sweep(accs, blocks, read, table, shift, low, high):
    parts = len(accs[0])

    def body(j, flat):
        flat = list(flat)
        tiles = read(j)
        squares = table.at[pl.ds(shift + 8 * blocks[0] - 8 * j, 8 * len(blocks))]
        for r in range(8):
            rows = [jnp.broadcast_to(t[r : r + 1, :], (8, LANES)) for t in tiles]
            for i in range(len(blocks)):
                square = squares[8 * i + 7 - r]
                for k in range(parts):
                    at = i * parts + k
                    flat[at] = jnp.minimum(flat[at], rows[k] + square)
        return tuple(flat)

    flat = lax.fori_loop(low, high, body, tuple(v for row in accs for v in row))
    return [list(flat[i * parts : (i + 1) * parts]) for i in range(len(blocks))]


def tiles_of(ref, j):
    rows = pl.ds(pl.multiple_of(8 * j, 8), 8)
    return [ref[rows, k * LANES : (k + 1) * LANES] for k in range(ref.shape[1] // LANES)]


def load_blocks(ref, blocks):
    return [tiles_of(ref, b) for b in blocks]


def save_blocks(ref, blocks, accs):
    for b, row in zip(blocks, accs):
        for k, v in enumerate(row):
            ref[8 * b : 8 * b + 8, k * LANES : (k + 1) * LANES] = v


def z_own_kernel(zm_ref, out_ref, table):
    count, half = LANES // 8, LANES // 16
    s = row_of((8, LANES)).astype(jnp.float32)
    for d in range(Z_FLOOR, LANES):
        v = s + float(d)
        table[d - Z_FLOOR] = v * v

    def read(j):
        at = row_of((8, LANES)) + 8 * j
        hide = (at == 0) | (at == LANES - 1)
        return [jnp.where(hide, HUGE, t) for t in tiles_of(zm_ref, j)]

    for first in (0, half):
        blocks = range(first, first + half)
        accs = [[jnp.full((8, LANES), HUGE, jnp.float32)] * (out_ref.shape[1] // LANES) for _ in blocks]
        save_blocks(out_ref, blocks, sweep(accs, blocks, read, table, -7 - Z_FLOOR, 0, count))


def border_minima(cost, size_x, size_y, partner):
    if not partner:
        return cost
    width = cost.shape[1]
    shape = (8, width)
    row, plane = row_of(shape), lane_of(shape) // size_y
    away = jnp.where(lax.axis_index("gx") == 0, size_x, -size_x)
    shift = jnp.where(row % 2 == 1, away, 0)
    best = None
    for r in range(size_x):
        source = jnp.where(plane >= r, plane - r, plane - r + size_x)
        d = (source + shift - plane).astype(jnp.float32)
        if r == 0:
            moved = cost
        else:
            cut = width - r * size_y
            moved = jnp.concatenate([cost[:, cut:], cost[:, :cut]], axis=1)
        moved = moved + d * d
        best = moved if best is None else jnp.minimum(best, moved)
    return jnp.minimum(best, pltpu.roll(best, 7, 0))


def z_far_kernel(even, partner, size_x, size_y, acc_ref, table, zm_ref, got_ref, out_ref, source, work):
    index, last = lax.axis_index("gz"), lax.axis_size("gz") - 1
    odd = index % 2 == 1
    low = odd if even else jnp.logical_not(odd)
    valid = jnp.where(low, index > 0, index < last)
    count, half = LANES // 8, LANES // 16
    out = out_ref if even else work

    own, got = zm_ref[LANES : LANES + 8, :], got_ref[LANES : LANES + 8, :]
    mine = jnp.where(low, own[0:2], own[2:4]) + jnp.where(valid, jnp.where(low, got[6:8], got[4:6]), 0.0)
    theirs = jnp.where(low, got[2:4] + own[4:6], got[0:2] + own[6:8])
    ends = border_minima(cost_of(jnp.concatenate([mine, theirs, mine, theirs], axis=0)), size_x, size_y, partner)
    source[...] = got_ref[0:LANES, :]

    squares = table.at[pl.ds(jnp.where(low, -Z_FLOOR, 1 - LANES - Z_FLOOR), LANES)]
    lanes = [slice(k * LANES, (k + 1) * LANES) for k in range(zm_ref.shape[1] // LANES)]
    rows = [jnp.broadcast_to(ends[0:1, cols], (8, LANES)) for cols in lanes]
    for b in range(count):
        for row, cols in zip(rows, lanes):
            span = slice(8 * b, 8 * b + 8)
            out[span, cols] = jnp.minimum(acc_ref[span, cols], row + squares[8 * b])

    def slanted(accs, blocks, offset, tiles, reach):
        for j in tiles:
            tile = tiles_of(source, j)
            for r in range(8):
                q = 8 * j + r
                rows = [jnp.broadcast_to(t[r : r + 1, :], (8, LANES)) for t in tile]
                for i, b in enumerate(blocks):
                    if reach(b, q):
                        square = table[8 * b - q + offset - Z_FLOOR]
                        accs[i] = [jnp.minimum(v, row + square) for v, row in zip(accs[i], rows)]
        return accs

    @pl.when(valid & low)
    def _():
        source[LANES - 1 : LANES, :] = ends[2:3]
        for first in (0, half):
            blocks = range(first, first + half)
            accs = load_blocks(out, blocks)
            accs = slanted(accs, blocks, LANES, blocks, lambda b, q: 8 * b < q)
            if blocks[-1] + 1 < count:
                read = functools.partial(tiles_of, source)
                accs = sweep(accs, blocks, read, table, LANES - 7 - Z_FLOOR, blocks[-1] + 1, count)
            save_blocks(out, blocks, accs)

    @pl.when(valid & jnp.logical_not(low))
    def _():
        source[0:1, :] = ends[2:3]
        for first in (0, half):
            blocks = range(first, first + half)
            accs = load_blocks(out, blocks)
            accs = slanted(accs, blocks, -LANES, blocks, lambda b, q: q < 8 * b + 7)
            if first:
                read = functools.partial(tiles_of, source)
                accs = sweep(accs, blocks, read, table, -LANES - 7 - Z_FLOOR, 0, first)
            save_blocks(out, blocks, accs)

    if not even:
        per = LANES // size_y
        for k, cols in enumerate(lanes):
            best = work[:, cols].T
            for i in range(per):
                out_ref[k * per + i] = best[i * size_y : (i + 1) * size_y]


def score_kernel(score_in, even_ref, odd_ref, _, score_ref):
    index, last = lax.axis_index("gz"), lax.axis_size("gz") - 1
    odd = index % 2 == 1
    size_y = score_in.shape[1]
    per = LANES // size_y
    for k in range(even_ref.shape[1] // LANES):
        cols = slice(k * LANES, (k + 1) * LANES)
        even_rows, odd_rows = even_ref[LANES : LANES + 8, cols], odd_ref[LANES : LANES + 8, cols]
        low = jnp.where(index > 0, jnp.where(odd, even_rows, odd_rows)[6:7], 0.0)
        high = jnp.where(index < last, jnp.where(odd, odd_rows, even_rows)[4:5], 0.0)
        middle = jnp.zeros((LANES - 2, LANES), jnp.float32)
        more = jnp.concatenate([low, middle, high], axis=0).T
        for i in range(per):
            x = k * per + i
            score_ref[x] = score_in[x] + more[i * size_y : (i + 1) * size_y]


def y_table(axis, hop, size_y, table):
    index = lax.axis_index(axis)
    away = (((index ^ hop) - index) * size_y).astype(jnp.float32)
    s = row_of((8, LANES)).astype(jnp.float32) - away
    for d in range(1 - size_y, size_y - 7):
        v = s + float(d)
        table[d - (1 - size_y)] = v * v


Y_BLOCKS = 4


def y_sweep(refs, tables, start, out_ref, scale):
    size_x, size_y, _ = out_ref.shape
    for first in range(0, size_y // 8, Y_BLOCKS):
        blocks = range(first, first + Y_BLOCKS)
        accs = []
        for b in blocks:
            span = slice(8 * b, 8 * b + 8)
            blank = jnp.full((8, LANES), HUGE, jnp.float32)
            accs.append([blank if start is None else start[x, span, :] for x in range(size_x)])
        for ref, table in zip(refs, tables):

            def read(j, ref=ref):
                return [ref[x, pl.ds(pl.multiple_of(8 * j, 8), 8), :] for x in range(size_x)]

            accs = sweep(accs, blocks, read, table, size_y - 8, 0, size_y // 8)
        for b, row in zip(blocks, accs):
            for x, v in enumerate(row):
                out_ref[x, 8 * b : 8 * b + 8, :] = v if scale == 1.0 else v * scale


def y_near_kernel(own_ref, chip_ref, out_ref, table_2, table_3, table_0, table_1):
    size_y = own_ref.shape[1]
    for hop, table in enumerate((table_0, table_1, table_2, table_3)):
        y_table("gy", hop, size_y, table)
    y_sweep((own_ref, chip_ref), (table_0, table_1), None, out_ref, 1.0)


def y_far_kernel(scale, start_ref, ref, table, out_ref):
    y_sweep((ref,), (table,), start_ref, out_ref, scale)


def swap(value, axis, hop):
    n = lax.axis_size(axis)
    return lax.ppermute(value, axis, [(i, i ^ hop) for i in range(n)])


def swap_xy(value, hop_x, hop_y):
    nx, ny = lax.axis_size("gx"), lax.axis_size("gy")
    pairs = [(x * ny + y, (x ^ hop_x) * ny + (y ^ hop_y)) for x in range(nx) for y in range(ny)]
    return lax.ppermute(value, ("gx", "gy"), pairs)


def neighbours(low, high, axis, beyond=0.0):
    n, index = lax.axis_size(axis), lax.axis_index(axis)
    odd = index % 2 == 1
    pairs = [(i, i + 1 if i % 2 else i - 1) for i in range(1, n - 1)]
    got_odd = lax.ppermute(jnp.where(odd, high, low), axis, pairs)
    got_even = lax.ppermute(jnp.where(odd, low, high), axis, [(i, i ^ 1) for i in range(n)])
    from_low = jnp.where(odd, got_even, got_odd)
    from_high = jnp.where(odd, got_odd, got_even)
    return jnp.where(index == 0, beyond, from_low), jnp.where(index == n - 1, beyond, from_high)


def z_swaps(value):
    n = lax.axis_size("gz")
    even = lax.ppermute(value, "gz", [(i, i ^ 1) for i in range(n)])
    return even, lax.ppermute(value, "gz", [(i, i + 1 if i % 2 else i - 1) for i in range(1, n - 1)])


def conv(features, conv_weight, mask, planes, count):
    channels, size_x, size_y, _ = features.shape
    return call(
        functools.partial(conv_kernel, planes),
        [(size_x, size_y, LANES), (count, size_y + 8, LANES), (count, 16, LANES)],
        [
            pltpu.VMEM(features.shape, jnp.bfloat16),
            pltpu.VMEM(conv_weight.shape, jnp.bfloat16),
            pltpu.VMEM(mask.shape, jnp.int32),
            pltpu.VMEM((9 * ROWS + 8, channels * 16), jnp.bfloat16),
            pltpu.VMEM((size_x + 2, 3, ROWS, size_y // 16 * LANES), jnp.float32),
            pltpu.SemaphoreType.DMA((size_x + 2,)),
        ],
        mib=24,
        in_specs=[HBM] * 3,
    )(*(pltpu.with_memory_space_constraint(v, pltpu.HBM) for v in (features, conv_weight, mask)))


def halo_with_partner(features, conv_weight, mask):
    _, size_x, size_y, _ = features.shape

    def planes():
        return [*range(1, size_x + 1), jnp.where(lax.axis_index("gx") == 0, size_x + 1, 0)]

    s, own, e = conv(features, conv_weight, mask, planes, size_x + 1)
    far = swap_xy(own, 1, 0)
    sides = [swap_xy(e, x, y) for x in range(2) for y in (1, 3)]
    return call(turn_kernel, [(size_x, size_y, LANES), (LANES + 8, size_x * size_y)])(s, own, far, *sides)


def halo_in_rounds(features, conv_weight, mask):
    _, size_x, size_y, _ = features.shape
    groups = size_y // 8
    planes = [*range(1, size_x + 1), 0, size_x + 1]
    s, rest, e = conv(features, conv_weight, mask, lambda: planes, size_x + 2)
    whole = jnp.concatenate([rest.at[:size_x, :size_y].set(s), e], axis=1)
    low, high = neighbours(whole[size_x], whole[size_x + 1], "gx")
    whole = whole[:size_x].at[0].add(low).at[size_x - 1].add(high)
    e = whole[:, size_y + 8 :]
    low, high = neighbours(e, e, "gy")
    whole = whole.at[:, 0].add(low[:, 0]).at[:, size_y - 1].add(high[:, 7])
    whole = whole.at[:, size_y].add(low[:, 8]).at[:, size_y + 7].add(high[:, 15])
    score, h = whole[:, :size_y], whole[:, size_y : size_y + 8]

    def line(value):
        return value.reshape(1, size_x * size_y)

    up = jnp.swapaxes(h[:, :, 0 : 2 * groups : 2], 1, 2)
    down = jnp.swapaxes(jnp.roll(h, 1, 2)[:, :, 0 : 2 * groups : 2], 1, 2)
    masked = jnp.where(mask == 1, HUGE, score)
    rows = jnp.transpose(cost_of(masked), (2, 0, 1)).reshape(LANES, size_x * size_y)
    ends = [line(v) for v in (masked[:, :, 0], masked[:, :, LANES - 1], down, up)]
    blank = [jnp.full_like(ends[0], HUGE)] * 2 + [jnp.zeros_like(ends[0])] * 2
    pairs = [v for pair in zip(ends, blank) for v in pair]
    return score, jnp.concatenate([rows, *pairs], axis=0)


def x_minima(value, size_x):
    n, index = lax.axis_size("gx"), lax.axis_index("gx")
    every = lax.all_gather(value, "gx", axis=0, tiled=True)
    at = index * size_x + jnp.arange(size_x)
    d = (at[:, None] - jnp.arange(n * size_x)[None, :]).astype(jnp.float32)
    return jnp.min(every[None] + (d * d)[:, :, None, None], axis=1)


def shards(features, conv_weight, mask):
    _, size_x, size_y, size_z = features.shape
    gx, gy = lax.axis_size("gx"), lax.axis_size("gy")
    assert size_z == LANES and size_y % 16 == 0 and LANES % size_y == 0 and gy == 4
    brick = (size_x, size_y, LANES)
    lines = size_x * size_y
    partner = gx == 2

    halo = halo_with_partner if partner else halo_in_rounds
    score, zm = halo(features, conv_weight, mask)

    even, odd = z_swaps(zm)
    best, table = call(z_own_kernel, [(LANES, lines), (LANES - Z_FLOOR, 8, LANES)])(zm)
    work = [pltpu.VMEM((LANES, lines), jnp.float32)] * 2
    for first, got, shape in ((True, even, (LANES, lines)), (False, odd, brick)):
        far = functools.partial(z_far_kernel, first, partner, size_x, size_y)
        (best,) = call(far, [shape], work)(best, table, zm, got)
    (score,) = call(score_kernel, [brick])(score, even, odd, best)
    if not partner:
        best = x_minima(best, size_x)

    tables = (2 * size_y - 8, 8, LANES)
    chip, across = swap(best, "gy", 1), swap(best, "gy", 2)
    near, table_2, table_3 = call(
        y_near_kernel, [brick, tables, tables], [pltpu.VMEM(tables, jnp.float32)] * 2
    )(best, chip)
    across, near = lax.optimization_barrier((across, near))
    forward = swap(across, "gy", 1)
    (near,) = call(functools.partial(y_far_kernel, 1.0), [brick])(near, across, table_2)
    (depth,) = call(functools.partial(y_far_kernel, 1.0 / RADIUS), [brick])(near, forward, table_3)
    return score, depth


def solution(mesh):
    in_specs = (P(None, "gx", "gy", "gz"), P(), P("gx", "gy", "gz"))
    out_specs = (P("gx", "gy", "gz"), P("gx", "gy", "gz"))
    return jax.shard_map(shards, mesh=mesh, in_specs=in_specs, out_specs=out_specs, check_vma=False)
```

profile of v0, /device:TPU:19, one launch (start us, length us, event | category | flops | bytes accessed | tf_op | source)
XLA Modules:
  0.0 31.2 jit_solution(9895917839550316579)
XLA Ops:
  0.6 2.6 %shard_map.50 = (f32[4,64,128]{2,1,0:T(8,128)S(1)}, f32[5,72,128]{2,1,0:T(8,128)S(1)}, f32[5,16,128]{2,1,0:T(8,128)S(1)}) custom-call(bf16[32,4,64,128]{3,2,1,0:T(8,128)(2,1)} %f_hbm.1, bf16[27,32]{1,0:T(8,128)(2,1)} %w_hbm.1, s32[4,64,128]{2,1,0:T(8,128)} %mask_hbm.1), custom_call_target="tpu_custom_call" | custom-call | tf_op jit(solution)/shard_map/pallas_call | solution.py:23
  3.2 0.3 %collective-permute-start = (f32[5,72,128]{2,1,0:T(8,128)S(1)}, f32[5,72,128]{2,1,0:T(8,128)S(1)}, u32[]{:S(2)}, u32[]{:S(2)}) collective-permute-start(f32[5,72,128]{2,1,0:T(8,128)S(1)} %get-tuple-element.15.own_ref), channel_id=1, source_target_pairs={{0,16},{4,20},{8,24},{12,28},{16,0},{20,4},{24,8},{28,12},{1,17},{... | collective-permute-start | bytes 552968 | tf_op jit(solution)/shard_map/ppermute | solution.py:438
  3.5 3.0 %collective-permute-start.4 = (f32[5,16,128]{2,1,0:T(8,128)S(1)}, f32[5,16,128]{2,1,0:T(8,128)S(1)}, u32[]{:S(2)}, u32[]{:S(2)}) collective-permute-start(f32[5,16,128]{2,1,0:T(8,128)S(1)} %get-tuple-element.16), channel_id=1, source_target_pairs={{0,28},{4,24},{8,20},{12,16},{16,12},{20,8},{24,4},{28,0},{1,29},{... | collective-permute-start | bytes 122888 | tf_op jit(solution)/shard_map/ppermute | solution.py:438
  6.5 0.0 collective-permute-start.3
  6.5 0.8 %collective-permute-start.2 = (f32[5,16,128]{2,1,0:T(8,128)S(1)}, f32[5,16,128]{2,1,0:T(8,128)S(1)}, u32[]{:S(2)}, u32[]{:S(2)}) collective-permute-start(f32[5,16,128]{2,1,0:T(8,128)S(1)} %get-tuple-element.16), channel_id=1, source_target_pairs={{0,12},{4,8},{8,4},{12,0},{16,28},{20,24},{24,20},{28,16},{1,13},{... | collective-permute-start | bytes 122888 | tf_op jit(solution)/shard_map/ppermute | solution.py:438
  7.3 0.0 collective-permute-start.1
  7.3 4.6 %collective-permute-done.4.xcross_ref = f32[5,16,128]{2,1,0:T(8,128)S(1)} collective-permute-done((f32[5,16,128]{2,1,0:T(8,128)S(1)}, f32[5,16,128]{2,1,0:T(8,128)S(1)}, u32[]{:S(2)}, u32[]{:S(2)}) %collective-permute-start.4) | collective-permute-done | bytes 40992 | tf_op jit(solution)/shard_map/ppermute | solution.py:438
  11.9 0.0 collective-permute-done.3.xchip_ref
  11.9 0.0 collective-permute-done.2.cross_ref
  11.9 0.0 collective-permute-done.1.chip_ref
  11.9 0.0 collective-permute-done.far_ref
  11.9 0.3 %shard_map.51 = (f32[4,64,128]{2,1,0:T(8,128)S(1)}, f32[136,256]{1,0:T(8,128)S(1)}) custom-call(f32[4,64,128]{2,1,0:T(8,128)S(1)} %get-tuple-element.14.s_ref, f32[5,72,128]{2,1,0:T(8,128)S(1)} %get-tuple-element.15.own_ref, f32[5,72,128]{2,1,0:T(8,128)S(1)} %collective-permute-done.far_ref, f32[5,16,128]{2,1,0:T(8,128)S(1)} %collective-permute-done.1.chip_ref, ...), custom_call_target="tpu_custom_call" | custom-call | tf_op jit(solution)/shard_map/pallas_call | solution.py:23
  12.2 1.4 %collective-permute-start.5 = (f32[136,256]{1,0:T(8,128)S(1)}, f32[136,256]{1,0:T(8,128)S(1)}, u32[]{:S(2)}, u32[]{:S(2)}) collective-permute-start(f32[136,256]{1,0:T(8,128)S(1)} %get-tuple-element.18.zm_ref), channel_id=1, source_target_pairs={{0,1},{1,0},{2,3},{3,2},{4,5},{5,4},{6,7},{7,6},{8,9},{9,8},{10,11... | collective-permute-start | bytes 417800 | tf_op jit(solution)/shard_map/ppermute | solution.py:454
  13.6 1.9 %collective-permute-start.6 = (f32[136,256]{1,0:T(8,128)S(1)}, f32[136,256]{1,0:T(8,128)S(1)}, u32[]{:S(2)}, u32[]{:S(2)}) collective-permute-start(f32[136,256]{1,0:T(8,128)S(1)} %get-tuple-element.18.zm_ref), channel_id=1, source_target_pairs={{1,2},{2,1},{5,6},{6,5},{9,10},{10,9},{13,14},{14,13},{17,18},{18,... | collective-permute-start | bytes 417800 | tf_op jit(solution)/shard_map/ppermute | solution.py:455
  15.5 1.4 %shard_map.52 = (f32[128,256]{1,0:T(8,128)S(1)}, f32[262,8,128]{2,1,0:T(8,128)S(1)}) custom-call(f32[136,256]{1,0:T(8,128)S(1)} %get-tuple-element.18.zm_ref), custom_call_target="tpu_custom_call" | custom-call | tf_op jit(solution)/shard_map/pallas_call | solution.py:23
  17.0 1.0 %collective-permute-done.5.got_ref.even_ref = f32[136,256]{1,0:T(8,128)S(1)} collective-permute-done((f32[136,256]{1,0:T(8,128)S(1)}, f32[136,256]{1,0:T(8,128)S(1)}, u32[]{:S(2)}, u32[]{:S(2)}) %collective-permute-start.5) | collective-permute-done | bytes 139296 | tf_op jit(solution)/shard_map/ppermute | solution.py:454
  18.0 0.8 %shard_map.53.acc_ref = f32[128,256]{1,0:T(8,128)S(1)} custom-call(f32[128,256]{1,0:T(8,128)S(1)} %get-tuple-element.19.acc_ref, f32[262,8,128]{2,1,0:T(8,128)S(1)} %get-tuple-element.20.table, f32[136,256]{1,0:T(8,128)S(1)} %get-tuple-element.18.zm_ref, f32[136,256]{1,0:T(8,128)S(1)} %collective-permute-done.5.got_ref.even_ref), custom_call_target="tpu_custom_call" | custom-call | tf_op jit(solution)/shard_map/pallas_call | solution.py:23
  18.7 2.2 %collective-permute-done.6.got_ref.odd_ref = f32[136,256]{1,0:T(8,128)S(1)} collective-permute-done((f32[136,256]{1,0:T(8,128)S(1)}, f32[136,256]{1,0:T(8,128)S(1)}, u32[]{:S(2)}, u32[]{:S(2)}) %collective-permute-start.6) | collective-permute-done | bytes 139296 | tf_op jit(solution)/shard_map/ppermute | solution.py:455
  20.9 0.9 %shard_map.54._.own_ref = f32[4,64,128]{2,1,0:T(8,128)S(1)} custom-call(f32[128,256]{1,0:T(8,128)S(1)} %shard_map.53.acc_ref, f32[262,8,128]{2,1,0:T(8,128)S(1)} %get-tuple-element.20.table, f32[136,256]{1,0:T(8,128)S(1)} %get-tuple-element.18.zm_ref, f32[136,256]{1,0:T(8,128)S(1)} %collective-permute-done.6.got_ref.odd_ref), custom_call_target="tpu_custom_call" | custom-call | tf_op jit(solution)/shard_map/pallas_call | solution.py:23
  21.9 0.7 %collective-permute-start.8 = (f32[4,64,128]{2,1,0:T(8,128)S(1)}, f32[4,64,128]{2,1,0:T(8,128)S(1)}, u32[]{:S(2)}, u32[]{:S(2)}) collective-permute-start(f32[4,64,128]{2,1,0:T(8,128)S(1)} %shard_map.54._.own_ref), channel_id=1, source_target_pairs={{0,4},{4,0},{8,12},{12,8},{1,5},{5,1},{9,13},{13,9},{2,6},{6,2},{1... | collective-permute-start | bytes 393224 | tf_op jit(solution)/shard_map/ppermute | solution.py:432
  22.6 0.7 %collective-permute-start.7 = (f32[4,64,128]{2,1,0:T(8,128)S(1)}, f32[4,64,128]{2,1,0:T(8,128)S(1)}, u32[]{:S(2)}, u32[]{:S(2)}) collective-permute-start(f32[4,64,128]{2,1,0:T(8,128)S(1)} %shard_map.54._.own_ref), channel_id=1, source_target_pairs={{0,8},{4,12},{8,0},{12,4},{1,9},{5,13},{9,1},{13,5},{2,10},{6,14},... | collective-permute-start | bytes 393224 | tf_op jit(solution)/shard_map/ppermute | solution.py:432
  23.3 0.3 collective-permute-done.8.chip_ref
  23.6 1.4 %shard_map.56 = (f32[4,64,128]{2,1,0:T(8,128)S(1)}, f32[120,8,128]{2,1,0:T(8,128)S(1)}, f32[120,8,128]{2,1,0:T(8,128)S(1)}) custom-call(f32[4,64,128]{2,1,0:T(8,128)S(1)} %shard_map.54._.own_ref, f32[4,64,128]{2,1,0:T(8,128)S(1)} %collective-permute-done.8.chip_ref), custom_call_target="tpu_custom_call" | custom-call | tf_op jit(solution)/shard_map/pallas_call | solution.py:23
  25.0 2.7 %collective-permute-done.7.ref = f32[4,64,128]{2,1,0:T(8,128)S(1)} collective-permute-done((f32[4,64,128]{2,1,0:T(8,128)S(1)}, f32[4,64,128]{2,1,0:T(8,128)S(1)}, u32[]{:S(2)}, u32[]{:S(2)}) %collective-permute-start.7) | collective-permute-done | bytes 131104 | tf_op jit(solution)/shard_map/ppermute | solution.py:432
  27.6 0.8 %collective-permute-start.9 = (f32[4,64,128]{2,1,0:T(8,128)S(1)}, f32[4,64,128]{2,1,0:T(8,128)S(1)}, u32[]{:S(2)}, u32[]{:S(2)}) collective-permute-start(f32[4,64,128]{2,1,0:T(8,128)S(1)} %collective-permute-done.7.ref), channel_id=1, source_target_pairs={{0,4},{4,0},{8,12},{12,8},{1,5},{5,1},{9,13},{13,9},{2,6},{6,2},{1... | collective-permute-start | bytes 393224 | tf_op jit(solution)/shard_map/ppermute | solution.py:432
  28.5 0.8 %shard_map.55 = f32[4,64,128]{2,1,0:T(8,128)} custom-call(f32[4,64,128]{2,1,0:T(8,128)S(1)} %get-tuple-element.17.score_in, f32[136,256]{1,0:T(8,128)S(1)} %collective-permute-done.5.got_ref.even_ref, f32[136,256]{1,0:T(8,128)S(1)} %collective-permute-done.6.got_ref.odd_ref, f32[4,64,128]{2,1,0:T(8,128)S(1)} %shard_map.54._.own_ref), custom_call_target="tpu_custom_call" | custom-call | tf_op jit(solution)/shard_map/pallas_call | solution.py:23
  29.3 0.6 %shard_map.57.start_ref = f32[4,64,128]{2,1,0:T(8,128)S(1)} custom-call(f32[4,64,128]{2,1,0:T(8,128)S(1)} %get-tuple-element.22.start_ref, f32[4,64,128]{2,1,0:T(8,128)S(1)} %collective-permute-done.7.ref, f32[120,8,128]{2,1,0:T(8,128)S(1)} %get-tuple-element.24.table), custom_call_target="tpu_custom_call" | custom-call | tf_op jit(solution)/shard_map/pallas_call | solution.py:23
  29.9 0.0 collective-permute-done.9.ref
  29.9 1.3 %shard_map.58 = f32[4,64,128]{2,1,0:T(8,128)} custom-call(f32[4,64,128]{2,1,0:T(8,128)S(1)} %shard_map.57.start_ref, f32[4,64,128]{2,1,0:T(8,128)S(1)} %collective-permute-done.9.ref, f32[120,8,128]{2,1,0:T(8,128)S(1)} %get-tuple-element.25.table), custom_call_target="tpu_custom_call" | custom-call | tf_op jit(solution)/shard_map/pallas_call | solution.py:23
Async XLA Ops:
  3.2 8.7 %collective-permute-start = (f32[5,72,128]{2,1,0:T(8,128)S(1)}, f32[5,72,128]{2,1,0:T(8,128)S(1)}, u32[]{:S(2)}, u32[]{:S(2)}) collective-permute-start(f32[5,72,128]{2,1,0:T(8,128)S(1)} %get-tuple-element.15.own_ref), channel_id=1, source_target_pairs={{0,16},{4,20},{8,24},{12,28},{16,0},{20,4},{24,8},{28,12},{1,17},{... | collective-permute-start | bytes 552968 | tf_op jit(solution)/shard_map/ppermute | solution.py:438
  3.5 8.4 %collective-permute-start.4 = (f32[5,16,128]{2,1,0:T(8,128)S(1)}, f32[5,16,128]{2,1,0:T(8,128)S(1)}, u32[]{:S(2)}, u32[]{:S(2)}) collective-permute-start(f32[5,16,128]{2,1,0:T(8,128)S(1)} %get-tuple-element.16), channel_id=1, source_target_pairs={{0,28},{4,24},{8,20},{12,16},{16,12},{20,8},{24,4},{28,0},{1,29},{... | collective-permute-start | bytes 122888 | tf_op jit(solution)/shard_map/ppermute | solution.py:438
  6.5 5.4 %collective-permute-start.3 = (f32[5,16,128]{2,1,0:T(8,128)S(1)}, f32[5,16,128]{2,1,0:T(8,128)S(1)}, u32[]{:S(2)}, u32[]{:S(2)}) collective-permute-start(f32[5,16,128]{2,1,0:T(8,128)S(1)} %get-tuple-element.16), channel_id=1, source_target_pairs={{0,20},{4,16},{8,28},{12,24},{16,4},{20,0},{24,12},{28,8},{1,21},{... | collective-permute-start | bytes 122888 | tf_op jit(solution)/shard_map/ppermute | solution.py:438
  6.5 5.4 %collective-permute-start.2 = (f32[5,16,128]{2,1,0:T(8,128)S(1)}, f32[5,16,128]{2,1,0:T(8,128)S(1)}, u32[]{:S(2)}, u32[]{:S(2)}) collective-permute-start(f32[5,16,128]{2,1,0:T(8,128)S(1)} %get-tuple-element.16), channel_id=1, source_target_pairs={{0,12},{4,8},{8,4},{12,0},{16,28},{20,24},{24,20},{28,16},{1,13},{... | collective-permute-start | bytes 122888 | tf_op jit(solution)/shard_map/ppermute | solution.py:438
  7.3 4.6 %collective-permute-start.1 = (f32[5,16,128]{2,1,0:T(8,128)S(1)}, f32[5,16,128]{2,1,0:T(8,128)S(1)}, u32[]{:S(2)}, u32[]{:S(2)}) collective-permute-start(f32[5,16,128]{2,1,0:T(8,128)S(1)} %get-tuple-element.16), channel_id=1, source_target_pairs={{0,4},{4,0},{8,12},{12,8},{16,20},{20,16},{24,28},{28,24},{1,5},{5... | collective-permute-start | bytes 122888 | tf_op jit(solution)/shard_map/ppermute | solution.py:438
  12.2 5.7 %collective-permute-start.5 = (f32[136,256]{1,0:T(8,128)S(1)}, f32[136,256]{1,0:T(8,128)S(1)}, u32[]{:S(2)}, u32[]{:S(2)}) collective-permute-start(f32[136,256]{1,0:T(8,128)S(1)} %get-tuple-element.18.zm_ref), channel_id=1, source_target_pairs={{0,1},{1,0},{2,3},{3,2},{4,5},{5,4},{6,7},{7,6},{8,9},{9,8},{10,11... | collective-permute-start | bytes 417800 | tf_op jit(solution)/shard_map/ppermute | solution.py:454
  13.6 7.3 %collective-permute-start.6 = (f32[136,256]{1,0:T(8,128)S(1)}, f32[136,256]{1,0:T(8,128)S(1)}, u32[]{:S(2)}, u32[]{:S(2)}) collective-permute-start(f32[136,256]{1,0:T(8,128)S(1)} %get-tuple-element.18.zm_ref), channel_id=1, source_target_pairs={{1,2},{2,1},{5,6},{6,5},{9,10},{10,9},{13,14},{14,13},{17,18},{18,... | collective-permute-start | bytes 417800 | tf_op jit(solution)/shard_map/ppermute | solution.py:455
  21.9 1.7 %collective-permute-start.8 = (f32[4,64,128]{2,1,0:T(8,128)S(1)}, f32[4,64,128]{2,1,0:T(8,128)S(1)}, u32[]{:S(2)}, u32[]{:S(2)}) collective-permute-start(f32[4,64,128]{2,1,0:T(8,128)S(1)} %shard_map.54._.own_ref), channel_id=1, source_target_pairs={{0,4},{4,0},{8,12},{12,8},{1,5},{5,1},{9,13},{13,9},{2,6},{6,2},{1... | collective-permute-start | bytes 393224 | tf_op jit(solution)/shard_map/ppermute | solution.py:432
  22.6 5.1 %collective-permute-start.7 = (f32[4,64,128]{2,1,0:T(8,128)S(1)}, f32[4,64,128]{2,1,0:T(8,128)S(1)}, u32[]{:S(2)}, u32[]{:S(2)}) collective-permute-start(f32[4,64,128]{2,1,0:T(8,128)S(1)} %shard_map.54._.own_ref), channel_id=1, source_target_pairs={{0,8},{4,12},{8,0},{12,4},{1,9},{5,13},{9,1},{13,5},{2,10},{6,14},... | collective-permute-start | bytes 393224 | tf_op jit(solution)/shard_map/ppermute | solution.py:432
  27.6 2.3 %collective-permute-start.9 = (f32[4,64,128]{2,1,0:T(8,128)S(1)}, f32[4,64,128]{2,1,0:T(8,128)S(1)}, u32[]{:S(2)}, u32[]{:S(2)}) collective-permute-start(f32[4,64,128]{2,1,0:T(8,128)S(1)} %collective-permute-done.7.ref), channel_id=1, source_target_pairs={{0,4},{4,0},{8,12},{12,8},{1,5},{5,1},{9,13},{13,9},{2,6},{6,2},{1... | collective-permute-start | bytes 393224 | tf_op jit(solution)/shard_map/ppermute | solution.py:432
where the time goes:
time: 31.4 us; the launch traced here: 31.2 us
  waiting for transfers between devices  10.8 us (34%)
  Pallas kernels  10.1 us (32%)
  starting transfers between devices  9.66 us (31%)
  between operations  0.71 us (2%)
    pallas_call x9, Pallas kernels, run(): pl.pallas_call(kernel, out_shape=shapes, in_specs=in_specs or [VMEM] * le...  10.1 us
    ppermute x5, waiting for transfers between devices, swap_xy(): return lax.ppermute(value, ('gx', 'gy'), pairs)  4.62 us
    ppermute x5, starting transfers between devices, swap_xy(): return lax.ppermute(value, ('gx', 'gy'), pairs)  4.09 us
    ppermute x3, waiting for transfers between devices, swap(): return lax.ppermute(value, axis, [(i, i ^ hop) for i in range(n)])  2.94 us
    ppermute x3, starting transfers between devices, swap(): return lax.ppermute(value, axis, [(i, i ^ hop) for i in range(n)])  2.29 us
    ppermute x1, waiting for transfers between devices, z_swaps(): lax.ppermute(value, 'gz', [(i, i + 1 if i % 2 else i - 1) for i in range(...  2.21 us
    ppermute x1, starting transfers between devices, z_swaps(): lax.ppermute(value, 'gz', [(i, i + 1 if i % 2 else i - 1) for i in range(...  1.91 us
    ppermute x1, starting transfers between devices, z_swaps(): even = lax.ppermute(value, 'gz', [(i, i ^ 1) for i in range(n)])  1.36 us
  transfers between devices with their start and end apart: 10, of which 5 were waited for; matrix products, arithmetic and copies ran while one was open for 0% of the time, Pallas kernels for 16%

commit v1 on v0

--- a/solution.py
+++ b/solution.py
@@ -44,7 +44,9 @@
     return CEILING / (1.0 + jnp.exp(-score))
 
 
-def conv_kernel(planes, f_hbm, w_hbm, mask_hbm, s_ref, m_ref, e_ref, f_vmem, w_vmem, mask_vmem, w_big, acc, sems):
+def conv_kernel(
+    planes, paired, f_hbm, w_hbm, mask_hbm, s_ref, m_ref, e_ref, d_ref, f_vmem, w_vmem, mask_vmem, w_big, acc, sems
+):
     channels, size_x, size_y, _ = f_vmem.shape
     tiles = size_y // 16
     depth = channels * 16
@@ -53,10 +55,10 @@
     copies = [
         pltpu.make_async_copy(f_hbm.at[:, x], f_vmem.at[:, x], sems.at[x]) for x in range(size_x)
     ]
+    masks = pltpu.make_async_copy(mask_hbm, mask_vmem, sems.at[size_x + 1])
+    masks.start()
     for copy in copies:
         copy.start()
-    masks = pltpu.make_async_copy(mask_hbm, mask_vmem, sems.at[size_x + 1])
-    masks.start()
 
     acc[...] = jnp.zeros_like(acc)
     spread = (
@@ -80,24 +82,13 @@
     blocks.append(jnp.zeros((8, depth), jnp.float32))
     w_big[...] = jnp.concatenate(blocks, axis=0).astype(jnp.bfloat16)
 
-    for x in range(size_x):
-        copies[x].wait()
-        right = jnp.concatenate(
-            [f_vmem[:, x, 16 * t : 16 * t + 16, :].reshape(depth, LANES) for t in range(tiles)],
-            axis=1,
-        )
-        got = jnp.dot(w_big[...], right, preferred_element_type=jnp.float32)
-        for a in range(3):
-            at = x + 2 - a
-            for c in range(3):
-                first = (3 * a + c) * ROWS
-                acc[at, c] = acc[at, c] + got[first : first + ROWS, :]
-
     shape = (8, LANES)
     row, lane = row_of(shape), lane_of(shape)
     groups = size_y // 8
-    masks.wait()
-    for p, at in enumerate(planes()):
+    to_first = lax.axis_index("gy") % 2 == 1 if paired else True
+    folds = []
+
+    def finish(p, at):
         fold = None
         for g in range(groups + 1):
             sums = []
@@ -107,9 +98,7 @@
                     return acc[at, c, low : low + 8, tile * LANES : tile * LANES + LANES]
 
                 if g == groups:
-                    part = jnp.where(row == 0, piece(tiles - 1, 16), 0.0) + jnp.where(
-                        row == 7, piece(0, 16), 0.0
-                    )
+                    part = jnp.where(row == 0, piece(tiles - 1, 16), piece(0, 16))
                 else:
                     tile, low = g // 2, 8 * (g % 2)
                     part = piece(tile, low)
@@ -125,16 +114,39 @@
             )
             outer = jnp.where(lane == 0, ahead, jnp.where(lane == LANES - 1, behind, 0.0))
             if g == groups:
-                e_ref[p, 0:8, :] = inner
-                e_ref[p, 8:16, :] = jnp.where(row == 7, pltpu.roll(outer, 2 * (groups - 1), 1), outer)
+                for up, down, at_row in (
+                    (inner, inner, p),
+                    (outer, pltpu.roll(outer, 2 * (groups - 1), 1), 8 + p),
+                ):
+                    e_ref[at_row : at_row + 1, :] = jnp.where(to_first, down[7:8], up[0:1])
+                    d_ref[at_row : at_row + 1, :] = jnp.where(to_first, up[0:1], down[7:8])
             else:
                 span = slice(8 * g, 8 * g + 8)
                 if p < size_x:
                     s_ref[p, span, :] = inner
                     inner = jnp.where(mask_vmem[p, span, :] == 1, HUGE, inner)
-                m_ref[p, span, :] = inner
-                fold = outer if g == 0 else fold + pltpu.roll(outer, 2 * g, 1)
-        m_ref[p, size_y : size_y + 8, :] = fold
+                m_ref[p * size_y + 8 * g : p * size_y + 8 * g + 8, :] = inner
+                shift = 16 * p + 2 * g
+                outer = pltpu.roll(outer, shift, 1) if shift else outer
+                fold = outer if g == 0 else fold + outer
+        folds.append(fold)
+
+    for x in range(size_x):
+        copies[x].wait()
+        right = jnp.concatenate(
+            [f_vmem[:, x, 16 * t : 16 * t + 16, :].reshape(depth, LANES) for t in range(tiles)],
+            axis=1,
+        )
+        got = jnp.dot(w_big[...], right, preferred_element_type=jnp.float32)
+        for a in range(3):
+            at = x + 2 - a
+            for c in range(3):
+                first = (3 * a + c) * ROWS
+                acc[at, c] = acc[at, c] + got[first : first + ROWS, :]
+    masks.wait()
+    for p, at in enumerate(planes()):
+        finish(p, at)
+    m_ref[len(folds) * size_y :, :] = functools.reduce(jnp.add, folds)
 
 
 def y_masks(axis, chip):
@@ -160,14 +172,8 @@
     )
 
 
-def edge_fold(masks, part):
-    low, high = masks
-    return jnp.where(low, part, jnp.where(high, part, 0.0))
-
-
 def turn_kernel(s_ref, own_ref, far_ref, chip_ref, cross_ref, xchip_ref, xcross_ref, score_ref, zm_ref):
     size_x, size_y, _ = s_ref.shape
-    rows, fold = slice(0, size_y), slice(size_y, size_y + 8)
     chip, cross = y_masks("gy", True), y_masks("gy", False)
     first = lax.axis_index("gx") == 0
     lane = lane_of((size_y, LANES))
@@ -175,17 +181,24 @@
     faces_own = {size_x - 1: jnp.where(first, 1.0, 0.0), 0: jnp.where(first, 0.0, 1.0)}
     faces_far = {0: faces_own[size_x - 1], size_x - 1: faces_own[0]}
 
+    def plane(ref, p):
+        return ref[p * size_y : (p + 1) * size_y, :]
+
+    def fold(ref, p):
+        rest = ref[(size_x + 1) * size_y :, :]
+        return pltpu.roll(rest, LANES - 16 * p, 1) if p else rest
+
     def complete(p, base, folded, face_ref, sides, faces):
         if p in faces:
-            base = base + faces[p] * face_ref[size_x, rows]
-            folded = folded + faces[p] * face_ref[size_x, fold]
+            base = base + faces[p] * plane(face_ref, size_x)
+            folded = folded + faces[p] * fold(face_ref, size_x)
         for masks, same, other in sides:
-            part, part_h = same[p, 0:8], same[p, 8:16]
+            part, part_h = same[p : p + 1], same[8 + p : 9 + p]
             if p in faces:
-                part = part + faces[p] * other[size_x, 0:8]
-                part_h = part_h + faces[p] * other[size_x, 8:16]
+                part = part + faces[p] * other[size_x : size_x + 1]
+                part_h = part_h + faces[p] * other[8 + size_x : 9 + size_x]
             base = base + edge_rows(masks, part, size_y)
-            folded = folded + edge_fold(masks, part_h)
+            folded = folded + jnp.where(masks[0] | masks[1], part_h, 0.0)
         return base, folded
 
     costs, turned = [], []
@@ -193,12 +206,12 @@
         for p in range(size_x):
             if far:
                 sides = ((chip, xchip_ref, chip_ref), (cross, xcross_ref, cross_ref))
-                masked, h = complete(p, far_ref[p, rows], far_ref[p, fold], own_ref, sides, faces_far)
+                masked, h = complete(p, plane(far_ref, p), fold(far_ref, p), own_ref, sides, faces_far)
             else:
                 sides = ((chip, chip_ref, xchip_ref), (cross, cross_ref, xcross_ref))
-                full, h = complete(p, s_ref[p], own_ref[p, fold], far_ref, sides, faces_own)
+                full, h = complete(p, s_ref[p], fold(own_ref, p), far_ref, sides, faces_own)
                 score_ref[p] = full
-                masked = jnp.where(own_ref[p, rows] == HUGE, HUGE, full)
+                masked = jnp.where(plane(own_ref, p) == HUGE, HUGE, full)
             costs.append(cost_of(masked))
             wide = jnp.concatenate(
                 [pltpu.roll(h, (2 - 2 * g) % LANES, 1) for g in range(size_y // 8)], axis=0
@@ -416,15 +429,27 @@
                 out_ref[x, 8 * b : 8 * b + 8, :] = v if scale == 1.0 else v * scale
 
 
-def y_near_kernel(own_ref, chip_ref, out_ref, table_2, table_3, table_0, table_1):
+def y_own_kernel(own_ref, out_ref, table_1, table_2, table_3, table_0):
     size_y = own_ref.shape[1]
     for hop, table in enumerate((table_0, table_1, table_2, table_3)):
         y_table("gy", hop, size_y, table)
-    y_sweep((own_ref, chip_ref), (table_0, table_1), None, out_ref, 1.0)
-
-
-def y_far_kernel(scale, start_ref, ref, table, out_ref):
-    y_sweep((ref,), (table,), start_ref, out_ref, scale)
+    y_sweep((own_ref,), (table_0,), None, out_ref, 1.0)
+
+
+def y_far_kernel(hop, scale, start_ref, ref, table, out_ref):
+    index = lax.axis_index("gy")
+    if hop < 3:
+        y_sweep((ref,), (table,), start_ref, out_ref, scale)
+        return
+    near = jnp.abs((index ^ hop) - index) < 3
+
+    @pl.when(near)
+    def _():
+        y_sweep((ref,), (table,), start_ref, out_ref, scale)
+
+    @pl.when(jnp.logical_not(near))
+    def _():
+        out_ref[...] = start_ref[...] * scale
 
 
 def swap(value, axis, hop):
@@ -455,11 +480,11 @@
     return even, lax.ppermute(value, "gz", [(i, i + 1 if i % 2 else i - 1) for i in range(1, n - 1)])
 
 
-def conv(features, conv_weight, mask, planes, count):
+def conv(features, conv_weight, mask, planes, count, paired):
     channels, size_x, size_y, _ = features.shape
     return call(
-        functools.partial(conv_kernel, planes),
-        [(size_x, size_y, LANES), (count, size_y + 8, LANES), (count, 16, LANES)],
+        functools.partial(conv_kernel, planes, paired),
+        [(size_x, size_y, LANES), (count * size_y + 8, LANES), (16, LANES), (16, LANES)],
         [
             pltpu.VMEM(features.shape, jnp.bfloat16),
             pltpu.VMEM(conv_weight.shape, jnp.bfloat16),
@@ -479,9 +504,9 @@
     def planes():
         return [*range(1, size_x + 1), jnp.where(lax.axis_index("gx") == 0, size_x + 1, 0)]
 
-    s, own, e = conv(features, conv_weight, mask, planes, size_x + 1)
+    s, own, chip, cross = conv(features, conv_weight, mask, planes, size_x + 1, True)
     far = swap_xy(own, 1, 0)
-    sides = [swap_xy(e, x, y) for x in range(2) for y in (1, 3)]
+    sides = [swap_xy(v, x, y) for x in range(2) for v, y in ((chip, 1), (cross, 3))]
     return call(turn_kernel, [(size_x, size_y, LANES), (LANES + 8, size_x * size_y)])(s, own, far, *sides)
 
 
@@ -489,15 +514,20 @@
     _, size_x, size_y, _ = features.shape
     groups = size_y // 8
     planes = [*range(1, size_x + 1), 0, size_x + 1]
-    s, rest, e = conv(features, conv_weight, mask, lambda: planes, size_x + 2)
-    whole = jnp.concatenate([rest.at[:size_x, :size_y].set(s), e], axis=1)
-    low, high = neighbours(whole[size_x], whole[size_x + 1], "gx")
-    whole = whole[:size_x].at[0].add(low).at[size_x - 1].add(high)
-    e = whole[:, size_y + 8 :]
-    low, high = neighbours(e, e, "gy")
-    whole = whole.at[:, 0].add(low[:, 0]).at[:, size_y - 1].add(high[:, 7])
-    whole = whole.at[:, size_y].add(low[:, 8]).at[:, size_y + 7].add(high[:, 15])
-    score, h = whole[:, :size_y], whole[:, size_y : size_y + 8]
+    s, rest, down, up = conv(features, conv_weight, mask, lambda: planes, size_x + 2, False)
+
+    def whole(k):
+        h = jnp.roll(rest[len(planes) * size_y :], -16 * k, 1)
+        part = s[k] if k < size_x else rest[k * size_y : (k + 1) * size_y]
+        return jnp.concatenate([part, h, *(e[i : i + 1] for e in (down, up) for i in (k, 8 + k))], axis=0)
+
+    low, high = neighbours(whole(size_x), whole(size_x + 1), "gx")
+    own = jnp.stack([whole(k) for k in range(size_x)]).at[0].add(low).at[size_x - 1].add(high)
+    e = own[:, size_y + 8 :]
+    low, high = neighbours(e[:, 0:2], e[:, 2:4], "gy")
+    own = own.at[:, 0].add(low[:, 0]).at[:, size_y - 1].add(high[:, 0])
+    own = own.at[:, size_y].add(low[:, 1]).at[:, size_y + 7].add(high[:, 1])
+    score, h = own[:, :size_y], own[:, size_y : size_y + 8]
 
     def line(value):
         return value.reshape(1, size_x * size_y)
@@ -542,15 +572,13 @@
         best = x_minima(best, size_x)
 
     tables = (2 * size_y - 8, 8, LANES)
-    chip, across = swap(best, "gy", 1), swap(best, "gy", 2)
-    near, table_2, table_3 = call(
-        y_near_kernel, [brick, tables, tables], [pltpu.VMEM(tables, jnp.float32)] * 2
-    )(best, chip)
-    across, near = lax.optimization_barrier((across, near))
-    forward = swap(across, "gy", 1)
-    (near,) = call(functools.partial(y_far_kernel, 1.0), [brick])(near, across, table_2)
-    (depth,) = call(functools.partial(y_far_kernel, 1.0 / RADIUS), [brick])(near, forward, table_3)
-    return score, depth
+    across, chip = swap(best, "gy", 2), swap(best, "gy", 1)
+    near, *kept = call(y_own_kernel, [brick, tables, tables, tables], [pltpu.VMEM(tables, jnp.float32)])(best)
+    blocks = {2: across, 1: chip, 3: lax.ppermute(best, "gy", [(1, 2), (2, 1)])}
+    for hop, block in blocks.items():
+        far = functools.partial(y_far_kernel, hop, 1.0 / RADIUS if hop == 3 else 1.0)
+        (near,) = call(far, [brick])(near, block, kept[hop - 1])
+    return score, near
 
 
 def solution(mesh):

time: 31.4 us -> 30.3 us (0.965)
  waiting for transfers between devices: 10.8 us -> 7.02 us
  starting transfers between devices: 9.66 us -> 12.1 us
    ppermute x0 -> x1, starting transfers between devices: none -> 3.02 us  [shards(): blocks = {2: across, 1: chip, 3: lax.ppermute(best, 'gy', [(1, 2), (2, 1)])}]
    ppermute x3 -> x2, waiting for transfers between devices: 2.94 us -> 0.01 us  [swap(): return lax.ppermute(value, axis, [(i, i ^ hop) for i in range(n)])]
    ppermute x5, waiting for transfers between devices: 4.62 us -> 3.89 us  [swap_xy(): return lax.ppermute(value, ('gx', 'gy'), pairs)]
    ppermute x3 -> x2, starting transfers between devices: 2.29 us -> 1.67 us  [swap(): return lax.ppermute(value, axis, [(i, i ^ hop) for i in range(n)])]
    ppermute x0 -> x1, waiting for transfers between devices: none -> 0.38 us  [shards(): blocks = {2: across, 1: chip, 3: lax.ppermute(best, 'gy', [(1, 2), (2, 1)])}]
    ppermute x1, waiting for transfers between devices: 0.99 us -> 0.65 us  [z_swaps(): even = lax.ppermute(value, 'gz', [(i, i ^ 1) for i in range(n)])]
    pallas_call x9 -> x10, Pallas kernels: 10.1 us -> 10.2 us  [run(): pl.pallas_call(kernel, out_shape=shapes, in_specs=in_specs or [VMEM] * le...]
  transfers between devices with their start and end apart: 10 -> 10, of which waited for: 5 -> 6; matrix products, arithmetic and copies ran while one was open for 0% -> 0% of each run, Pallas kernels for 16% -> 17%
where the time goes in v1:
time: 30.3 us; the launch traced here: 30 us
  starting transfers between devices  12.1 us (40%)
  Pallas kernels  10.2 us (34%)
  waiting for transfers between devices  7.02 us (23%)
  between operations  0.71 us (2%)
    pallas_call x10, Pallas kernels, run(): pl.pallas_call(kernel, out_shape=shapes, in_specs=in_specs or [VMEM] * le...  10.2 us
    ppermute x5, starting transfers between devices, swap_xy(): return lax.ppermute(value, ('gx', 'gy'), pairs)  4.09 us
    ppermute x5, waiting for transfers between devices, swap_xy(): return lax.ppermute(value, ('gx', 'gy'), pairs)  3.89 us
    ppermute x1, starting transfers between devices, shards(): blocks = {2: across, 1: chip, 3: lax.ppermute(best, 'gy', [(1, 2), (2, 1)])}  3.02 us
    ppermute x1, waiting for transfers between devices, z_swaps(): lax.ppermute(value, 'gz', [(i, i + 1 if i % 2 else i - 1) for i in range(...  2.1 us
    ppermute x1, starting transfers between devices, z_swaps(): lax.ppermute(value, 'gz', [(i, i + 1 if i % 2 else i - 1) for i in range(...  1.91 us
    ppermute x2, starting transfers between devices, swap(): return lax.ppermute(value, axis, [(i, i ^ hop) for i in range(n)])  1.67 us
    ppermute x1, starting transfers between devices, z_swaps(): even = lax.ppermute(value, 'gz', [(i, i ^ 1) for i in range(n)])  1.36 us
  transfers between devices with their start and end apart: 10, of which 6 were waited for; matrix products, arithmetic and copies ran while one was open for 0% of the time, Pallas kernels for 17%

profile of v1, /device:TPU:19, one launch (start us, length us, event | category | flops | bytes accessed | tf_op | source)
XLA Modules:
  0.0 30.0 jit_solution(864197814215907130)
XLA Ops:
  0.6 2.6 %shard_map.50 = (f32[4,64,128]{2,1,0:T(8,128)S(1)}, f32[328,128]{1,0:T(8,128)S(1)}, f32[16,128]{1,0:T(8,128)S(1)}, f32[16,128]{1,0:T(8,128)S(1)}) custom-call(bf16[32,4,64,128]{3,2,1,0:T(8,128)(2,1)} %f_hbm.1, bf16[27,32]{1,0:T(8,128)(2,1)} %w_hbm.1, s32[4,64,128]{2,1,0:T(8,128)} %mask_hbm.1), custom_call_target="tpu_custom_call" | custom-call | tf_op jit(solution)/shard_map/pallas_call | solution.py:23
  3.3 0.3 %collective-permute-start = (f32[328,128]{1,0:T(8,128)S(1)}, f32[328,128]{1,0:T(8,128)S(1)}, u32[]{:S(2)}, u32[]{:S(2)}) collective-permute-start(f32[328,128]{1,0:T(8,128)S(1)} %get-tuple-element.15.own_ref), channel_id=1, source_target_pairs={{0,16},{4,20},{8,24},{12,28},{16,0},{20,4},{24,8},{28,12},{1,17},{... | collective-permute-start | bytes 503816 | tf_op jit(solution)/shard_map/ppermute | solution.py:463
  3.6 1.0 %collective-permute-start.1 = (f32[16,128]{1,0:T(8,128)S(1)}, f32[16,128]{1,0:T(8,128)S(1)}, u32[]{:S(2)}, u32[]{:S(2)}) collective-permute-start(f32[16,128]{1,0:T(8,128)S(1)} %get-tuple-element.16), channel_id=1, source_target_pairs={{0,4},{4,0},{8,12},{12,8},{16,20},{20,16},{24,28},{28,24},{1,5},{5... | collective-permute-start | bytes 24584 | tf_op jit(solution)/shard_map/ppermute | solution.py:463
  4.5 1.1 %collective-permute-start.2 = (f32[16,128]{1,0:T(8,128)S(1)}, f32[16,128]{1,0:T(8,128)S(1)}, u32[]{:S(2)}, u32[]{:S(2)}) collective-permute-start(f32[16,128]{1,0:T(8,128)S(1)} %get-tuple-element.17), channel_id=1, source_target_pairs={{0,12},{4,8},{8,4},{12,0},{16,28},{20,24},{24,20},{28,16},{1,13},{... | collective-permute-start | bytes 24584 | tf_op jit(solution)/shard_map/ppermute | solution.py:463
  5.7 1.6 %collective-permute-start.3 = (f32[16,128]{1,0:T(8,128)S(1)}, f32[16,128]{1,0:T(8,128)S(1)}, u32[]{:S(2)}, u32[]{:S(2)}) collective-permute-start(f32[16,128]{1,0:T(8,128)S(1)} %get-tuple-element.16), channel_id=1, source_target_pairs={{0,20},{4,16},{8,28},{12,24},{16,4},{20,0},{24,12},{28,8},{1,21},{... | collective-permute-start | bytes 24584 | tf_op jit(solution)/shard_map/ppermute | solution.py:463
  7.3 0.1 collective-permute-start.4
  7.4 0.0 collective-permute-done.1.chip_ref
  7.4 0.6 %collective-permute-done.2.cross_ref = f32[16,128]{1,0:T(8,128)S(1)} collective-permute-done((f32[16,128]{1,0:T(8,128)S(1)}, f32[16,128]{1,0:T(8,128)S(1)}, u32[]{:S(2)}, u32[]{:S(2)}) %collective-permute-start.2) | collective-permute-done | bytes 8224 | tf_op jit(solution)/shard_map/ppermute | solution.py:463
  7.9 1.8 %collective-permute-done.3.xchip_ref = f32[16,128]{1,0:T(8,128)S(1)} collective-permute-done((f32[16,128]{1,0:T(8,128)S(1)}, f32[16,128]{1,0:T(8,128)S(1)}, u32[]{:S(2)}, u32[]{:S(2)}) %collective-permute-start.3) | collective-permute-done | bytes 8224 | tf_op jit(solution)/shard_map/ppermute | solution.py:463
  9.7 1.5 %collective-permute-done.4.xcross_ref = f32[16,128]{1,0:T(8,128)S(1)} collective-permute-done((f32[16,128]{1,0:T(8,128)S(1)}, f32[16,128]{1,0:T(8,128)S(1)}, u32[]{:S(2)}, u32[]{:S(2)}) %collective-permute-start.4) | collective-permute-done | bytes 8224 | tf_op jit(solution)/shard_map/ppermute | solution.py:463
  11.3 0.0 collective-permute-done.far_ref
  11.3 0.3 %shard_map.51 = (f32[4,64,128]{2,1,0:T(8,128)S(1)}, f32[136,256]{1,0:T(8,128)S(1)}) custom-call(f32[4,64,128]{2,1,0:T(8,128)S(1)} %get-tuple-element.14.s_ref, f32[328,128]{1,0:T(8,128)S(1)} %get-tuple-element.15.own_ref, f32[328,128]{1,0:T(8,128)S(1)} %collective-permute-done.far_ref, f32[16,128]{1,0:T(8,128)S(1)} %collective-permute-done.1.chip_ref, ...), custom_call_target="tpu_custom_call" | custom-call | tf_op jit(solution)/shard_map/pallas_call | solution.py:23
  11.6 1.4 %collective-permute-start.5 = (f32[136,256]{1,0:T(8,128)S(1)}, f32[136,256]{1,0:T(8,128)S(1)}, u32[]{:S(2)}, u32[]{:S(2)}) collective-permute-start(f32[136,256]{1,0:T(8,128)S(1)} %get-tuple-element.19.zm_ref), channel_id=1, source_target_pairs={{0,1},{1,0},{2,3},{3,2},{4,5},{5,4},{6,7},{7,6},{8,9},{9,8},{10,11... | collective-permute-start | bytes 417800 | tf_op jit(solution)/shard_map/ppermute | solution.py:479
  13.0 1.9 %collective-permute-start.6 = (f32[136,256]{1,0:T(8,128)S(1)}, f32[136,256]{1,0:T(8,128)S(1)}, u32[]{:S(2)}, u32[]{:S(2)}) collective-permute-start(f32[136,256]{1,0:T(8,128)S(1)} %get-tuple-element.19.zm_ref), channel_id=1, source_target_pairs={{1,2},{2,1},{5,6},{6,5},{9,10},{10,9},{13,14},{14,13},{17,18},{18,... | collective-permute-start | bytes 417800 | tf_op jit(solution)/shard_map/ppermute | solution.py:480
  14.9 1.4 %shard_map.52 = (f32[128,256]{1,0:T(8,128)S(1)}, f32[262,8,128]{2,1,0:T(8,128)S(1)}) custom-call(f32[136,256]{1,0:T(8,128)S(1)} %get-tuple-element.19.zm_ref), custom_call_target="tpu_custom_call" | custom-call | tf_op jit(solution)/shard_map/pallas_call | solution.py:23
  16.3 0.6 %collective-permute-done.5.got_ref.even_ref = f32[136,256]{1,0:T(8,128)S(1)} collective-permute-done((f32[136,256]{1,0:T(8,128)S(1)}, f32[136,256]{1,0:T(8,128)S(1)}, u32[]{:S(2)}, u32[]{:S(2)}) %collective-permute-start.5) | collective-permute-done | bytes 139296 | tf_op jit(solution)/shard_map/ppermute | solution.py:479
  17.0 0.8 %shard_map.53.acc_ref = f32[128,256]{1,0:T(8,128)S(1)} custom-call(f32[128,256]{1,0:T(8,128)S(1)} %get-tuple-element.20.acc_ref, f32[262,8,128]{2,1,0:T(8,128)S(1)} %get-tuple-element.21.table, f32[136,256]{1,0:T(8,128)S(1)} %get-tuple-element.19.zm_ref, f32[136,256]{1,0:T(8,128)S(1)} %collective-permute-done.5.got_ref.even_ref), custom_call_target="tpu_custom_call" | custom-call | tf_op jit(solution)/shard_map/pallas_call | solution.py:23
  17.7 2.1 %collective-permute-done.6.got_ref.odd_ref = f32[136,256]{1,0:T(8,128)S(1)} collective-permute-done((f32[136,256]{1,0:T(8,128)S(1)}, f32[136,256]{1,0:T(8,128)S(1)}, u32[]{:S(2)}, u32[]{:S(2)}) %collective-permute-start.6) | collective-permute-done | bytes 139296 | tf_op jit(solution)/shard_map/ppermute | solution.py:480
  19.8 0.9 %shard_map.54._.own_ref = f32[4,64,128]{2,1,0:T(8,128)S(1)} custom-call(f32[128,256]{1,0:T(8,128)S(1)} %shard_map.53.acc_ref, f32[262,8,128]{2,1,0:T(8,128)S(1)} %get-tuple-element.21.table, f32[136,256]{1,0:T(8,128)S(1)} %get-tuple-element.19.zm_ref, f32[136,256]{1,0:T(8,128)S(1)} %collective-permute-done.6.got_ref.odd_ref), custom_call_target="tpu_custom_call" | custom-call | tf_op jit(solution)/shard_map/pallas_call | solution.py:23
  20.8 0.3 collective-permute-start.7
  21.1 1.4 %collective-permute-start.8 = (f32[4,64,128]{2,1,0:T(8,128)S(1)}, f32[4,64,128]{2,1,0:T(8,128)S(1)}, u32[]{:S(2)}, u32[]{:S(2)}) collective-permute-start(f32[4,64,128]{2,1,0:T(8,128)S(1)} %shard_map.54._.own_ref), channel_id=1, source_target_pairs={{0,4},{4,0},{8,12},{12,8},{1,5},{5,1},{9,13},{13,9},{2,6},{6,2},{1... | collective-permute-start | bytes 393224 | tf_op jit(solution)/shard_map/ppermute | solution.py:457
  22.4 3.0 %collective-permute-start.9 = (f32[4,64,128]{2,1,0:T(8,128)S(1)}, f32[4,64,128]{2,1,0:T(8,128)S(1)}, u32[]{:S(2)}, u32[]{:S(2)}) collective-permute-start(f32[4,64,128]{2,1,0:T(8,128)S(1)} %shard_map.54._.own_ref), channel_id=1, source_target_pairs={{4,8},{8,4},{5,9},{9,5},{6,10},{10,6},{7,11},{11,7},{20,24},{24,20... | collective-permute-start | bytes 393224 | tf_op jit(solution)/shard_map/ppermute | solution.py:577
  25.5 0.8 %shard_map.56 = (f32[4,64,128]{2,1,0:T(8,128)S(1)}, f32[120,8,128]{2,1,0:T(8,128)S(1)}, f32[120,8,128]{2,1,0:T(8,128)S(1)}, f32[120,8,128]{2,1,0:T(8,128)S(1)}) custom-call(f32[4,64,128]{2,1,0:T(8,128)S(1)} %shard_map.54._.own_ref), custom_call_target="tpu_custom_call" | custom-call | tf_op jit(solution)/shard_map/pallas_call | solution.py:23
  26.2 0.8 %shard_map.55 = f32[4,64,128]{2,1,0:T(8,128)} custom-call(f32[4,64,128]{2,1,0:T(8,128)S(1)} %get-tuple-element.18.score_in, f32[136,256]{1,0:T(8,128)S(1)} %collective-permute-done.5.got_ref.even_ref, f32[136,256]{1,0:T(8,128)S(1)} %collective-permute-done.6.got_ref.odd_ref, f32[4,64,128]{2,1,0:T(8,128)S(1)} %shard_map.54._.own_ref), custom_call_target="tpu_custom_call" | custom-call | tf_op jit(solution)/shard_map/pallas_call | solution.py:23
  27.0 0.0 collective-permute-done.7.ref
  27.0 0.6 %shard_map.57.start_ref = f32[4,64,128]{2,1,0:T(8,128)S(1)} custom-call(f32[4,64,128]{2,1,0:T(8,128)S(1)} %get-tuple-element.22.start_ref, f32[4,64,128]{2,1,0:T(8,128)S(1)} %collective-permute-done.7.ref, f32[120,8,128]{2,1,0:T(8,128)S(1)} %get-tuple-element.23.table), custom_call_target="tpu_custom_call" | custom-call | tf_op jit(solution)/shard_map/pallas_call | solution.py:23
  27.7 0.0 collective-permute-done.8.ref
  27.7 0.6 %shard_map.58.start_ref = f32[4,64,128]{2,1,0:T(8,128)S(1)} custom-call(f32[4,64,128]{2,1,0:T(8,128)S(1)} %shard_map.57.start_ref, f32[4,64,128]{2,1,0:T(8,128)S(1)} %collective-permute-done.8.ref, f32[120,8,128]{2,1,0:T(8,128)S(1)} %get-tuple-element.24.table), custom_call_target="tpu_custom_call" | custom-call | tf_op jit(solution)/shard_map/pallas_call | solution.py:23
  28.3 0.4 %collective-permute-done.9.ref = f32[4,64,128]{2,1,0:T(8,128)S(1)} collective-permute-done((f32[4,64,128]{2,1,0:T(8,128)S(1)}, f32[4,64,128]{2,1,0:T(8,128)S(1)}, u32[]{:S(2)}, u32[]{:S(2)}) %collective-permute-start.9) | collective-permute-done | bytes 131104 | tf_op jit(solution)/shard_map/ppermute | solution.py:577
  28.7 1.3 %shard_map.59 = f32[4,64,128]{2,1,0:T(8,128)} custom-call(f32[4,64,128]{2,1,0:T(8,128)S(1)} %shard_map.58.start_ref, f32[4,64,128]{2,1,0:T(8,128)S(1)} %collective-permute-done.9.ref, f32[120,8,128]{2,1,0:T(8,128)S(1)} %get-tuple-element.25.table), custom_call_target="tpu_custom_call" | custom-call | tf_op jit(solution)/shard_map/pallas_call | solution.py:23
Async XLA Ops:
  3.3 8.0 %collective-permute-start = (f32[328,128]{1,0:T(8,128)S(1)}, f32[328,128]{1,0:T(8,128)S(1)}, u32[]{:S(2)}, u32[]{:S(2)}) collective-permute-start(f32[328,128]{1,0:T(8,128)S(1)} %get-tuple-element.15.own_ref), channel_id=1, source_target_pairs={{0,16},{4,20},{8,24},{12,28},{16,0},{20,4},{24,8},{28,12},{1,17},{... | collective-permute-start | bytes 503816 | tf_op jit(solution)/shard_map/ppermute | solution.py:463
  3.6 3.8 %collective-permute-start.1 = (f32[16,128]{1,0:T(8,128)S(1)}, f32[16,128]{1,0:T(8,128)S(1)}, u32[]{:S(2)}, u32[]{:S(2)}) collective-permute-start(f32[16,128]{1,0:T(8,128)S(1)} %get-tuple-element.16), channel_id=1, source_target_pairs={{0,4},{4,0},{8,12},{12,8},{16,20},{20,16},{24,28},{28,24},{1,5},{5... | collective-permute-start | bytes 24584 | tf_op jit(solution)/shard_map/ppermute | solution.py:463
  4.5 3.4 %collective-permute-start.2 = (f32[16,128]{1,0:T(8,128)S(1)}, f32[16,128]{1,0:T(8,128)S(1)}, u32[]{:S(2)}, u32[]{:S(2)}) collective-permute-start(f32[16,128]{1,0:T(8,128)S(1)} %get-tuple-element.17), channel_id=1, source_target_pairs={{0,12},{4,8},{8,4},{12,0},{16,28},{20,24},{24,20},{28,16},{1,13},{... | collective-permute-start | bytes 24584 | tf_op jit(solution)/shard_map/ppermute | solution.py:463
  5.7 4.1 %collective-permute-start.3 = (f32[16,128]{1,0:T(8,128)S(1)}, f32[16,128]{1,0:T(8,128)S(1)}, u32[]{:S(2)}, u32[]{:S(2)}) collective-permute-start(f32[16,128]{1,0:T(8,128)S(1)} %get-tuple-element.16), channel_id=1, source_target_pairs={{0,20},{4,16},{8,28},{12,24},{16,4},{20,0},{24,12},{28,8},{1,21},{... | collective-permute-start | bytes 24584 | tf_op jit(solution)/shard_map/ppermute | solution.py:463
  7.3 4.0 %collective-permute-start.4 = (f32[16,128]{1,0:T(8,128)S(1)}, f32[16,128]{1,0:T(8,128)S(1)}, u32[]{:S(2)}, u32[]{:S(2)}) collective-permute-start(f32[16,128]{1,0:T(8,128)S(1)} %get-tuple-element.17), channel_id=1, source_target_pairs={{0,28},{4,24},{8,20},{12,16},{16,12},{20,8},{24,4},{28,0},{1,29},{... | collective-permute-start | bytes 24584 | tf_op jit(solution)/shard_map/ppermute | solution.py:463
  11.6 5.4 %collective-permute-start.5 = (f32[136,256]{1,0:T(8,128)S(1)}, f32[136,256]{1,0:T(8,128)S(1)}, u32[]{:S(2)}, u32[]{:S(2)}) collective-permute-start(f32[136,256]{1,0:T(8,128)S(1)} %get-tuple-element.19.zm_ref), channel_id=1, source_target_pairs={{0,1},{1,0},{2,3},{3,2},{4,5},{5,4},{6,7},{7,6},{8,9},{9,8},{10,11... | collective-permute-start | bytes 417800 | tf_op jit(solution)/shard_map/ppermute | solution.py:479
  13.0 6.9 %collective-permute-start.6 = (f32[136,256]{1,0:T(8,128)S(1)}, f32[136,256]{1,0:T(8,128)S(1)}, u32[]{:S(2)}, u32[]{:S(2)}) collective-permute-start(f32[136,256]{1,0:T(8,128)S(1)} %get-tuple-element.19.zm_ref), channel_id=1, source_target_pairs={{1,2},{2,1},{5,6},{6,5},{9,10},{10,9},{13,14},{14,13},{17,18},{18,... | collective-permute-start | bytes 417800 | tf_op jit(solution)/shard_map/ppermute | solution.py:480
  20.8 6.3 %collective-permute-start.7 = (f32[4,64,128]{2,1,0:T(8,128)S(1)}, f32[4,64,128]{2,1,0:T(8,128)S(1)}, u32[]{:S(2)}, u32[]{:S(2)}) collective-permute-start(f32[4,64,128]{2,1,0:T(8,128)S(1)} %shard_map.54._.own_ref), channel_id=1, source_target_pairs={{0,8},{4,12},{8,0},{12,4},{1,9},{5,13},{9,1},{13,5},{2,10},{6,14},... | collective-permute-start | bytes 393224 | tf_op jit(solution)/shard_map/ppermute | solution.py:457
  21.1 6.6 %collective-permute-start.8 = (f32[4,64,128]{2,1,0:T(8,128)S(1)}, f32[4,64,128]{2,1,0:T(8,128)S(1)}, u32[]{:S(2)}, u32[]{:S(2)}) collective-permute-start(f32[4,64,128]{2,1,0:T(8,128)S(1)} %shard_map.54._.own_ref), channel_id=1, source_target_pairs={{0,4},{4,0},{8,12},{12,8},{1,5},{5,1},{9,13},{13,9},{2,6},{6,2},{1... | collective-permute-start | bytes 393224 | tf_op jit(solution)/shard_map/ppermute | solution.py:457
  22.4 6.3 %collective-permute-start.9 = (f32[4,64,128]{2,1,0:T(8,128)S(1)}, f32[4,64,128]{2,1,0:T(8,128)S(1)}, u32[]{:S(2)}, u32[]{:S(2)}) collective-permute-start(f32[4,64,128]{2,1,0:T(8,128)S(1)} %shard_map.54._.own_ref), channel_id=1, source_target_pairs={{4,8},{8,4},{5,9},{9,5},{6,10},{10,6},{7,11},{11,7},{20,24},{24,20... | collective-permute-start | bytes 393224 | tf_op jit(solution)/shard_map/ppermute | solution.py:577

commit v2 on v1

--- a/solution.py
+++ b/solution.py
@@ -475,9 +475,22 @@
 
 
 def z_swaps(value):
-    n = lax.axis_size("gz")
+    nx, ny, n = (lax.axis_size(axis) for axis in ("gx", "gy", "gz"))
     even = lax.ppermute(value, "gz", [(i, i ^ 1) for i in range(n)])
-    return even, lax.ppermute(value, "gz", [(i, i + 1 if i % 2 else i - 1) for i in range(1, n - 1)])
+    pairs = []
+    for i in range(nx * ny * n):
+        xy, z = i // n, i % n
+        pairs.append((i, (xy ^ 1) * n + z if z in (0, n - 1) else xy * n + (z + 1 if z % 2 else z - 1)))
+    return even, lax.ppermute(value, ("gx", "gy", "gz"), pairs)
+
+
+def corner_swap(value):
+    nx, ny = lax.axis_size("gx"), lax.axis_size("gy")
+    pairs = []
+    for i in range(nx * ny):
+        x, y = i // ny, i % ny
+        pairs.append((i, (x ^ 1) * ny + y if y in (0, ny - 1) else x * ny + (y + 1 if y % 2 else y - 1)))
+    return lax.ppermute(value, ("gx", "gy"), pairs)
 
 
 def conv(features, conv_weight, mask, planes, count, paired):
@@ -574,7 +587,7 @@
     tables = (2 * size_y - 8, 8, LANES)
     across, chip = swap(best, "gy", 2), swap(best, "gy", 1)
     near, *kept = call(y_own_kernel, [brick, tables, tables, tables], [pltpu.VMEM(tables, jnp.float32)])(best)
-    blocks = {2: across, 1: chip, 3: lax.ppermute(best, "gy", [(1, 2), (2, 1)])}
+    blocks = {2: across, 1: chip, 3: corner_swap(best)}
     for hop, block in blocks.items():
         far = functools.partial(y_far_kernel, hop, 1.0 / RADIUS if hop == 3 else 1.0)
         (near,) = call(far, [brick])(near, block, kept[hop - 1])

time: 30.3 us -> 27.3 us (0.901)
  starting transfers between devices: 12.1 us -> 8.26 us
  waiting for transfers between devices: 7.02 us -> 7.86 us
    ppermute x2, starting transfers between devices: 4.93 us -> 1.13 us  [the longest x1 1.13 us: corner_swap(): return lax.ppermute(value, ('gx', 'gy'), pairs)]
    ppermute x1, waiting for transfers between devices: 0.65 us -> 2.56 us  [z_swaps(): even = lax.ppermute(value, 'gz', [(i, i ^ 1) for i in range(n)])]
    ppermute x2, waiting for transfers between devices: 2.48 us -> 1.4 us  [the longest x1 1.19 us: corner_swap(): return lax.ppermute(value, ('gx', 'gy'), pairs)]
  transfers between devices with their start and end apart: 10 -> 10, of which waited for: 6 -> 6; matrix products, arithmetic and copies ran while one was open for 0% -> 0% of each run, Pallas kernels for 17% -> 19%
where the time goes in v2:
time: 27.3 us; the launch traced here: 27 us
  Pallas kernels  10.2 us (37%)
  starting transfers between devices  8.26 us (30%)
  waiting for transfers between devices  7.86 us (29%)
  between operations  0.7 us (3%)
    pallas_call x10, Pallas kernels, run(): pl.pallas_call(kernel, out_shape=shapes, in_specs=in_specs or [VMEM] * le...  10.2 us
    ppermute x5, starting transfers between devices, swap_xy(): return lax.ppermute(value, ('gx', 'gy'), pairs)  4.09 us
    ppermute x5, waiting for transfers between devices, swap_xy(): return lax.ppermute(value, ('gx', 'gy'), pairs)  3.89 us
    ppermute x1, waiting for transfers between devices, z_swaps(): even = lax.ppermute(value, 'gz', [(i, i ^ 1) for i in range(n)])  2.56 us
    ppermute x2, starting transfers between devices, swap(): return lax.ppermute(value, axis, [(i, i ^ hop) for i in range(n)])  1.67 us
    ppermute x1, starting transfers between devices, z_swaps(): even = lax.ppermute(value, 'gz', [(i, i ^ 1) for i in range(n)])  1.36 us
    ppermute x1, waiting for transfers between devices, corner_swap(): return lax.ppermute(value, ('gx', 'gy'), pairs)  1.19 us
    ppermute x1, starting transfers between devices, corner_swap(): return lax.ppermute(value, ('gx', 'gy'), pairs)  1.13 us
  transfers between devices with their start and end apart: 10, of which 6 were waited for; matrix products, arithmetic and copies ran while one was open for 0% of the time, Pallas kernels for 19%

profile of v2, /device:TPU:19, one launch (start us, length us, event | category | flops | bytes accessed | tf_op | source)
XLA Modules:
  0.0 27.0 jit_solution(6981362704651681889)
XLA Ops:
  0.6 2.6 %shard_map.50 = (f32[4,64,128]{2,1,0:T(8,128)S(1)}, f32[328,128]{1,0:T(8,128)S(1)}, f32[16,128]{1,0:T(8,128)S(1)}, f32[16,128]{1,0:T(8,128)S(1)}) custom-call(bf16[32,4,64,128]{3,2,1,0:T(8,128)(2,1)} %f_hbm.1, bf16[27,32]{1,0:T(8,128)(2,1)} %w_hbm.1, s32[4,64,128]{2,1,0:T(8,128)} %mask_hbm.1), custom_call_target="tpu_custom_call" | custom-call | tf_op jit(solution)/shard_map/pallas_call | solution.py:23
  3.3 0.3 %collective-permute-start = (f32[328,128]{1,0:T(8,128)S(1)}, f32[328,128]{1,0:T(8,128)S(1)}, u32[]{:S(2)}, u32[]{:S(2)}) collective-permute-start(f32[328,128]{1,0:T(8,128)S(1)} %get-tuple-element.15.own_ref), channel_id=1, source_target_pairs={{0,16},{4,20},{8,24},{12,28},{16,0},{20,4},{24,8},{28,12},{1,17},{... | collective-permute-start | bytes 503816 | tf_op jit(solution)/shard_map/ppermute | solution.py:463
  3.6 1.0 %collective-permute-start.1 = (f32[16,128]{1,0:T(8,128)S(1)}, f32[16,128]{1,0:T(8,128)S(1)}, u32[]{:S(2)}, u32[]{:S(2)}) collective-permute-start(f32[16,128]{1,0:T(8,128)S(1)} %get-tuple-element.16), channel_id=1, source_target_pairs={{0,4},{4,0},{8,12},{12,8},{16,20},{20,16},{24,28},{28,24},{1,5},{5... | collective-permute-start | bytes 24584 | tf_op jit(solution)/shard_map/ppermute | solution.py:463
  4.5 1.1 %collective-permute-start.2 = (f32[16,128]{1,0:T(8,128)S(1)}, f32[16,128]{1,0:T(8,128)S(1)}, u32[]{:S(2)}, u32[]{:S(2)}) collective-permute-start(f32[16,128]{1,0:T(8,128)S(1)} %get-tuple-element.17), channel_id=1, source_target_pairs={{0,12},{4,8},{8,4},{12,0},{16,28},{20,24},{24,20},{28,16},{1,13},{... | collective-permute-start | bytes 24584 | tf_op jit(solution)/shard_map/ppermute | solution.py:463
  5.7 1.6 %collective-permute-start.3 = (f32[16,128]{1,0:T(8,128)S(1)}, f32[16,128]{1,0:T(8,128)S(1)}, u32[]{:S(2)}, u32[]{:S(2)}) collective-permute-start(f32[16,128]{1,0:T(8,128)S(1)} %get-tuple-element.16), channel_id=1, source_target_pairs={{0,20},{4,16},{8,28},{12,24},{16,4},{20,0},{24,12},{28,8},{1,21},{... | collective-permute-start | bytes 24584 | tf_op jit(solution)/shard_map/ppermute | solution.py:463
  7.3 0.1 collective-permute-start.4
  7.4 0.0 collective-permute-done.1.chip_ref
  7.4 0.6 %collective-permute-done.2.cross_ref = f32[16,128]{1,0:T(8,128)S(1)} collective-permute-done((f32[16,128]{1,0:T(8,128)S(1)}, f32[16,128]{1,0:T(8,128)S(1)}, u32[]{:S(2)}, u32[]{:S(2)}) %collective-permute-start.2) | collective-permute-done | bytes 8224 | tf_op jit(solution)/shard_map/ppermute | solution.py:463
  7.9 1.8 %collective-permute-done.3.xchip_ref = f32[16,128]{1,0:T(8,128)S(1)} collective-permute-done((f32[16,128]{1,0:T(8,128)S(1)}, f32[16,128]{1,0:T(8,128)S(1)}, u32[]{:S(2)}, u32[]{:S(2)}) %collective-permute-start.3) | collective-permute-done | bytes 8224 | tf_op jit(solution)/shard_map/ppermute | solution.py:463
  9.7 1.5 %collective-permute-done.4.xcross_ref = f32[16,128]{1,0:T(8,128)S(1)} collective-permute-done((f32[16,128]{1,0:T(8,128)S(1)}, f32[16,128]{1,0:T(8,128)S(1)}, u32[]{:S(2)}, u32[]{:S(2)}) %collective-permute-start.4) | collective-permute-done | bytes 8224 | tf_op jit(solution)/shard_map/ppermute | solution.py:463
  11.3 0.0 collective-permute-done.far_ref
  11.3 0.3 %shard_map.51 = (f32[4,64,128]{2,1,0:T(8,128)S(1)}, f32[136,256]{1,0:T(8,128)S(1)}) custom-call(f32[4,64,128]{2,1,0:T(8,128)S(1)} %get-tuple-element.14.s_ref, f32[328,128]{1,0:T(8,128)S(1)} %get-tuple-element.15.own_ref, f32[328,128]{1,0:T(8,128)S(1)} %collective-permute-done.far_ref, f32[16,128]{1,0:T(8,128)S(1)} %collective-permute-done.1.chip_ref, ...), custom_call_target="tpu_custom_call" | custom-call | tf_op jit(solution)/shard_map/pallas_call | solution.py:23
  11.6 1.4 %collective-permute-start.5 = (f32[136,256]{1,0:T(8,128)S(1)}, f32[136,256]{1,0:T(8,128)S(1)}, u32[]{:S(2)}, u32[]{:S(2)}) collective-permute-start(f32[136,256]{1,0:T(8,128)S(1)} %get-tuple-element.19.zm_ref), channel_id=1, source_target_pairs={{0,1},{1,0},{2,3},{3,2},{4,5},{5,4},{6,7},{7,6},{8,9},{9,8},{10,11... | collective-permute-start | bytes 417800 | tf_op jit(solution)/shard_map/ppermute | solution.py:479
  13.0 0.0 collective-permute-start.6
  13.0 1.4 %shard_map.52 = (f32[128,256]{1,0:T(8,128)S(1)}, f32[262,8,128]{2,1,0:T(8,128)S(1)}) custom-call(f32[136,256]{1,0:T(8,128)S(1)} %get-tuple-element.19.zm_ref), custom_call_target="tpu_custom_call" | custom-call | tf_op jit(solution)/shard_map/pallas_call | solution.py:23
  14.4 2.6 %collective-permute-done.5.got_ref.even_ref = f32[136,256]{1,0:T(8,128)S(1)} collective-permute-done((f32[136,256]{1,0:T(8,128)S(1)}, f32[136,256]{1,0:T(8,128)S(1)}, u32[]{:S(2)}, u32[]{:S(2)}) %collective-permute-start.5) | collective-permute-done | bytes 139296 | tf_op jit(solution)/shard_map/ppermute | solution.py:479
  17.0 0.8 %shard_map.53.acc_ref = f32[128,256]{1,0:T(8,128)S(1)} custom-call(f32[128,256]{1,0:T(8,128)S(1)} %get-tuple-element.20.acc_ref, f32[262,8,128]{2,1,0:T(8,128)S(1)} %get-tuple-element.21.table, f32[136,256]{1,0:T(8,128)S(1)} %get-tuple-element.19.zm_ref, f32[136,256]{1,0:T(8,128)S(1)} %collective-permute-done.5.got_ref.even_ref), custom_call_target="tpu_custom_call" | custom-call | tf_op jit(solution)/shard_map/pallas_call | solution.py:23
  17.7 0.2 collective-permute-done.6.got_ref.odd_ref
  18.0 0.9 %shard_map.54._.own_ref = f32[4,64,128]{2,1,0:T(8,128)S(1)} custom-call(f32[128,256]{1,0:T(8,128)S(1)} %shard_map.53.acc_ref, f32[262,8,128]{2,1,0:T(8,128)S(1)} %get-tuple-element.21.table, f32[136,256]{1,0:T(8,128)S(1)} %get-tuple-element.19.zm_ref, f32[136,256]{1,0:T(8,128)S(1)} %collective-permute-done.6.got_ref.odd_ref), custom_call_target="tpu_custom_call" | custom-call | tf_op jit(solution)/shard_map/pallas_call | solution.py:23
  18.9 0.3 %collective-permute-start.7 = (f32[4,64,128]{2,1,0:T(8,128)S(1)}, f32[4,64,128]{2,1,0:T(8,128)S(1)}, u32[]{:S(2)}, u32[]{:S(2)}) collective-permute-start(f32[4,64,128]{2,1,0:T(8,128)S(1)} %shard_map.54._.own_ref), channel_id=1, source_target_pairs={{0,8},{4,12},{8,0},{12,4},{1,9},{5,13},{9,1},{13,5},{2,10},{6,14},... | collective-permute-start | bytes 393224 | tf_op jit(solution)/shard_map/ppermute | solution.py:457
  19.2 1.4 %collective-permute-start.8 = (f32[4,64,128]{2,1,0:T(8,128)S(1)}, f32[4,64,128]{2,1,0:T(8,128)S(1)}, u32[]{:S(2)}, u32[]{:S(2)}) collective-permute-start(f32[4,64,128]{2,1,0:T(8,128)S(1)} %shard_map.54._.own_ref), channel_id=1, source_target_pairs={{0,4},{4,0},{8,12},{12,8},{1,5},{5,1},{9,13},{13,9},{2,6},{6,2},{1... | collective-permute-start | bytes 393224 | tf_op jit(solution)/shard_map/ppermute | solution.py:457
  20.6 1.1 %collective-permute-start.9 = (f32[4,64,128]{2,1,0:T(8,128)S(1)}, f32[4,64,128]{2,1,0:T(8,128)S(1)}, u32[]{:S(2)}, u32[]{:S(2)}) collective-permute-start(f32[4,64,128]{2,1,0:T(8,128)S(1)} %shard_map.54._.own_ref), channel_id=1, source_target_pairs={{0,16},{4,8},{8,4},{12,28},{16,0},{20,24},{24,20},{28,12},{1,17},{... | collective-permute-start | bytes 393224 | tf_op jit(solution)/shard_map/ppermute | solution.py:493
  21.7 0.8 %shard_map.56 = (f32[4,64,128]{2,1,0:T(8,128)S(1)}, f32[120,8,128]{2,1,0:T(8,128)S(1)}, f32[120,8,128]{2,1,0:T(8,128)S(1)}, f32[120,8,128]{2,1,0:T(8,128)S(1)}) custom-call(f32[4,64,128]{2,1,0:T(8,128)S(1)} %shard_map.54._.own_ref), custom_call_target="tpu_custom_call" | custom-call | tf_op jit(solution)/shard_map/pallas_call | solution.py:23
  22.5 0.8 %shard_map.55 = f32[4,64,128]{2,1,0:T(8,128)} custom-call(f32[4,64,128]{2,1,0:T(8,128)S(1)} %get-tuple-element.18.score_in, f32[136,256]{1,0:T(8,128)S(1)} %collective-permute-done.5.got_ref.even_ref, f32[136,256]{1,0:T(8,128)S(1)} %collective-permute-done.6.got_ref.odd_ref, f32[4,64,128]{2,1,0:T(8,128)S(1)} %shard_map.54._.own_ref), custom_call_target="tpu_custom_call" | custom-call | tf_op jit(solution)/shard_map/pallas_call | solution.py:23
  23.2 0.0 collective-permute-done.7.ref
  23.2 0.6 %shard_map.57.start_ref = f32[4,64,128]{2,1,0:T(8,128)S(1)} custom-call(f32[4,64,128]{2,1,0:T(8,128)S(1)} %get-tuple-element.22.start_ref, f32[4,64,128]{2,1,0:T(8,128)S(1)} %collective-permute-done.7.ref, f32[120,8,128]{2,1,0:T(8,128)S(1)} %get-tuple-element.23.table), custom_call_target="tpu_custom_call" | custom-call | tf_op jit(solution)/shard_map/pallas_call | solution.py:23
  23.9 0.0 collective-permute-done.8.ref
  23.9 0.6 %shard_map.58.start_ref = f32[4,64,128]{2,1,0:T(8,128)S(1)} custom-call(f32[4,64,128]{2,1,0:T(8,128)S(1)} %shard_map.57.start_ref, f32[4,64,128]{2,1,0:T(8,128)S(1)} %collective-permute-done.8.ref, f32[120,8,128]{2,1,0:T(8,128)S(1)} %get-tuple-element.24.table), custom_call_target="tpu_custom_call" | custom-call | tf_op jit(solution)/shard_map/pallas_call | solution.py:23
  24.5 1.2 %collective-permute-done.9.ref = f32[4,64,128]{2,1,0:T(8,128)S(1)} collective-permute-done((f32[4,64,128]{2,1,0:T(8,128)S(1)}, f32[4,64,128]{2,1,0:T(8,128)S(1)}, u32[]{:S(2)}, u32[]{:S(2)}) %collective-permute-start.9) | collective-permute-done | bytes 131104 | tf_op jit(solution)/shard_map/ppermute | solution.py:493
  25.7 1.3 %shard_map.59 = f32[4,64,128]{2,1,0:T(8,128)} custom-call(f32[4,64,128]{2,1,0:T(8,128)S(1)} %shard_map.58.start_ref, f32[4,64,128]{2,1,0:T(8,128)S(1)} %collective-permute-done.9.ref, f32[120,8,128]{2,1,0:T(8,128)S(1)} %get-tuple-element.25.table), custom_call_target="tpu_custom_call" | custom-call | tf_op jit(solution)/shard_map/pallas_call | solution.py:23
Async XLA Ops:
  3.3 8.0 %collective-permute-start = (f32[328,128]{1,0:T(8,128)S(1)}, f32[328,128]{1,0:T(8,128)S(1)}, u32[]{:S(2)}, u32[]{:S(2)}) collective-permute-start(f32[328,128]{1,0:T(8,128)S(1)} %get-tuple-element.15.own_ref), channel_id=1, source_target_pairs={{0,16},{4,20},{8,24},{12,28},{16,0},{20,4},{24,8},{28,12},{1,17},{... | collective-permute-start | bytes 503816 | tf_op jit(solution)/shard_map/ppermute | solution.py:463
  3.6 3.8 %collective-permute-start.1 = (f32[16,128]{1,0:T(8,128)S(1)}, f32[16,128]{1,0:T(8,128)S(1)}, u32[]{:S(2)}, u32[]{:S(2)}) collective-permute-start(f32[16,128]{1,0:T(8,128)S(1)} %get-tuple-element.16), channel_id=1, source_target_pairs={{0,4},{4,0},{8,12},{12,8},{16,20},{20,16},{24,28},{28,24},{1,5},{5... | collective-permute-start | bytes 24584 | tf_op jit(solution)/shard_map/ppermute | solution.py:463
  4.5 3.4 %collective-permute-start.2 = (f32[16,128]{1,0:T(8,128)S(1)}, f32[16,128]{1,0:T(8,128)S(1)}, u32[]{:S(2)}, u32[]{:S(2)}) collective-permute-start(f32[16,128]{1,0:T(8,128)S(1)} %get-tuple-element.17), channel_id=1, source_target_pairs={{0,12},{4,8},{8,4},{12,0},{16,28},{20,24},{24,20},{28,16},{1,13},{... | collective-permute-start | bytes 24584 | tf_op jit(solution)/shard_map/ppermute | solution.py:463
  5.7 4.1 %collective-permute-start.3 = (f32[16,128]{1,0:T(8,128)S(1)}, f32[16,128]{1,0:T(8,128)S(1)}, u32[]{:S(2)}, u32[]{:S(2)}) collective-permute-start(f32[16,128]{1,0:T(8,128)S(1)} %get-tuple-element.16), channel_id=1, source_target_pairs={{0,20},{4,16},{8,28},{12,24},{16,4},{20,0},{24,12},{28,8},{1,21},{... | collective-permute-start | bytes 24584 | tf_op jit(solution)/shard_map/ppermute | solution.py:463
  7.3 4.0 %collective-permute-start.4 = (f32[16,128]{1,0:T(8,128)S(1)}, f32[16,128]{1,0:T(8,128)S(1)}, u32[]{:S(2)}, u32[]{:S(2)}) collective-permute-start(f32[16,128]{1,0:T(8,128)S(1)} %get-tuple-element.17), channel_id=1, source_target_pairs={{0,28},{4,24},{8,20},{12,16},{16,12},{20,8},{24,4},{28,0},{1,29},{... | collective-permute-start | bytes 24584 | tf_op jit(solution)/shard_map/ppermute | solution.py:463
  11.6 5.4 %collective-permute-start.5 = (f32[136,256]{1,0:T(8,128)S(1)}, f32[136,256]{1,0:T(8,128)S(1)}, u32[]{:S(2)}, u32[]{:S(2)}) collective-permute-start(f32[136,256]{1,0:T(8,128)S(1)} %get-tuple-element.19.zm_ref), channel_id=1, source_target_pairs={{0,1},{1,0},{2,3},{3,2},{4,5},{5,4},{6,7},{7,6},{8,9},{9,8},{10,11... | collective-permute-start | bytes 417800 | tf_op jit(solution)/shard_map/ppermute | solution.py:479
  13.0 5.0 %collective-permute-start.6 = (f32[136,256]{1,0:T(8,128)S(1)}, f32[136,256]{1,0:T(8,128)S(1)}, u32[]{:S(2)}, u32[]{:S(2)}) collective-permute-start(f32[136,256]{1,0:T(8,128)S(1)} %get-tuple-element.19.zm_ref), channel_id=1, source_target_pairs={{0,4},{1,2},{2,1},{3,7},{4,0},{5,6},{6,5},{7,3},{8,12},{9,10},{10,... | collective-permute-start | bytes 417800 | tf_op jit(solution)/shard_map/ppermute | solution.py:484
  18.9 4.4 %collective-permute-start.7 = (f32[4,64,128]{2,1,0:T(8,128)S(1)}, f32[4,64,128]{2,1,0:T(8,128)S(1)}, u32[]{:S(2)}, u32[]{:S(2)}) collective-permute-start(f32[4,64,128]{2,1,0:T(8,128)S(1)} %shard_map.54._.own_ref), channel_id=1, source_target_pairs={{0,8},{4,12},{8,0},{12,4},{1,9},{5,13},{9,1},{13,5},{2,10},{6,14},... | collective-permute-start | bytes 393224 | tf_op jit(solution)/shard_map/ppermute | solution.py:457
  19.2 4.7 %collective-permute-start.8 = (f32[4,64,128]{2,1,0:T(8,128)S(1)}, f32[4,64,128]{2,1,0:T(8,128)S(1)}, u32[]{:S(2)}, u32[]{:S(2)}) collective-permute-start(f32[4,64,128]{2,1,0:T(8,128)S(1)} %shard_map.54._.own_ref), channel_id=1, source_target_pairs={{0,4},{4,0},{8,12},{12,8},{1,5},{5,1},{9,13},{13,9},{2,6},{6,2},{1... | collective-permute-start | bytes 393224 | tf_op jit(solution)/shard_map/ppermute | solution.py:457
  20.6 5.2 %collective-permute-start.9 = (f32[4,64,128]{2,1,0:T(8,128)S(1)}, f32[4,64,128]{2,1,0:T(8,128)S(1)}, u32[]{:S(2)}, u32[]{:S(2)}) collective-permute-start(f32[4,64,128]{2,1,0:T(8,128)S(1)} %shard_map.54._.own_ref), channel_id=1, source_target_pairs={{0,16},{4,8},{8,4},{12,28},{16,0},{20,24},{24,20},{28,12},{1,17},{... | collective-permute-start | bytes 393224 | tf_op jit(solution)/shard_map/ppermute | solution.py:493

commit v3 on v2

--- a/solution.py
+++ b/solution.py
@@ -16,8 +16,8 @@
 HBM = pl.BlockSpec(memory_space=pltpu.HBM)
 
 
-def call(kernel, outs, scratch=(), mib=8, in_specs=None):
-    shapes = [jax.ShapeDtypeStruct(s, jnp.float32) for s in outs]
+def call(kernel, outs, scratch=(), mib=8, in_specs=None, kind=jnp.float32):
+    shapes = [jax.ShapeDtypeStruct(s, kind) for s in outs]
 
     def run(*args):
         return pl.pallas_call(
@@ -172,7 +172,7 @@
     )
 
 
-def turn_kernel(s_ref, own_ref, far_ref, chip_ref, cross_ref, xchip_ref, xcross_ref, score_ref, zm_ref):
+def turn_kernel(s_ref, own_ref, far_ref, cross_ref, xcross_ref, chip_ref, xchip_ref, score_ref, zm_ref):
     size_x, size_y, _ = s_ref.shape
     chip, cross = y_masks("gy", True), y_masks("gy", False)
     first = lax.axis_index("gx") == 0
@@ -274,8 +274,19 @@
             ref[8 * b : 8 * b + 8, k * LANES : (k + 1) * LANES] = v
 
 
-def z_own_kernel(zm_ref, out_ref, table):
+def y_table(axis, hop, size_y, table):
+    index = lax.axis_index(axis)
+    away = (((index ^ hop) - index) * size_y).astype(jnp.float32)
+    s = row_of((8, LANES)).astype(jnp.float32) - away
+    for d in range(1 - size_y, size_y - 7):
+        v = s + float(d)
+        table[d - (1 - size_y)] = v * v
+
+
+def z_own_kernel(size_y, zm_ref, out_ref, table, *y_tables):
     count, half = LANES // 8, LANES // 16
+    for hop, y_one in enumerate(y_tables):
+        y_table("gy", hop, size_y, y_one)
     s = row_of((8, LANES)).astype(jnp.float32)
     for d in range(Z_FLOOR, LANES):
         v = s + float(d)
@@ -397,15 +408,6 @@
             score_ref[x] = score_in[x] + more[i * size_y : (i + 1) * size_y]
 
 
-def y_table(axis, hop, size_y, table):
-    index = lax.axis_index(axis)
-    away = (((index ^ hop) - index) * size_y).astype(jnp.float32)
-    s = row_of((8, LANES)).astype(jnp.float32) - away
-    for d in range(1 - size_y, size_y - 7):
-        v = s + float(d)
-        table[d - (1 - size_y)] = v * v
-
-
 Y_BLOCKS = 4
 
 
@@ -429,27 +431,42 @@
                 out_ref[x, 8 * b : 8 * b + 8, :] = v if scale == 1.0 else v * scale
 
 
-def y_own_kernel(own_ref, out_ref, table_1, table_2, table_3, table_0):
-    size_y = own_ref.shape[1]
-    for hop, table in enumerate((table_0, table_1, table_2, table_3)):
-        y_table("gy", hop, size_y, table)
-    y_sweep((own_ref,), (table_0,), None, out_ref, 1.0)
-
-
-def y_far_kernel(hop, scale, start_ref, ref, table, out_ref):
+CODES = 4681.0
+LN2 = 0.6931471805599453
+
+
+def encode_kernel(value_ref, code_ref):
+    code = jnp.round(jnp.log(value_ref[...] + 1.0) * (CODES / LN2)) - 32768.0
+    code_ref[...] = jnp.clip(code, -32768.0, 32767.0).astype(jnp.int32).astype(jnp.int16)
+
+
+def decode(code):
+    level = code.astype(jnp.int32).astype(jnp.float32) + 32768.0
+    return jnp.exp(level * (LN2 / CODES)) - 1.0
+
+
+def y_own_kernel(own_ref, table, out_ref):
+    y_sweep((own_ref,), (table,), None, out_ref, 1.0)
+
+
+def y_far_kernel(start_ref, code_ref, table, out_ref, block):
+    block[...] = decode(code_ref[...])
+    y_sweep((block,), (table,), start_ref, out_ref, 1.0)
+
+
+def y_last_kernel(start_ref, code_ref, table, score_in, out_ref, score_ref, block):
     index = lax.axis_index("gy")
-    if hop < 3:
-        y_sweep((ref,), (table,), start_ref, out_ref, scale)
-        return
-    near = jnp.abs((index ^ hop) - index) < 3
+    near = jnp.abs((index ^ 3) - index) < 3
+    score_ref[...] = score_in[...]
 
     @pl.when(near)
     def _():
-        y_sweep((ref,), (table,), start_ref, out_ref, scale)
+        block[...] = decode(code_ref[...])
+        y_sweep((block,), (table,), start_ref, out_ref, 1.0 / RADIUS)
 
     @pl.when(jnp.logical_not(near))
     def _():
-        out_ref[...] = start_ref[...] * scale
+        out_ref[...] = start_ref[...] * (1.0 / RADIUS)
 
 
 def swap(value, axis, hop):
@@ -519,7 +536,7 @@
 
     s, own, chip, cross = conv(features, conv_weight, mask, planes, size_x + 1, True)
     far = swap_xy(own, 1, 0)
-    sides = [swap_xy(v, x, y) for x in range(2) for v, y in ((chip, 1), (cross, 3))]
+    sides = [swap_xy(cross, 0, 3), swap_xy(cross, 1, 3), swap_xy(chip, 0, 1), swap_xy(chip, 1, 1)]
     return call(turn_kernel, [(size_x, size_y, LANES), (LANES + 8, size_x * size_y)])(s, own, far, *sides)
 
 
@@ -575,7 +592,9 @@
     score, zm = halo(features, conv_weight, mask)
 
     even, odd = z_swaps(zm)
-    best, table = call(z_own_kernel, [(LANES, lines), (LANES - Z_FLOOR, 8, LANES)])(zm)
+    tables = (2 * size_y - 8, 8, LANES)
+    own = functools.partial(z_own_kernel, size_y)
+    best, table, *kept = call(own, [(LANES, lines), (LANES - Z_FLOOR, 8, LANES)] + [tables] * 4)(zm)
     work = [pltpu.VMEM((LANES, lines), jnp.float32)] * 2
     for first, got, shape in ((True, even, (LANES, lines)), (False, odd, brick)):
         far = functools.partial(z_far_kernel, first, partner, size_x, size_y)
@@ -584,14 +603,14 @@
     if not partner:
         best = x_minima(best, size_x)
 
-    tables = (2 * size_y - 8, 8, LANES)
-    across, chip = swap(best, "gy", 2), swap(best, "gy", 1)
-    near, *kept = call(y_own_kernel, [brick, tables, tables, tables], [pltpu.VMEM(tables, jnp.float32)])(best)
-    blocks = {2: across, 1: chip, 3: corner_swap(best)}
-    for hop, block in blocks.items():
-        far = functools.partial(y_far_kernel, hop, 1.0 / RADIUS if hop == 3 else 1.0)
-        (near,) = call(far, [brick])(near, block, kept[hop - 1])
-    return score, near
+    (code,) = call(encode_kernel, [brick], kind=jnp.int16)(best)
+    blocks = {2: swap(code, "gy", 2), 1: swap(code, "gy", 1), 3: corner_swap(code)}
+    (near,) = call(y_own_kernel, [brick])(best, kept[0])
+    block = [pltpu.VMEM(brick, jnp.float32)]
+    for hop in (2, 1):
+        (near,) = call(y_far_kernel, [brick], block)(near, blocks[hop], kept[hop])
+    depth, score = call(y_last_kernel, [brick, brick], block)(near, blocks[3], kept[3], score)
+    return score, depth
 
 
 def solution(mesh):

time: 27.3 us -> 25.8 us (0.945)
  waiting for transfers between devices: 7.86 us -> 7.07 us
  Pallas kernels: 10.2 us -> 9.73 us
    ppermute x5, waiting for transfers between devices: 3.89 us -> 3.13 us  [swap_xy(): return lax.ppermute(value, ('gx', 'gy'), pairs)]
    pallas_call x10 -> x11, Pallas kernels: 10.2 us -> 9.73 us  [run(): pl.pallas_call(kernel, out_shape=shapes, in_specs=in_specs or [VMEM] * le...]
    ppermute x1, starting transfers between devices: 1.13 us -> 0.7 us  [corner_swap(): return lax.ppermute(value, ('gx', 'gy'), pairs)]
  transfers between devices with their start and end apart: 10 -> 10, of which waited for: 6 -> 4; matrix products, arithmetic and copies ran while one was open for 0% -> 0% of each run, Pallas kernels for 19% -> 17%
where the time goes in v3:
time: 25.8 us; the launch traced here: 25.6 us
  Pallas kernels  9.73 us (38%)
  starting transfers between devices  8.02 us (31%)
  waiting for transfers between devices  7.07 us (27%)
  between operations  0.73 us (3%)
    pallas_call x11, Pallas kernels, run(): pl.pallas_call(kernel, out_shape=shapes, in_specs=in_specs or [VMEM] * le...  9.73 us
    ppermute x5, starting transfers between devices, swap_xy(): return lax.ppermute(value, ('gx', 'gy'), pairs)  4.09 us
    ppermute x5, waiting for transfers between devices, swap_xy(): return lax.ppermute(value, ('gx', 'gy'), pairs)  3.13 us
    ppermute x1, waiting for transfers between devices, z_swaps(): even = lax.ppermute(value, 'gz', [(i, i ^ 1) for i in range(n)])  2.54 us
    ppermute x2, starting transfers between devices, swap(): return lax.ppermute(value, axis, [(i, i ^ hop) for i in range(n)])  1.86 us
    ppermute x1, starting transfers between devices, z_swaps(): even = lax.ppermute(value, 'gz', [(i, i ^ 1) for i in range(n)])  1.36 us
    ppermute x1, waiting for transfers between devices, corner_swap(): return lax.ppermute(value, ('gx', 'gy'), pairs)  1.02 us
    ppermute x1, starting transfers between devices, corner_swap(): return lax.ppermute(value, ('gx', 'gy'), pairs)  0.7 us
  transfers between devices with their start and end apart: 10, of which 4 were waited for; matrix products, arithmetic and copies ran while one was open for 0% of the time, Pallas kernels for 17%

profile of v3, /device:TPU:19, one launch (start us, length us, event | category | flops | bytes accessed | tf_op | source)
XLA Modules:
  0.0 25.6 jit_solution(18302266904888309469)
XLA Ops:
  0.6 2.6 %shard_map.50 = (f32[4,64,128]{2,1,0:T(8,128)S(1)}, f32[328,128]{1,0:T(8,128)S(1)}, f32[16,128]{1,0:T(8,128)S(1)}, f32[16,128]{1,0:T(8,128)S(1)}) custom-call(bf16[32,4,64,128]{3,2,1,0:T(8,128)(2,1)} %f_hbm.1, bf16[27,32]{1,0:T(8,128)(2,1)} %w_hbm.1, s32[4,64,128]{2,1,0:T(8,128)} %mask_hbm.1), custom_call_target="tpu_custom_call" | custom-call | tf_op jit(solution)/shard_map/pallas_call | solution.py:23
  3.3 0.3 %collective-permute-start = (f32[328,128]{1,0:T(8,128)S(1)}, f32[328,128]{1,0:T(8,128)S(1)}, u32[]{:S(2)}, u32[]{:S(2)}) collective-permute-start(f32[328,128]{1,0:T(8,128)S(1)} %get-tuple-element.17.own_ref), channel_id=1, source_target_pairs={{0,16},{4,20},{8,24},{12,28},{16,0},{20,4},{24,8},{28,12},{1,17},{... | collective-permute-start | bytes 503816 | tf_op jit(solution)/shard_map/ppermute | solution.py:480
  3.6 3.0 %collective-permute-start.2 = (f32[16,128]{1,0:T(8,128)S(1)}, f32[16,128]{1,0:T(8,128)S(1)}, u32[]{:S(2)}, u32[]{:S(2)}) collective-permute-start(f32[16,128]{1,0:T(8,128)S(1)} %get-tuple-element.18), channel_id=1, source_target_pairs={{0,28},{4,24},{8,20},{12,16},{16,12},{20,8},{24,4},{28,0},{1,29},{... | collective-permute-start | bytes 24584 | tf_op jit(solution)/shard_map/ppermute | solution.py:480
  6.6 0.0 collective-permute-start.1
  6.6 0.8 %collective-permute-start.4 = (f32[16,128]{1,0:T(8,128)S(1)}, f32[16,128]{1,0:T(8,128)S(1)}, u32[]{:S(2)}, u32[]{:S(2)}) collective-permute-start(f32[16,128]{1,0:T(8,128)S(1)} %get-tuple-element.19), channel_id=1, source_target_pairs={{0,20},{4,16},{8,28},{12,24},{16,4},{20,0},{24,12},{28,8},{1,21},{... | collective-permute-start | bytes 24584 | tf_op jit(solution)/shard_map/ppermute | solution.py:480
  7.4 0.0 collective-permute-start.3
  7.4 3.1 %collective-permute-done.2.xcross_ref = f32[16,128]{1,0:T(8,128)S(1)} collective-permute-done((f32[16,128]{1,0:T(8,128)S(1)}, f32[16,128]{1,0:T(8,128)S(1)}, u32[]{:S(2)}, u32[]{:S(2)}) %collective-permute-start.2) | collective-permute-done | bytes 8224 | tf_op jit(solution)/shard_map/ppermute | solution.py:480
  10.5 0.0 collective-permute-done.1.cross_ref
  10.5 0.0 collective-permute-done.4.xchip_ref
  10.5 0.0 collective-permute-done.3.chip_ref
  10.5 0.0 collective-permute-done.far_ref
  10.5 0.3 %shard_map.51 = (f32[4,64,128]{2,1,0:T(8,128)S(1)}, f32[136,256]{1,0:T(8,128)S(1)}) custom-call(f32[4,64,128]{2,1,0:T(8,128)S(1)} %get-tuple-element.16.s_ref, f32[328,128]{1,0:T(8,128)S(1)} %get-tuple-element.17.own_ref, f32[328,128]{1,0:T(8,128)S(1)} %collective-permute-done.far_ref, f32[16,128]{1,0:T(8,128)S(1)} %collective-permute-done.1.cross_ref, ...), custom_call_target="tpu_custom_call" | custom-call | tf_op jit(solution)/shard_map/pallas_call | solution.py:23
  10.9 1.4 %collective-permute-start.5 = (f32[136,256]{1,0:T(8,128)S(1)}, f32[136,256]{1,0:T(8,128)S(1)}, u32[]{:S(2)}, u32[]{:S(2)}) collective-permute-start(f32[136,256]{1,0:T(8,128)S(1)} %get-tuple-element.20.zm_ref), channel_id=1, source_target_pairs={{0,1},{1,0},{2,3},{3,2},{4,5},{5,4},{6,7},{7,6},{8,9},{9,8},{10,11... | collective-permute-start | bytes 417800 | tf_op jit(solution)/shard_map/ppermute | solution.py:496
  12.2 0.0 collective-permute-start.6
  12.2 1.6 %shard_map.52 = (f32[128,256]{1,0:T(8,128)S(1)}, f32[262,8,128]{2,1,0:T(8,128)S(1)}, f32[120,8,128]{2,1,0:T(8,128)S(1)}, f32[120,8,128]{2,1,0:T(8,128)S(1)}, f32...) custom-call(f32[136,256]{1,0:T(8,128)S(1)} %get-tuple-element.20.zm_ref), custom_call_target="tpu_custom_call" | custom-call | tf_op jit(solution)/shard_map/pallas_call | solution.py:23
  13.8 2.5 %collective-permute-done.5.got_ref.even_ref = f32[136,256]{1,0:T(8,128)S(1)} collective-permute-done((f32[136,256]{1,0:T(8,128)S(1)}, f32[136,256]{1,0:T(8,128)S(1)}, u32[]{:S(2)}, u32[]{:S(2)}) %collective-permute-start.5) | collective-permute-done | bytes 139296 | tf_op jit(solution)/shard_map/ppermute | solution.py:496
  16.3 0.7 %shard_map.53.acc_ref = f32[128,256]{1,0:T(8,128)S(1)} custom-call(f32[128,256]{1,0:T(8,128)S(1)} %get-tuple-element.21.acc_ref, f32[262,8,128]{2,1,0:T(8,128)S(1)} %get-tuple-element.22.table, f32[136,256]{1,0:T(8,128)S(1)} %get-tuple-element.20.zm_ref, f32[136,256]{1,0:T(8,128)S(1)} %collective-permute-done.5.got_ref.even_ref), custom_call_target="tpu_custom_call" | custom-call | tf_op jit(solution)/shard_map/pallas_call | solution.py:23
  17.1 0.4 %collective-permute-done.6.got_ref.odd_ref = f32[136,256]{1,0:T(8,128)S(1)} collective-permute-done((f32[136,256]{1,0:T(8,128)S(1)}, f32[136,256]{1,0:T(8,128)S(1)}, u32[]{:S(2)}, u32[]{:S(2)}) %collective-permute-start.6) | collective-permute-done | bytes 139296 | tf_op jit(solution)/shard_map/ppermute | solution.py:501
  17.5 0.9 %shard_map.54.own_ref.value_ref._ = f32[4,64,128]{2,1,0:T(8,128)S(1)} custom-call(f32[128,256]{1,0:T(8,128)S(1)} %shard_map.53.acc_ref, f32[262,8,128]{2,1,0:T(8,128)S(1)} %get-tuple-element.22.table, f32[136,256]{1,0:T(8,128)S(1)} %get-tuple-element.20.zm_ref, f32[136,256]{1,0:T(8,128)S(1)} %collective-permute-done.6.got_ref.odd_ref), custom_call_target="tpu_custom_call" | custom-call | tf_op jit(solution)/shard_map/pallas_call | solution.py:23
  18.3 0.1 shard_map.56
  18.4 0.1 collective-permute-start.7
  18.5 1.8 %collective-permute-start.8 = (s16[4,64,128]{2,1,0:T(8,128)(2,1)S(1)}, s16[4,64,128]{2,1,0:T(8,128)(2,1)S(1)}, u32[]{:S(2)}, u32[]{:S(2)}) collective-permute-start(s16[4,64,128]{2,1,0:T(8,128)(2,1)S(1)} %shard_map.56), channel_id=1, source_target_pairs={{0,4},{4,0},{8,12},{12,8},{1,5},{5,1},{9,13},{13,9},{2,6},{6,2},{1... | collective-permute-start | bytes 196616 | tf_op jit(solution)/shard_map/ppermute | solution.py:474
  20.3 0.7 %collective-permute-start.9 = (s16[4,64,128]{2,1,0:T(8,128)(2,1)S(1)}, s16[4,64,128]{2,1,0:T(8,128)(2,1)S(1)}, u32[]{:S(2)}, u32[]{:S(2)}) collective-permute-start(s16[4,64,128]{2,1,0:T(8,128)(2,1)S(1)} %shard_map.56), channel_id=1, source_target_pairs={{0,16},{4,8},{8,4},{12,28},{16,0},{20,24},{24,20},{28,12},{1,17},{... | collective-permute-start | bytes 196616 | tf_op jit(solution)/shard_map/ppermute | solution.py:510
  21.0 0.6 %shard_map.55.start_ref = f32[4,64,128]{2,1,0:T(8,128)S(1)} custom-call(f32[4,64,128]{2,1,0:T(8,128)S(1)} %shard_map.54.own_ref.value_ref._, f32[120,8,128]{2,1,0:T(8,128)S(1)} %get-tuple-element.23.table), custom_call_target="tpu_custom_call" | custom-call | tf_op jit(solution)/shard_map/pallas_call | solution.py:23
  21.6 0.1 shard_map.59.score_in
  21.7 0.0 collective-permute-done.7.code_ref
  21.8 0.7 %shard_map.57.start_ref = f32[4,64,128]{2,1,0:T(8,128)S(1)} custom-call(f32[4,64,128]{2,1,0:T(8,128)S(1)} %shard_map.55.start_ref, s16[4,64,128]{2,1,0:T(8,128)(2,1)S(1)} %collective-permute-done.7.code_ref, f32[120,8,128]{2,1,0:T(8,128)S(1)} %get-tuple-element.24.table), custom_call_target="tpu_custom_call" | custom-call | tf_op jit(solution)/shard_map/pallas_call | solution.py:23
  22.4 0.0 collective-permute-done.8.code_ref
  22.4 0.7 %shard_map.58.start_ref = f32[4,64,128]{2,1,0:T(8,128)S(1)} custom-call(f32[4,64,128]{2,1,0:T(8,128)S(1)} %shard_map.57.start_ref, s16[4,64,128]{2,1,0:T(8,128)(2,1)S(1)} %collective-permute-done.8.code_ref, f32[120,8,128]{2,1,0:T(8,128)S(1)} %get-tuple-element.25.table), custom_call_target="tpu_custom_call" | custom-call | tf_op jit(solution)/shard_map/pallas_call | solution.py:23
  23.1 1.0 %collective-permute-done.9.code_ref = s16[4,64,128]{2,1,0:T(8,128)(2,1)S(1)} collective-permute-done((s16[4,64,128]{2,1,0:T(8,128)(2,1)S(1)}, s16[4,64,128]{2,1,0:T(8,128)(2,1)S(1)}, u32[]{:S(2)}, u32[]{:S(2)}) %collective-permute-start.9) | collective-permute-done | bytes 65568 | tf_op jit(solution)/shard_map/ppermute | solution.py:510
  24.2 1.4 %shard_map.60 = (f32[4,64,128]{2,1,0:T(8,128)}, f32[4,64,128]{2,1,0:T(8,128)}) custom-call(f32[4,64,128]{2,1,0:T(8,128)S(1)} %shard_map.58.start_ref, s16[4,64,128]{2,1,0:T(8,128)(2,1)S(1)} %collective-permute-done.9.code_ref, f32[120,8,128]{2,1,0:T(8,128)S(1)} %get-tuple-element.26.table, f32[4,64,128]{2,1,0:T(8,128)S(1)} %shard_map.59.score_in), custom_call_target="tpu_custom_call" | custom-call | tf_op jit(solution)/shard_map/pallas_call | solution.py:23
Async XLA Ops:
  3.3 7.2 %collective-permute-start = (f32[328,128]{1,0:T(8,128)S(1)}, f32[328,128]{1,0:T(8,128)S(1)}, u32[]{:S(2)}, u32[]{:S(2)}) collective-permute-start(f32[328,128]{1,0:T(8,128)S(1)} %get-tuple-element.17.own_ref), channel_id=1, source_target_pairs={{0,16},{4,20},{8,24},{12,28},{16,0},{20,4},{24,8},{28,12},{1,17},{... | collective-permute-start | bytes 503816 | tf_op jit(solution)/shard_map/ppermute | solution.py:480
  3.6 6.9 %collective-permute-start.2 = (f32[16,128]{1,0:T(8,128)S(1)}, f32[16,128]{1,0:T(8,128)S(1)}, u32[]{:S(2)}, u32[]{:S(2)}) collective-permute-start(f32[16,128]{1,0:T(8,128)S(1)} %get-tuple-element.18), channel_id=1, source_target_pairs={{0,28},{4,24},{8,20},{12,16},{16,12},{20,8},{24,4},{28,0},{1,29},{... | collective-permute-start | bytes 24584 | tf_op jit(solution)/shard_map/ppermute | solution.py:480
  6.6 3.9 %collective-permute-start.1 = (f32[16,128]{1,0:T(8,128)S(1)}, f32[16,128]{1,0:T(8,128)S(1)}, u32[]{:S(2)}, u32[]{:S(2)}) collective-permute-start(f32[16,128]{1,0:T(8,128)S(1)} %get-tuple-element.18), channel_id=1, source_target_pairs={{0,12},{4,8},{8,4},{12,0},{16,28},{20,24},{24,20},{28,16},{1,13},{... | collective-permute-start | bytes 24584 | tf_op jit(solution)/shard_map/ppermute | solution.py:480
  6.6 3.9 %collective-permute-start.4 = (f32[16,128]{1,0:T(8,128)S(1)}, f32[16,128]{1,0:T(8,128)S(1)}, u32[]{:S(2)}, u32[]{:S(2)}) collective-permute-start(f32[16,128]{1,0:T(8,128)S(1)} %get-tuple-element.19), channel_id=1, source_target_pairs={{0,20},{4,16},{8,28},{12,24},{16,4},{20,0},{24,12},{28,8},{1,21},{... | collective-permute-start | bytes 24584 | tf_op jit(solution)/shard_map/ppermute | solution.py:480
  7.4 3.1 %collective-permute-start.3 = (f32[16,128]{1,0:T(8,128)S(1)}, f32[16,128]{1,0:T(8,128)S(1)}, u32[]{:S(2)}, u32[]{:S(2)}) collective-permute-start(f32[16,128]{1,0:T(8,128)S(1)} %get-tuple-element.19), channel_id=1, source_target_pairs={{0,4},{4,0},{8,12},{12,8},{16,20},{20,16},{24,28},{28,24},{1,5},{5... | collective-permute-start | bytes 24584 | tf_op jit(solution)/shard_map/ppermute | solution.py:480
  10.9 5.5 %collective-permute-start.5 = (f32[136,256]{1,0:T(8,128)S(1)}, f32[136,256]{1,0:T(8,128)S(1)}, u32[]{:S(2)}, u32[]{:S(2)}) collective-permute-start(f32[136,256]{1,0:T(8,128)S(1)} %get-tuple-element.20.zm_ref), channel_id=1, source_target_pairs={{0,1},{1,0},{2,3},{3,2},{4,5},{5,4},{6,7},{7,6},{8,9},{9,8},{10,11... | collective-permute-start | bytes 417800 | tf_op jit(solution)/shard_map/ppermute | solution.py:496
  12.2 5.2 %collective-permute-start.6 = (f32[136,256]{1,0:T(8,128)S(1)}, f32[136,256]{1,0:T(8,128)S(1)}, u32[]{:S(2)}, u32[]{:S(2)}) collective-permute-start(f32[136,256]{1,0:T(8,128)S(1)} %get-tuple-element.20.zm_ref), channel_id=1, source_target_pairs={{0,4},{1,2},{2,1},{3,7},{4,0},{5,6},{6,5},{7,3},{8,12},{9,10},{10,... | collective-permute-start | bytes 417800 | tf_op jit(solution)/shard_map/ppermute | solution.py:501
  18.4 3.3 %collective-permute-start.7 = (s16[4,64,128]{2,1,0:T(8,128)(2,1)S(1)}, s16[4,64,128]{2,1,0:T(8,128)(2,1)S(1)}, u32[]{:S(2)}, u32[]{:S(2)}) collective-permute-start(s16[4,64,128]{2,1,0:T(8,128)(2,1)S(1)} %shard_map.56), channel_id=1, source_target_pairs={{0,8},{4,12},{8,0},{12,4},{1,9},{5,13},{9,1},{13,5},{2,10},{6,14},... | collective-permute-start | bytes 196616 | tf_op jit(solution)/shard_map/ppermute | solution.py:474
  18.5 4.0 %collective-permute-start.8 = (s16[4,64,128]{2,1,0:T(8,128)(2,1)S(1)}, s16[4,64,128]{2,1,0:T(8,128)(2,1)S(1)}, u32[]{:S(2)}, u32[]{:S(2)}) collective-permute-start(s16[4,64,128]{2,1,0:T(8,128)(2,1)S(1)} %shard_map.56), channel_id=1, source_target_pairs={{0,4},{4,0},{8,12},{12,8},{1,5},{5,1},{9,13},{13,9},{2,6},{6,2},{1... | collective-permute-start | bytes 196616 | tf_op jit(solution)/shard_map/ppermute | solution.py:474
  20.3 3.9 %collective-permute-start.9 = (s16[4,64,128]{2,1,0:T(8,128)(2,1)S(1)}, s16[4,64,128]{2,1,0:T(8,128)(2,1)S(1)}, u32[]{:S(2)}, u32[]{:S(2)}) collective-permute-start(s16[4,64,128]{2,1,0:T(8,128)(2,1)S(1)} %shard_map.56), channel_id=1, source_target_pairs={{0,16},{4,8},{8,4},{12,28},{16,0},{20,24},{24,20},{28,12},{1,17},{... | collective-permute-start | bytes 196616 | tf_op jit(solution)/shard_map/ppermute | solution.py:510

commit v4 on v3

--- a/solution.py
+++ b/solution.py
@@ -16,15 +16,15 @@
 HBM = pl.BlockSpec(memory_space=pltpu.HBM)
 
 
-def call(kernel, outs, scratch=(), mib=8, in_specs=None, kind=jnp.float32):
-    shapes = [jax.ShapeDtypeStruct(s, kind) for s in outs]
+def call(kernel, outs, scratch=(), mib=8, in_specs=None, kind=jnp.float32, out_spec=VMEM):
+    shapes = [s if isinstance(s, jax.ShapeDtypeStruct) else jax.ShapeDtypeStruct(s, kind) for s in outs]
 
     def run(*args):
         return pl.pallas_call(
             kernel,
             out_shape=shapes,
             in_specs=in_specs or [VMEM] * len(args),
-            out_specs=[VMEM] * len(shapes),
+            out_specs=[out_spec] * len(shapes),
             scratch_shapes=list(scratch),
             compiler_params=pltpu.CompilerParams(vmem_limit_bytes=mib * 1024 * 1024),
         )(*args)
@@ -60,7 +60,6 @@
     for copy in copies:
         copy.start()
 
-    acc[...] = jnp.zeros_like(acc)
     spread = (
         lax.broadcasted_iota(jnp.int32, (channels, depth), 1) // 16
         == lax.broadcasted_iota(jnp.int32, (channels, depth), 0)
@@ -131,8 +130,16 @@
                 fold = outer if g == 0 else fold + outer
         folds.append(fold)
 
+    at_plane = planes()
+    half = size_x // 2
     for x in range(size_x):
-        copies[x].wait()
+        if x % half == 0:
+            for copy in copies[x : x + half]:
+                copy.wait()
+            if x:
+                masks.wait()
+                for p in range(x - 1):
+                    finish(p, at_plane[p])
         right = jnp.concatenate(
             [f_vmem[:, x, 16 * t : 16 * t + 16, :].reshape(depth, LANES) for t in range(tiles)],
             axis=1,
@@ -142,11 +149,49 @@
             at = x + 2 - a
             for c in range(3):
                 first = (3 * a + c) * ROWS
-                acc[at, c] = acc[at, c] + got[first : first + ROWS, :]
-    masks.wait()
-    for p, at in enumerate(planes()):
-        finish(p, at)
+                part = got[first : first + ROWS, :]
+                acc[at, c] = part if a == 0 or x == 0 else acc[at, c] + part
+    for p in range(half - 1, len(at_plane)):
+        finish(p, at_plane[p])
     m_ref[len(folds) * size_y :, :] = functools.reduce(jnp.add, folds)
+
+
+CODES = 4681.0
+LN2 = 0.6931471805599453
+TOP = 2.0**30
+
+
+def encode(value):
+    code = jnp.round(jnp.log(value + 1.0) * (CODES / LN2)) - 32768.0
+    return jnp.clip(code, -32768.0, 32767.0).astype(jnp.int32)
+
+
+def decode(code):
+    level = code.astype(jnp.int32).astype(jnp.float32) + 32768.0
+    return jnp.exp(level * (LN2 / CODES)) - 1.0
+
+
+def pack_z(rows, ends):
+    half = LANES // 2
+    code = encode(rows)
+    masked = ends >= 0.5 * HUGE
+    most = jnp.max(jnp.where(masked, 0.0, jnp.abs(ends)), axis=1, keepdims=True)
+    most = jnp.max(most, axis=0, keepdims=True)
+    power = jnp.ceil(jnp.log(jnp.maximum(most, 1e-18)) * (1.0 / LN2)) + 1.0
+    scores = jnp.round(jnp.where(masked, TOP, ends * (jnp.exp(power * -LN2) * TOP))).astype(jnp.int32)
+    first = jnp.where(row_of((half, rows.shape[1])) == 0, power.astype(jnp.int32), code[:half])
+    return jnp.concatenate([(first << 16) | (code[half:] & 0xFFFF), scores], axis=0)
+
+
+def unpack_rows(words):
+    return decode(words >> 16), decode((words << 16) >> 16)
+
+
+def unpack_ends(ref):
+    half = LANES // 2
+    power = (ref[0:8, :] >> 16)[0:1].astype(jnp.float32)
+    scores = ref[half : half + 8, :].astype(jnp.float32)
+    return jnp.where(scores >= 0.75 * TOP, HUGE, scores * (jnp.exp(power * LN2) * (1.0 / TOP)))
 
 
 def y_masks(axis, chip):
@@ -172,7 +217,7 @@
     )
 
 
-def turn_kernel(s_ref, own_ref, far_ref, cross_ref, xcross_ref, chip_ref, xchip_ref, score_ref, zm_ref):
+def turn_kernel(s_ref, own_ref, far_ref, cross_ref, xcross_ref, chip_ref, xchip_ref, score_ref, zm_ref, words_ref):
     size_x, size_y, _ = s_ref.shape
     chip, cross = y_masks("gy", True), y_masks("gy", False)
     first = lax.axis_index("gx") == 0
@@ -227,13 +272,16 @@
             d = float(j - i) + away
             best = jnp.minimum(best, costs[size_x + j] + d * d)
         lines.append(best)
-    zm_ref[0:LANES, :] = jnp.concatenate(lines, axis=0).T
     width = size_x * size_y
+    rows = jnp.concatenate(lines, axis=0).T
     ends = jnp.concatenate(turned, axis=0).T
-    zm_ref[LANES : LANES + 8, :] = jnp.concatenate(
+    ends = jnp.concatenate(
         [ends[r : r + 1, k * width : (k + 1) * width] for r in (0, LANES - 1, 1, 2) for k in range(2)],
         axis=0,
     )
+    zm_ref[0:LANES, :] = rows
+    zm_ref[LANES : LANES + 8, :] = ends
+    words_ref[...] = pack_z(rows, ends)
 
 
 Z_FLOOR = -(LANES + 6)
@@ -333,11 +381,11 @@
     count, half = LANES // 8, LANES // 16
     out = out_ref if even else work
 
-    own, got = zm_ref[LANES : LANES + 8, :], got_ref[LANES : LANES + 8, :]
+    own, got = zm_ref[LANES : LANES + 8, :], unpack_ends(got_ref)
     mine = jnp.where(low, own[0:2], own[2:4]) + jnp.where(valid, jnp.where(low, got[6:8], got[4:6]), 0.0)
     theirs = jnp.where(low, got[2:4] + own[4:6], got[0:2] + own[6:8])
     ends = border_minima(cost_of(jnp.concatenate([mine, theirs, mine, theirs], axis=0)), size_x, size_y, partner)
-    source[...] = got_ref[0:LANES, :]
+    source[0 : LANES // 2, :], source[LANES // 2 :, :] = unpack_rows(got_ref[0 : LANES // 2, :])
 
     squares = table.at[pl.ds(jnp.where(low, -Z_FLOOR, 1 - LANES - Z_FLOOR), LANES)]
     lanes = [slice(k * LANES, (k + 1) * LANES) for k in range(zm_ref.shape[1] // LANES)]
@@ -396,9 +444,10 @@
     odd = index % 2 == 1
     size_y = score_in.shape[1]
     per = LANES // size_y
+    even_ends, odd_ends = unpack_ends(even_ref), unpack_ends(odd_ref)
     for k in range(even_ref.shape[1] // LANES):
         cols = slice(k * LANES, (k + 1) * LANES)
-        even_rows, odd_rows = even_ref[LANES : LANES + 8, cols], odd_ref[LANES : LANES + 8, cols]
+        even_rows, odd_rows = even_ends[:, cols], odd_ends[:, cols]
         low = jnp.where(index > 0, jnp.where(odd, even_rows, odd_rows)[6:7], 0.0)
         high = jnp.where(index < last, jnp.where(odd, odd_rows, even_rows)[4:5], 0.0)
         middle = jnp.zeros((LANES - 2, LANES), jnp.float32)
@@ -411,9 +460,10 @@
 Y_BLOCKS = 4
 
 
-def y_sweep(refs, tables, start, out_ref, scale):
+def y_sweep(refs, tables, start, out_ref, scale, span=None):
     size_x, size_y, _ = out_ref.shape
-    for first in range(0, size_y // 8, Y_BLOCKS):
+    span = span or range(size_y // 8)
+    for first in range(span[0], span[-1] + 1, Y_BLOCKS):
         blocks = range(first, first + Y_BLOCKS)
         accs = []
         for b in blocks:
@@ -431,42 +481,58 @@
                 out_ref[x, 8 * b : 8 * b + 8, :] = v if scale == 1.0 else v * scale
 
 
-CODES = 4681.0
-LN2 = 0.6931471805599453
-
-
 def encode_kernel(value_ref, code_ref):
-    code = jnp.round(jnp.log(value_ref[...] + 1.0) * (CODES / LN2)) - 32768.0
-    code_ref[...] = jnp.clip(code, -32768.0, 32767.0).astype(jnp.int32).astype(jnp.int16)
-
-
-def decode(code):
-    level = code.astype(jnp.int32).astype(jnp.float32) + 32768.0
-    return jnp.exp(level * (LN2 / CODES)) - 1.0
+    code_ref[...] = encode(value_ref[...]).astype(jnp.int16)
 
 
 def y_own_kernel(own_ref, table, out_ref):
     y_sweep((own_ref,), (table,), None, out_ref, 1.0)
 
 
-def y_far_kernel(start_ref, code_ref, table, out_ref, block):
-    block[...] = decode(code_ref[...])
-    y_sweep((block,), (table,), start_ref, out_ref, 1.0)
-
-
-def y_last_kernel(start_ref, code_ref, table, score_in, out_ref, score_ref, block):
+def in_reach(hop):
     index = lax.axis_index("gy")
-    near = jnp.abs((index ^ 3) - index) < 3
-    score_ref[...] = score_in[...]
+    return jnp.abs((index ^ hop) - index) < 3
+
+
+def y_far_kernel(hop, start_ref, code_ref, table, out_ref, block):
+    near = in_reach(hop)
 
     @pl.when(near)
     def _():
         block[...] = decode(code_ref[...])
-        y_sweep((block,), (table,), start_ref, out_ref, 1.0 / RADIUS)
+        y_sweep((block,), (table,), start_ref, out_ref, 1.0)
 
     @pl.when(jnp.logical_not(near))
     def _():
-        out_ref[...] = start_ref[...] * (1.0 / RADIUS)
+        out_ref[...] = start_ref[...]
+
+
+def y_last_kernel(hop, start_ref, code_ref, table, score_ref, depth_hbm, score_hbm, block, depth, sems):
+    near = in_reach(hop)
+    size_y = depth.shape[1]
+    scores = pltpu.make_async_copy(score_ref, score_hbm, sems.at[0])
+    scores.start()
+    parts = [
+        pltpu.make_async_copy(depth.at[:, rows], depth_hbm.at[:, rows], sems.at[1 + i])
+        for i, rows in enumerate(pl.ds(f, size_y // 2) for f in (0, size_y // 2))
+    ]
+
+    @pl.when(near)
+    def _():
+        block[...] = decode(code_ref[...])
+        half = size_y // 16
+        for i, part in enumerate(parts):
+            y_sweep((block,), (table,), start_ref, depth, 1.0 / RADIUS, range(i * half, (i + 1) * half))
+            part.start()
+
+    @pl.when(jnp.logical_not(near))
+    def _():
+        depth[...] = start_ref[...] * (1.0 / RADIUS)
+        for part in parts:
+            part.start()
+
+    for copy in (scores, *parts):
+        copy.wait()
 
 
 def swap(value, axis, hop):
@@ -537,7 +603,9 @@
     s, own, chip, cross = conv(features, conv_weight, mask, planes, size_x + 1, True)
     far = swap_xy(own, 1, 0)
     sides = [swap_xy(cross, 0, 3), swap_xy(cross, 1, 3), swap_xy(chip, 0, 1), swap_xy(chip, 1, 1)]
-    return call(turn_kernel, [(size_x, size_y, LANES), (LANES + 8, size_x * size_y)])(s, own, far, *sides)
+    lines = size_x * size_y
+    words = jax.ShapeDtypeStruct((LANES // 2 + 8, lines), jnp.int32)
+    return call(turn_kernel, [(size_x, size_y, LANES), (LANES + 8, lines), words])(s, own, far, *sides)
 
 
 def halo_in_rounds(features, conv_weight, mask):
@@ -569,7 +637,8 @@
     ends = [line(v) for v in (masked[:, :, 0], masked[:, :, LANES - 1], down, up)]
     blank = [jnp.full_like(ends[0], HUGE)] * 2 + [jnp.zeros_like(ends[0])] * 2
     pairs = [v for pair in zip(ends, blank) for v in pair]
-    return score, jnp.concatenate([rows, *pairs], axis=0)
+    ends = jnp.concatenate(pairs, axis=0)
+    return score, jnp.concatenate([rows, ends], axis=0), pack_z(rows, ends)
 
 
 def x_minima(value, size_x):
@@ -589,9 +658,9 @@
     partner = gx == 2
 
     halo = halo_with_partner if partner else halo_in_rounds
-    score, zm = halo(features, conv_weight, mask)
-
-    even, odd = z_swaps(zm)
+    score, zm, words = halo(features, conv_weight, mask)
+
+    even, odd = z_swaps(words)
     tables = (2 * size_y - 8, 8, LANES)
     own = functools.partial(z_own_kernel, size_y)
     best, table, *kept = call(own, [(LANES, lines), (LANES - Z_FLOOR, 8, LANES)] + [tables] * 4)(zm)
@@ -604,12 +673,17 @@
         best = x_minima(best, size_x)
 
     (code,) = call(encode_kernel, [brick], kind=jnp.int16)(best)
-    blocks = {2: swap(code, "gy", 2), 1: swap(code, "gy", 1), 3: corner_swap(code)}
+    blocks = {1: swap(code, "gy", 1), 2: swap(code, "gy", 2), 3: corner_swap(code)}
     (near,) = call(y_own_kernel, [brick])(best, kept[0])
     block = [pltpu.VMEM(brick, jnp.float32)]
-    for hop in (2, 1):
-        (near,) = call(y_far_kernel, [brick], block)(near, blocks[hop], kept[hop])
-    depth, score = call(y_last_kernel, [brick, brick], block)(near, blocks[3], kept[3], score)
+    *hops, final = blocks
+    for hop in hops:
+        far = functools.partial(y_far_kernel, hop)
+        (near,) = call(far, [brick], block)(near, blocks[hop], kept[hop])
+    last = [*block, *block, pltpu.SemaphoreType.DMA((3,))]
+    depth, score = call(
+        functools.partial(y_last_kernel, final), [brick, brick], last, out_spec=HBM
+    )(near, blocks[final], kept[final], score)
     return score, depth
 
 

time: 25.8 us -> 24.4 us (0.946)
  waiting for transfers between devices: 7.07 us -> 5.82 us
    ppermute x1, waiting for transfers between devices: 2.54 us -> 1.13 us  [z_swaps(): even = lax.ppermute(value, 'gz', [(i, i ^ 1) for i in range(n)])]
    ppermute x2, waiting for transfers between devices: 0.01 us -> 0.48 us  [swap(): return lax.ppermute(value, axis, [(i, i ^ hop) for i in range(n)])]
    ppermute x1, waiting for transfers between devices: 1.02 us -> 0.71 us  [corner_swap(): return lax.ppermute(value, ('gx', 'gy'), pairs)]
  transfers between devices with their start and end apart: 10 -> 10, of which waited for: 4 -> 5; matrix products, arithmetic and copies ran while one was open for 0% -> 0% of each run, Pallas kernels for 17% -> 18%
where the time goes in v4:
time: 24.4 us; the launch traced here: 24.2 us
  Pallas kernels  9.56 us (39%)
  starting transfers between devices  8.1 us (33%)
  waiting for transfers between devices  5.82 us (24%)
  between operations  0.73 us (3%)
    pallas_call x11, Pallas kernels, run(): pl.pallas_call(kernel, out_shape=shapes, in_specs=in_specs or [VMEM] * le...  9.56 us
    ppermute x5, starting transfers between devices, swap_xy(): return lax.ppermute(value, ('gx', 'gy'), pairs)  4.09 us
    ppermute x5, waiting for transfers between devices, swap_xy(): return lax.ppermute(value, ('gx', 'gy'), pairs)  3.13 us
    ppermute x2, starting transfers between devices, swap(): return lax.ppermute(value, axis, [(i, i ^ hop) for i in range(n)])  2.01 us
    ppermute x1, starting transfers between devices, z_swaps(): even = lax.ppermute(value, 'gz', [(i, i ^ 1) for i in range(n)])  1.36 us
    ppermute x1, waiting for transfers between devices, z_swaps(): even = lax.ppermute(value, 'gz', [(i, i ^ 1) for i in range(n)])  1.13 us
    ppermute x1, waiting for transfers between devices, corner_swap(): return lax.ppermute(value, ('gx', 'gy'), pairs)  0.71 us
    ppermute x1, starting transfers between devices, corner_swap(): return lax.ppermute(value, ('gx', 'gy'), pairs)  0.63 us
  transfers between devices with their start and end apart: 10, of which 5 were waited for; matrix products, arithmetic and copies ran while one was open for 0% of the time, Pallas kernels for 18%

profile of v4, /device:TPU:19, one launch (start us, length us, event | category | flops | bytes accessed | tf_op | source)
XLA Modules:
  0.0 24.2 jit_solution(1002088335764101789)
XLA Ops:
  0.6 2.4 %shard_map.50 = (f32[4,64,128]{2,1,0:T(8,128)S(1)}, f32[328,128]{1,0:T(8,128)S(1)}, f32[16,128]{1,0:T(8,128)S(1)}, f32[16,128]{1,0:T(8,128)S(1)}) custom-call(bf16[32,4,64,128]{3,2,1,0:T(8,128)(2,1)} %f_hbm.1, bf16[27,32]{1,0:T(8,128)(2,1)} %w_hbm.1, s32[4,64,128]{2,1,0:T(8,128)} %mask_hbm.1), custom_call_target="tpu_custom_call" | custom-call | tf_op jit(solution)/shard_map/pallas_call | solution.py:23
  3.0 0.3 %collective-permute-start = (f32[328,128]{1,0:T(8,128)S(1)}, f32[328,128]{1,0:T(8,128)S(1)}, u32[]{:S(2)}, u32[]{:S(2)}) collective-permute-start(f32[328,128]{1,0:T(8,128)S(1)} %get-tuple-element.18.own_ref), channel_id=1, source_target_pairs={{0,16},{4,20},{8,24},{12,28},{16,0},{20,4},{24,8},{28,12},{1,17},{... | collective-permute-start | bytes 503816 | tf_op jit(solution)/shard_map/ppermute | solution.py:546
  3.3 3.0 %collective-permute-start.2 = (f32[16,128]{1,0:T(8,128)S(1)}, f32[16,128]{1,0:T(8,128)S(1)}, u32[]{:S(2)}, u32[]{:S(2)}) collective-permute-start(f32[16,128]{1,0:T(8,128)S(1)} %get-tuple-element.19), channel_id=1, source_target_pairs={{0,28},{4,24},{8,20},{12,16},{16,12},{20,8},{24,4},{28,0},{1,29},{... | collective-permute-start | bytes 24584 | tf_op jit(solution)/shard_map/ppermute | solution.py:546
  6.3 0.0 collective-permute-start.1
  6.3 0.8 %collective-permute-start.4 = (f32[16,128]{1,0:T(8,128)S(1)}, f32[16,128]{1,0:T(8,128)S(1)}, u32[]{:S(2)}, u32[]{:S(2)}) collective-permute-start(f32[16,128]{1,0:T(8,128)S(1)} %get-tuple-element.20), channel_id=1, source_target_pairs={{0,20},{4,16},{8,28},{12,24},{16,4},{20,0},{24,12},{28,8},{1,21},{... | collective-permute-start | bytes 24584 | tf_op jit(solution)/shard_map/ppermute | solution.py:546
  7.1 0.0 collective-permute-start.3
  7.1 3.1 %collective-permute-done.2.xcross_ref = f32[16,128]{1,0:T(8,128)S(1)} collective-permute-done((f32[16,128]{1,0:T(8,128)S(1)}, f32[16,128]{1,0:T(8,128)S(1)}, u32[]{:S(2)}, u32[]{:S(2)}) %collective-permute-start.2) | collective-permute-done | bytes 8224 | tf_op jit(solution)/shard_map/ppermute | solution.py:546
  10.2 0.0 collective-permute-done.1.cross_ref
  10.2 0.0 collective-permute-done.4.xchip_ref
  10.2 0.0 collective-permute-done.3.chip_ref
  10.2 0.0 collective-permute-done.far_ref
  10.2 0.5 %shard_map.51 = (f32[4,64,128]{2,1,0:T(8,128)S(1)}, f32[136,256]{1,0:T(8,128)S(1)}, s32[72,256]{1,0:T(8,128)S(1)}) custom-call(f32[4,64,128]{2,1,0:T(8,128)S(1)} %get-tuple-element.17.s_ref, f32[328,128]{1,0:T(8,128)S(1)} %get-tuple-element.18.own_ref, f32[328,128]{1,0:T(8,128)S(1)} %collective-permute-done.far_ref, ...), custom_call_target="tpu_custom_call" | custom-call | tf_op jit(solution)/shard_map/pallas_call | solution.py:23
  10.7 1.4 %collective-permute-start.5 = (s32[72,256]{1,0:T(8,128)S(1)}, s32[72,256]{1,0:T(8,128)S(1)}, u32[]{:S(2)}, u32[]{:S(2)}) collective-permute-start(s32[72,256]{1,0:T(8,128)S(1)} %get-tuple-element.24), channel_id=1, source_target_pairs={{0,1},{1,0},{2,3},{3,2},{4,5},{5,4},{6,7},{7,6},{8,9},{9,8},{10,11... | collective-permute-start | bytes 221192 | tf_op jit(solution)/shard_map/ppermute | solution.py:562
  12.1 0.0 collective-permute-start.6
  12.1 1.6 %shard_map.52 = (f32[128,256]{1,0:T(8,128)S(1)}, f32[262,8,128]{2,1,0:T(8,128)S(1)}, f32[120,8,128]{2,1,0:T(8,128)S(1)}, f32[120,8,128]{2,1,0:T(8,128)S(1)}, f32...) custom-call(f32[136,256]{1,0:T(8,128)S(1)} %get-tuple-element.21.zm_ref), custom_call_target="tpu_custom_call" | custom-call | tf_op jit(solution)/shard_map/pallas_call | solution.py:23
  13.7 1.1 %collective-permute-done.5.got_ref.even_ref = s32[72,256]{1,0:T(8,128)S(1)} collective-permute-done((s32[72,256]{1,0:T(8,128)S(1)}, s32[72,256]{1,0:T(8,128)S(1)}, u32[]{:S(2)}, u32[]{:S(2)}) %collective-permute-start.5) | collective-permute-done | bytes 73760 | tf_op jit(solution)/shard_map/ppermute | solution.py:562
  14.8 0.8 %shard_map.53.acc_ref = f32[128,256]{1,0:T(8,128)S(1)} custom-call(f32[128,256]{1,0:T(8,128)S(1)} %get-tuple-element.22.acc_ref, f32[262,8,128]{2,1,0:T(8,128)S(1)} %get-tuple-element.23.table, f32[136,256]{1,0:T(8,128)S(1)} %get-tuple-element.21.zm_ref, s32[72,256]{1,0:T(8,128)S(1)} %collective-permute-done.5.got_ref.even_ref), custom_call_target="tpu_custom_call" | custom-call | tf_op jit(solution)/shard_map/pallas_call | solution.py:23
  15.5 0.4 %collective-permute-done.6.got_ref.odd_ref = s32[72,256]{1,0:T(8,128)S(1)} collective-permute-done((s32[72,256]{1,0:T(8,128)S(1)}, s32[72,256]{1,0:T(8,128)S(1)}, u32[]{:S(2)}, u32[]{:S(2)}) %collective-permute-start.6) | collective-permute-done | bytes 73760 | tf_op jit(solution)/shard_map/ppermute | solution.py:567
  15.9 0.9 %shard_map.54.own_ref.value_ref._ = f32[4,64,128]{2,1,0:T(8,128)S(1)} custom-call(f32[128,256]{1,0:T(8,128)S(1)} %shard_map.53.acc_ref, f32[262,8,128]{2,1,0:T(8,128)S(1)} %get-tuple-element.23.table, f32[136,256]{1,0:T(8,128)S(1)} %get-tuple-element.21.zm_ref, s32[72,256]{1,0:T(8,128)S(1)} %collective-permute-done.6.got_ref.odd_ref), custom_call_target="tpu_custom_call" | custom-call | tf_op jit(solution)/shard_map/pallas_call | solution.py:23
  16.8 0.1 shard_map.56
  16.9 0.9 %collective-permute-start.7 = (s16[4,64,128]{2,1,0:T(8,128)(2,1)S(1)}, s16[4,64,128]{2,1,0:T(8,128)(2,1)S(1)}, u32[]{:S(2)}, u32[]{:S(2)}) collective-permute-start(s16[4,64,128]{2,1,0:T(8,128)(2,1)S(1)} %shard_map.56), channel_id=1, source_target_pairs={{0,4},{4,0},{8,12},{12,8},{1,5},{5,1},{9,13},{13,9},{2,6},{6,2},{1... | collective-permute-start | bytes 196616 | tf_op jit(solution)/shard_map/ppermute | solution.py:540
  17.8 1.1 %collective-permute-start.8 = (s16[4,64,128]{2,1,0:T(8,128)(2,1)S(1)}, s16[4,64,128]{2,1,0:T(8,128)(2,1)S(1)}, u32[]{:S(2)}, u32[]{:S(2)}) collective-permute-start(s16[4,64,128]{2,1,0:T(8,128)(2,1)S(1)} %shard_map.56), channel_id=1, source_target_pairs={{0,8},{4,12},{8,0},{12,4},{1,9},{5,13},{9,1},{13,5},{2,10},{6,14},... | collective-permute-start | bytes 196616 | tf_op jit(solution)/shard_map/ppermute | solution.py:540
  18.9 0.6 %collective-permute-start.9 = (s16[4,64,128]{2,1,0:T(8,128)(2,1)S(1)}, s16[4,64,128]{2,1,0:T(8,128)(2,1)S(1)}, u32[]{:S(2)}, u32[]{:S(2)}) collective-permute-start(s16[4,64,128]{2,1,0:T(8,128)(2,1)S(1)} %shard_map.56), channel_id=1, source_target_pairs={{0,16},{4,8},{8,4},{12,28},{16,0},{20,24},{24,20},{28,12},{1,17},{... | collective-permute-start | bytes 196616 | tf_op jit(solution)/shard_map/ppermute | solution.py:576
  19.5 0.6 %shard_map.55.start_ref = f32[4,64,128]{2,1,0:T(8,128)S(1)} custom-call(f32[4,64,128]{2,1,0:T(8,128)S(1)} %shard_map.54.own_ref.value_ref._, f32[120,8,128]{2,1,0:T(8,128)S(1)} %get-tuple-element.25.table), custom_call_target="tpu_custom_call" | custom-call | tf_op jit(solution)/shard_map/pallas_call | solution.py:23
  20.2 0.1 shard_map.59.score_ref
  20.3 0.0 collective-permute-done.7.code_ref
  20.3 0.7 %shard_map.57.start_ref = f32[4,64,128]{2,1,0:T(8,128)S(1)} custom-call(f32[4,64,128]{2,1,0:T(8,128)S(1)} %shard_map.55.start_ref, s16[4,64,128]{2,1,0:T(8,128)(2,1)S(1)} %collective-permute-done.7.code_ref, f32[120,8,128]{2,1,0:T(8,128)S(1)} %get-tuple-element.26.table), custom_call_target="tpu_custom_call" | custom-call | tf_op jit(solution)/shard_map/pallas_call | solution.py:23
  21.0 0.5 %collective-permute-done.8.code_ref = s16[4,64,128]{2,1,0:T(8,128)(2,1)S(1)} collective-permute-done((s16[4,64,128]{2,1,0:T(8,128)(2,1)S(1)}, s16[4,64,128]{2,1,0:T(8,128)(2,1)S(1)}, u32[]{:S(2)}, u32[]{:S(2)}) %collective-permute-start.8) | collective-permute-done | bytes 65568 | tf_op jit(solution)/shard_map/ppermute | solution.py:540
  21.5 0.7 %shard_map.58.start_ref = f32[4,64,128]{2,1,0:T(8,128)S(1)} custom-call(f32[4,64,128]{2,1,0:T(8,128)S(1)} %shard_map.57.start_ref, s16[4,64,128]{2,1,0:T(8,128)(2,1)S(1)} %collective-permute-done.8.code_ref, f32[120,8,128]{2,1,0:T(8,128)S(1)} %get-tuple-element.27.table), custom_call_target="tpu_custom_call" | custom-call | tf_op jit(solution)/shard_map/pallas_call | solution.py:23
  22.2 0.7 %collective-permute-done.9.code_ref = s16[4,64,128]{2,1,0:T(8,128)(2,1)S(1)} collective-permute-done((s16[4,64,128]{2,1,0:T(8,128)(2,1)S(1)}, s16[4,64,128]{2,1,0:T(8,128)(2,1)S(1)}, u32[]{:S(2)}, u32[]{:S(2)}) %collective-permute-start.9) | collective-permute-done | bytes 65568 | tf_op jit(solution)/shard_map/ppermute | solution.py:576
  22.9 1.3 %shard_map.60 = (f32[4,64,128]{2,1,0:T(8,128)}, f32[4,64,128]{2,1,0:T(8,128)}) custom-call(f32[4,64,128]{2,1,0:T(8,128)S(1)} %shard_map.58.start_ref, s16[4,64,128]{2,1,0:T(8,128)(2,1)S(1)} %collective-permute-done.9.code_ref, f32[120,8,128]{2,1,0:T(8,128)S(1)} %get-tuple-element.28.table, f32[4,64,128]{2,1,0:T(8,128)S(1)} %shard_map.59.score_ref), custom_call_target="tpu_custom_call" | custom-call | tf_op jit(solution)/shard_map/pallas_call | solution.py:23
Async XLA Ops:
  3.0 7.2 %collective-permute-start = (f32[328,128]{1,0:T(8,128)S(1)}, f32[328,128]{1,0:T(8,128)S(1)}, u32[]{:S(2)}, u32[]{:S(2)}) collective-permute-start(f32[328,128]{1,0:T(8,128)S(1)} %get-tuple-element.18.own_ref), channel_id=1, source_target_pairs={{0,16},{4,20},{8,24},{12,28},{16,0},{20,4},{24,8},{28,12},{1,17},{... | collective-permute-start | bytes 503816 | tf_op jit(solution)/shard_map/ppermute | solution.py:546
  3.3 6.9 %collective-permute-start.2 = (f32[16,128]{1,0:T(8,128)S(1)}, f32[16,128]{1,0:T(8,128)S(1)}, u32[]{:S(2)}, u32[]{:S(2)}) collective-permute-start(f32[16,128]{1,0:T(8,128)S(1)} %get-tuple-element.19), channel_id=1, source_target_pairs={{0,28},{4,24},{8,20},{12,16},{16,12},{20,8},{24,4},{28,0},{1,29},{... | collective-permute-start | bytes 24584 | tf_op jit(solution)/shard_map/ppermute | solution.py:546
  6.3 3.9 %collective-permute-start.1 = (f32[16,128]{1,0:T(8,128)S(1)}, f32[16,128]{1,0:T(8,128)S(1)}, u32[]{:S(2)}, u32[]{:S(2)}) collective-permute-start(f32[16,128]{1,0:T(8,128)S(1)} %get-tuple-element.19), channel_id=1, source_target_pairs={{0,12},{4,8},{8,4},{12,0},{16,28},{20,24},{24,20},{28,16},{1,13},{... | collective-permute-start | bytes 24584 | tf_op jit(solution)/shard_map/ppermute | solution.py:546
  6.3 3.9 %collective-permute-start.4 = (f32[16,128]{1,0:T(8,128)S(1)}, f32[16,128]{1,0:T(8,128)S(1)}, u32[]{:S(2)}, u32[]{:S(2)}) collective-permute-start(f32[16,128]{1,0:T(8,128)S(1)} %get-tuple-element.20), channel_id=1, source_target_pairs={{0,20},{4,16},{8,28},{12,24},{16,4},{20,0},{24,12},{28,8},{1,21},{... | collective-permute-start | bytes 24584 | tf_op jit(solution)/shard_map/ppermute | solution.py:546
  7.1 3.1 %collective-permute-start.3 = (f32[16,128]{1,0:T(8,128)S(1)}, f32[16,128]{1,0:T(8,128)S(1)}, u32[]{:S(2)}, u32[]{:S(2)}) collective-permute-start(f32[16,128]{1,0:T(8,128)S(1)} %get-tuple-element.20), channel_id=1, source_target_pairs={{0,4},{4,0},{8,12},{12,8},{16,20},{20,16},{24,28},{28,24},{1,5},{5... | collective-permute-start | bytes 24584 | tf_op jit(solution)/shard_map/ppermute | solution.py:546
  10.7 4.1 %collective-permute-start.5 = (s32[72,256]{1,0:T(8,128)S(1)}, s32[72,256]{1,0:T(8,128)S(1)}, u32[]{:S(2)}, u32[]{:S(2)}) collective-permute-start(s32[72,256]{1,0:T(8,128)S(1)} %get-tuple-element.24), channel_id=1, source_target_pairs={{0,1},{1,0},{2,3},{3,2},{4,5},{5,4},{6,7},{7,6},{8,9},{9,8},{10,11... | collective-permute-start | bytes 221192 | tf_op jit(solution)/shard_map/ppermute | solution.py:562
  12.1 3.8 %collective-permute-start.6 = (s32[72,256]{1,0:T(8,128)S(1)}, s32[72,256]{1,0:T(8,128)S(1)}, u32[]{:S(2)}, u32[]{:S(2)}) collective-permute-start(s32[72,256]{1,0:T(8,128)S(1)} %get-tuple-element.24), channel_id=1, source_target_pairs={{0,4},{1,2},{2,1},{3,7},{4,0},{5,6},{6,5},{7,3},{8,12},{9,10},{10,... | collective-permute-start | bytes 221192 | tf_op jit(solution)/shard_map/ppermute | solution.py:567
  16.9 3.4 %collective-permute-start.7 = (s16[4,64,128]{2,1,0:T(8,128)(2,1)S(1)}, s16[4,64,128]{2,1,0:T(8,128)(2,1)S(1)}, u32[]{:S(2)}, u32[]{:S(2)}) collective-permute-start(s16[4,64,128]{2,1,0:T(8,128)(2,1)S(1)} %shard_map.56), channel_id=1, source_target_pairs={{0,4},{4,0},{8,12},{12,8},{1,5},{5,1},{9,13},{13,9},{2,6},{6,2},{1... | collective-permute-start | bytes 196616 | tf_op jit(solution)/shard_map/ppermute | solution.py:540
  17.8 3.7 %collective-permute-start.8 = (s16[4,64,128]{2,1,0:T(8,128)(2,1)S(1)}, s16[4,64,128]{2,1,0:T(8,128)(2,1)S(1)}, u32[]{:S(2)}, u32[]{:S(2)}) collective-permute-start(s16[4,64,128]{2,1,0:T(8,128)(2,1)S(1)} %shard_map.56), channel_id=1, source_target_pairs={{0,8},{4,12},{8,0},{12,4},{1,9},{5,13},{9,1},{13,5},{2,10},{6,14},... | collective-permute-start | bytes 196616 | tf_op jit(solution)/shard_map/ppermute | solution.py:540
  18.9 4.0 %collective-permute-start.9 = (s16[4,64,128]{2,1,0:T(8,128)(2,1)S(1)}, s16[4,64,128]{2,1,0:T(8,128)(2,1)S(1)}, u32[]{:S(2)}, u32[]{:S(2)}) collective-permute-start(s16[4,64,128]{2,1,0:T(8,128)(2,1)S(1)} %shard_map.56), channel_id=1, source_target_pairs={{0,16},{4,8},{8,4},{12,28},{16,0},{20,24},{24,20},{28,12},{1,17},{... | collective-permute-start | bytes 196616 | tf_op jit(solution)/shard_map/ppermute | solution.py:576

commit v5 on v4

--- a/solution.py
+++ b/solution.py
@@ -373,7 +373,8 @@
     return jnp.minimum(best, pltpu.roll(best, 7, 0))
 
 
-def z_far_kernel(even, partner, size_x, size_y, acc_ref, table, zm_ref, got_ref, out_ref, source, work):
+def z_far_kernel(even, partner, size_x, size_y, acc_ref, table, zm_ref, got_ref, out_ref, *refs):
+    *code_ref, source, work = refs
     index, last = lax.axis_index("gz"), lax.axis_size("gz") - 1
     odd = index % 2 == 1
     low = odd if even else jnp.logical_not(odd)
@@ -435,8 +436,10 @@
         per = LANES // size_y
         for k, cols in enumerate(lanes):
             best = work[:, cols].T
+            code = encode(best).astype(jnp.int16)
             for i in range(per):
                 out_ref[k * per + i] = best[i * size_y : (i + 1) * size_y]
+                code_ref[0][k * per + i] = code[i * size_y : (i + 1) * size_y]
 
 
 def score_kernel(score_in, even_ref, odd_ref, _, score_ref):
@@ -481,34 +484,19 @@
                 out_ref[x, 8 * b : 8 * b + 8, :] = v if scale == 1.0 else v * scale
 
 
-def encode_kernel(value_ref, code_ref):
-    code_ref[...] = encode(value_ref[...]).astype(jnp.int16)
-
-
-def y_own_kernel(own_ref, table, out_ref):
-    y_sweep((own_ref,), (table,), None, out_ref, 1.0)
-
-
-def in_reach(hop):
+def y_near_kernel(own_ref, code_ref, table_0, table_1, out_ref, block):
+    block[...] = decode(code_ref[...])
+    y_sweep((own_ref, block), (table_0, table_1), None, out_ref, 1.0)
+
+
+def y_across_kernel(start_ref, code_ref, table, out_ref, block):
+    block[...] = decode(code_ref[...])
+    y_sweep((block,), (table,), start_ref, out_ref, 1.0)
+
+
+def y_last_kernel(start_ref, code_ref, table, score_ref, depth_hbm, score_hbm, block, depth, sems):
     index = lax.axis_index("gy")
-    return jnp.abs((index ^ hop) - index) < 3
-
-
-def y_far_kernel(hop, start_ref, code_ref, table, out_ref, block):
-    near = in_reach(hop)
-
-    @pl.when(near)
-    def _():
-        block[...] = decode(code_ref[...])
-        y_sweep((block,), (table,), start_ref, out_ref, 1.0)
-
-    @pl.when(jnp.logical_not(near))
-    def _():
-        out_ref[...] = start_ref[...]
-
-
-def y_last_kernel(hop, start_ref, code_ref, table, score_ref, depth_hbm, score_hbm, block, depth, sems):
-    near = in_reach(hop)
+    near = jnp.abs((index ^ 3) - index) < 3
     size_y = depth.shape[1]
     scores = pltpu.make_async_copy(score_ref, score_hbm, sems.at[0])
     scores.start()
@@ -665,25 +653,22 @@
     own = functools.partial(z_own_kernel, size_y)
     best, table, *kept = call(own, [(LANES, lines), (LANES - Z_FLOOR, 8, LANES)] + [tables] * 4)(zm)
     work = [pltpu.VMEM((LANES, lines), jnp.float32)] * 2
-    for first, got, shape in ((True, even, (LANES, lines)), (False, odd, brick)):
+    coded = jax.ShapeDtypeStruct(brick, jnp.int16)
+    for first, got, shapes in ((True, even, [(LANES, lines)]), (False, odd, [brick, coded])):
         far = functools.partial(z_far_kernel, first, partner, size_x, size_y)
-        (best,) = call(far, [shape], work)(best, table, zm, got)
-    (score,) = call(score_kernel, [brick])(score, even, odd, best)
+        best, *code = call(far, shapes, work)(best, table, zm, got)
     if not partner:
         best = x_minima(best, size_x)
-
-    (code,) = call(encode_kernel, [brick], kind=jnp.int16)(best)
-    blocks = {1: swap(code, "gy", 1), 2: swap(code, "gy", 2), 3: corner_swap(code)}
-    (near,) = call(y_own_kernel, [brick])(best, kept[0])
+        code = [encode(best).astype(jnp.int16)]
+
+    code = code[0]
+    chip, across, corner = swap(code, "gy", 1), swap(code, "gy", 2), corner_swap(code)
     block = [pltpu.VMEM(brick, jnp.float32)]
-    *hops, final = blocks
-    for hop in hops:
-        far = functools.partial(y_far_kernel, hop)
-        (near,) = call(far, [brick], block)(near, blocks[hop], kept[hop])
+    (near,) = call(y_near_kernel, [brick], block)(best, chip, kept[0], kept[1])
+    (near,) = call(y_across_kernel, [brick], block)(near, across, kept[2])
+    (score,) = call(score_kernel, [brick])(score, even, odd, near)
     last = [*block, *block, pltpu.SemaphoreType.DMA((3,))]
-    depth, score = call(
-        functools.partial(y_last_kernel, final), [brick, brick], last, out_spec=HBM
-    )(near, blocks[final], kept[final], score)
+    depth, score = call(y_last_kernel, [brick, brick], last, out_spec=HBM)(near, corner, kept[3], score)
     return score, depth
 
 

time: 24.4 us -> 24.4 us (level)
    pallas_call x11 -> x9, Pallas kernels: 9.56 us -> 9.52 us  [run(): pl.pallas_call(kernel, out_shape=shapes, in_specs=in_specs or [VMEM] * le...]
where the time goes in v5:
time: 24.4 us; the launch traced here: 24.2 us
  Pallas kernels  9.52 us (39%)
  starting transfers between devices  8.1 us (33%)
  waiting for transfers between devices  5.87 us (24%)
  between operations  0.7 us (3%)
    pallas_call x9, Pallas kernels, run(): pl.pallas_call(kernel, out_shape=shapes, in_specs=in_specs or [VMEM] * le...  9.52 us
    ppermute x5, starting transfers between devices, swap_xy(): return lax.ppermute(value, ('gx', 'gy'), pairs)  4.09 us
    ppermute x5, waiting for transfers between devices, swap_xy(): return lax.ppermute(value, ('gx', 'gy'), pairs)  3.13 us
    ppermute x2, starting transfers between devices, swap(): return lax.ppermute(value, axis, [(i, i ^ hop) for i in range(n)])  2.01 us
    ppermute x1, starting transfers between devices, z_swaps(): even = lax.ppermute(value, 'gz', [(i, i ^ 1) for i in range(n)])  1.36 us
    ppermute x1, waiting for transfers between devices, z_swaps(): even = lax.ppermute(value, 'gz', [(i, i ^ 1) for i in range(n)])  1.13 us
    ppermute x2, waiting for transfers between devices, swap(): return lax.ppermute(value, axis, [(i, i ^ hop) for i in range(n)])  0.65 us
    ppermute x1, starting transfers between devices, corner_swap(): return lax.ppermute(value, ('gx', 'gy'), pairs)  0.63 us
  transfers between devices with their start and end apart: 10, of which 5 were waited for; matrix products, arithmetic and copies ran while one was open for 0% of the time, Pallas kernels for 18%

profile of v5, /device:TPU:19, one launch (start us, length us, event | category | flops | bytes accessed | tf_op | source)
XLA Modules:
  0.0 24.2 jit_solution(6350743621717601545)
XLA Ops:
  0.6 2.4 %shard_map.50 = (f32[4,64,128]{2,1,0:T(8,128)S(1)}, f32[328,128]{1,0:T(8,128)S(1)}, f32[16,128]{1,0:T(8,128)S(1)}, f32[16,128]{1,0:T(8,128)S(1)}) custom-call(bf16[32,4,64,128]{3,2,1,0:T(8,128)(2,1)} %f_hbm.1, bf16[27,32]{1,0:T(8,128)(2,1)} %w_hbm.1, s32[4,64,128]{2,1,0:T(8,128)} %mask_hbm.1), custom_call_target="tpu_custom_call" | custom-call | tf_op jit(solution)/shard_map/pallas_call | solution.py:23
  3.0 0.3 %collective-permute-start = (f32[328,128]{1,0:T(8,128)S(1)}, f32[328,128]{1,0:T(8,128)S(1)}, u32[]{:S(2)}, u32[]{:S(2)}) collective-permute-start(f32[328,128]{1,0:T(8,128)S(1)} %get-tuple-element.20.own_ref), channel_id=1, source_target_pairs={{0,16},{4,20},{8,24},{12,28},{16,0},{20,4},{24,8},{28,12},{1,17},{... | collective-permute-start | bytes 503816 | tf_op jit(solution)/shard_map/ppermute | solution.py:534
  3.3 3.0 %collective-permute-start.2 = (f32[16,128]{1,0:T(8,128)S(1)}, f32[16,128]{1,0:T(8,128)S(1)}, u32[]{:S(2)}, u32[]{:S(2)}) collective-permute-start(f32[16,128]{1,0:T(8,128)S(1)} %get-tuple-element.21), channel_id=1, source_target_pairs={{0,28},{4,24},{8,20},{12,16},{16,12},{20,8},{24,4},{28,0},{1,29},{... | collective-permute-start | bytes 24584 | tf_op jit(solution)/shard_map/ppermute | solution.py:534
  6.3 0.0 collective-permute-start.1
  6.3 0.8 %collective-permute-start.4 = (f32[16,128]{1,0:T(8,128)S(1)}, f32[16,128]{1,0:T(8,128)S(1)}, u32[]{:S(2)}, u32[]{:S(2)}) collective-permute-start(f32[16,128]{1,0:T(8,128)S(1)} %get-tuple-element.22), channel_id=1, source_target_pairs={{0,20},{4,16},{8,28},{12,24},{16,4},{20,0},{24,12},{28,8},{1,21},{... | collective-permute-start | bytes 24584 | tf_op jit(solution)/shard_map/ppermute | solution.py:534
  7.1 0.0 collective-permute-start.3
  7.1 3.1 %collective-permute-done.2.xcross_ref = f32[16,128]{1,0:T(8,128)S(1)} collective-permute-done((f32[16,128]{1,0:T(8,128)S(1)}, f32[16,128]{1,0:T(8,128)S(1)}, u32[]{:S(2)}, u32[]{:S(2)}) %collective-permute-start.2) | collective-permute-done | bytes 8224 | tf_op jit(solution)/shard_map/ppermute | solution.py:534
  10.2 0.0 collective-permute-done.1.cross_ref
  10.2 0.0 collective-permute-done.4.xchip_ref
  10.2 0.0 collective-permute-done.3.chip_ref
  10.2 0.0 collective-permute-done.far_ref
  10.2 0.5 %shard_map.51 = (f32[4,64,128]{2,1,0:T(8,128)S(1)}, f32[136,256]{1,0:T(8,128)S(1)}, s32[72,256]{1,0:T(8,128)S(1)}) custom-call(f32[4,64,128]{2,1,0:T(8,128)S(1)} %get-tuple-element.19.s_ref, f32[328,128]{1,0:T(8,128)S(1)} %get-tuple-element.20.own_ref, f32[328,128]{1,0:T(8,128)S(1)} %collective-permute-done.far_ref, ...), custom_call_target="tpu_custom_call" | custom-call | tf_op jit(solution)/shard_map/pallas_call | solution.py:23
  10.7 1.4 %collective-permute-start.5 = (s32[72,256]{1,0:T(8,128)S(1)}, s32[72,256]{1,0:T(8,128)S(1)}, u32[]{:S(2)}, u32[]{:S(2)}) collective-permute-start(s32[72,256]{1,0:T(8,128)S(1)} %get-tuple-element.26), channel_id=1, source_target_pairs={{0,1},{1,0},{2,3},{3,2},{4,5},{5,4},{6,7},{7,6},{8,9},{9,8},{10,11... | collective-permute-start | bytes 221192 | tf_op jit(solution)/shard_map/ppermute | solution.py:550
  12.1 0.0 collective-permute-start.6
  12.1 1.6 %shard_map.52 = (f32[128,256]{1,0:T(8,128)S(1)}, f32[262,8,128]{2,1,0:T(8,128)S(1)}, f32[120,8,128]{2,1,0:T(8,128)S(1)}, f32[120,8,128]{2,1,0:T(8,128)S(1)}, f32...) custom-call(f32[136,256]{1,0:T(8,128)S(1)} %get-tuple-element.23.zm_ref), custom_call_target="tpu_custom_call" | custom-call | tf_op jit(solution)/shard_map/pallas_call | solution.py:23
  13.7 1.1 %collective-permute-done.5.got_ref.even_ref = s32[72,256]{1,0:T(8,128)S(1)} collective-permute-done((s32[72,256]{1,0:T(8,128)S(1)}, s32[72,256]{1,0:T(8,128)S(1)}, u32[]{:S(2)}, u32[]{:S(2)}) %collective-permute-start.5) | collective-permute-done | bytes 73760 | tf_op jit(solution)/shard_map/ppermute | solution.py:550
  14.8 0.8 %shard_map.53.acc_ref = f32[128,256]{1,0:T(8,128)S(1)} custom-call(f32[128,256]{1,0:T(8,128)S(1)} %get-tuple-element.24.acc_ref, f32[262,8,128]{2,1,0:T(8,128)S(1)} %get-tuple-element.25.table, f32[136,256]{1,0:T(8,128)S(1)} %get-tuple-element.23.zm_ref, s32[72,256]{1,0:T(8,128)S(1)} %collective-permute-done.5.got_ref.even_ref), custom_call_target="tpu_custom_call" | custom-call | tf_op jit(solution)/shard_map/pallas_call | solution.py:23
  15.5 0.4 %collective-permute-done.6.got_ref.odd_ref = s32[72,256]{1,0:T(8,128)S(1)} collective-permute-done((s32[72,256]{1,0:T(8,128)S(1)}, s32[72,256]{1,0:T(8,128)S(1)}, u32[]{:S(2)}, u32[]{:S(2)}) %collective-permute-start.6) | collective-permute-done | bytes 73760 | tf_op jit(solution)/shard_map/ppermute | solution.py:555
  15.9 0.9 %shard_map.54 = (f32[4,64,128]{2,1,0:T(8,128)S(1)}, s16[4,64,128]{2,1,0:T(8,128)(2,1)S(1)}) custom-call(f32[128,256]{1,0:T(8,128)S(1)} %shard_map.53.acc_ref, f32[262,8,128]{2,1,0:T(8,128)S(1)} %get-tuple-element.25.table, f32[136,256]{1,0:T(8,128)S(1)} %get-tuple-element.23.zm_ref, s32[72,256]{1,0:T(8,128)S(1)} %collective-permute-done.6.got_ref.odd_ref), custom_call_target="tpu_custom_call" | custom-call | tf_op jit(solution)/shard_map/pallas_call | solution.py:23
  16.8 0.9 %collective-permute-start.7 = (s16[4,64,128]{2,1,0:T(8,128)(2,1)S(1)}, s16[4,64,128]{2,1,0:T(8,128)(2,1)S(1)}, u32[]{:S(2)}, u32[]{:S(2)}) collective-permute-start(s16[4,64,128]{2,1,0:T(8,128)(2,1)S(1)} %get-tuple-element.28), channel_id=1, source_target_pairs={{0,4},{4,0},{8,12},{12,8},{1,5},{5,1},{9,13},{13,9},{2,6},{6,2},{1... | collective-permute-start | bytes 196616 | tf_op jit(solution)/shard_map/ppermute | solution.py:528
  17.8 1.1 %collective-permute-start.8 = (s16[4,64,128]{2,1,0:T(8,128)(2,1)S(1)}, s16[4,64,128]{2,1,0:T(8,128)(2,1)S(1)}, u32[]{:S(2)}, u32[]{:S(2)}) collective-permute-start(s16[4,64,128]{2,1,0:T(8,128)(2,1)S(1)} %get-tuple-element.28), channel_id=1, source_target_pairs={{0,8},{4,12},{8,0},{12,4},{1,9},{5,13},{9,1},{13,5},{2,10},{6,14},... | collective-permute-start | bytes 196616 | tf_op jit(solution)/shard_map/ppermute | solution.py:528
  18.9 0.6 %collective-permute-start.9 = (s16[4,64,128]{2,1,0:T(8,128)(2,1)S(1)}, s16[4,64,128]{2,1,0:T(8,128)(2,1)S(1)}, u32[]{:S(2)}, u32[]{:S(2)}) collective-permute-start(s16[4,64,128]{2,1,0:T(8,128)(2,1)S(1)} %get-tuple-element.28), channel_id=1, source_target_pairs={{0,16},{4,8},{8,4},{12,28},{16,0},{20,24},{24,20},{28,12},{1,17},{... | collective-permute-start | bytes 196616 | tf_op jit(solution)/shard_map/ppermute | solution.py:564
  19.5 0.0 collective-permute-done.7.code_ref
  19.5 1.3 %shard_map.55.start_ref = f32[4,64,128]{2,1,0:T(8,128)S(1)} custom-call(f32[4,64,128]{2,1,0:T(8,128)S(1)} %get-tuple-element.27.own_ref, s16[4,64,128]{2,1,0:T(8,128)(2,1)S(1)} %collective-permute-done.7.code_ref, f32[120,8,128]{2,1,0:T(8,128)S(1)} %get-tuple-element.29.table_0, f32[120,8,128]{2,1,0:T(8,128)S(1)} %get-tuple-element.30.table_1), custom_call_target="tpu_custom_call" | custom-call | tf_op jit(solution)/shard_map/pallas_call | solution.py:23
  20.8 0.6 %collective-permute-done.8.code_ref = s16[4,64,128]{2,1,0:T(8,128)(2,1)S(1)} collective-permute-done((s16[4,64,128]{2,1,0:T(8,128)(2,1)S(1)}, s16[4,64,128]{2,1,0:T(8,128)(2,1)S(1)}, u32[]{:S(2)}, u32[]{:S(2)}) %collective-permute-start.8) | collective-permute-done | bytes 65568 | tf_op jit(solution)/shard_map/ppermute | solution.py:528
  21.5 0.7 %shard_map.56._.start_ref = f32[4,64,128]{2,1,0:T(8,128)S(1)} custom-call(f32[4,64,128]{2,1,0:T(8,128)S(1)} %shard_map.55.start_ref, s16[4,64,128]{2,1,0:T(8,128)(2,1)S(1)} %collective-permute-done.8.code_ref, f32[120,8,128]{2,1,0:T(8,128)S(1)} %get-tuple-element.31.table), custom_call_target="tpu_custom_call" | custom-call | tf_op jit(solution)/shard_map/pallas_call | solution.py:23
  22.1 0.1 shard_map.57.score_ref
  22.3 0.6 %collective-permute-done.9.code_ref = s16[4,64,128]{2,1,0:T(8,128)(2,1)S(1)} collective-permute-done((s16[4,64,128]{2,1,0:T(8,128)(2,1)S(1)}, s16[4,64,128]{2,1,0:T(8,128)(2,1)S(1)}, u32[]{:S(2)}, u32[]{:S(2)}) %collective-permute-start.9) | collective-permute-done | bytes 65568 | tf_op jit(solution)/shard_map/ppermute | solution.py:564
  22.8 1.3 %shard_map.58 = (f32[4,64,128]{2,1,0:T(8,128)}, f32[4,64,128]{2,1,0:T(8,128)}) custom-call(f32[4,64,128]{2,1,0:T(8,128)S(1)} %shard_map.56._.start_ref, s16[4,64,128]{2,1,0:T(8,128)(2,1)S(1)} %collective-permute-done.9.code_ref, f32[120,8,128]{2,1,0:T(8,128)S(1)} %get-tuple-element.32.table, f32[4,64,128]{2,1,0:T(8,128)S(1)} %shard_map.57.score_ref), custom_call_target="tpu_custom_call" | custom-call | tf_op jit(solution)/shard_map/pallas_call | solution.py:23
Async XLA Ops:
  3.0 7.2 %collective-permute-start = (f32[328,128]{1,0:T(8,128)S(1)}, f32[328,128]{1,0:T(8,128)S(1)}, u32[]{:S(2)}, u32[]{:S(2)}) collective-permute-start(f32[328,128]{1,0:T(8,128)S(1)} %get-tuple-element.20.own_ref), channel_id=1, source_target_pairs={{0,16},{4,20},{8,24},{12,28},{16,0},{20,4},{24,8},{28,12},{1,17},{... | collective-permute-start | bytes 503816 | tf_op jit(solution)/shard_map/ppermute | solution.py:534
  3.3 6.9 %collective-permute-start.2 = (f32[16,128]{1,0:T(8,128)S(1)}, f32[16,128]{1,0:T(8,128)S(1)}, u32[]{:S(2)}, u32[]{:S(2)}) collective-permute-start(f32[16,128]{1,0:T(8,128)S(1)} %get-tuple-element.21), channel_id=1, source_target_pairs={{0,28},{4,24},{8,20},{12,16},{16,12},{20,8},{24,4},{28,0},{1,29},{... | collective-permute-start | bytes 24584 | tf_op jit(solution)/shard_map/ppermute | solution.py:534
  6.3 3.9 %collective-permute-start.1 = (f32[16,128]{1,0:T(8,128)S(1)}, f32[16,128]{1,0:T(8,128)S(1)}, u32[]{:S(2)}, u32[]{:S(2)}) collective-permute-start(f32[16,128]{1,0:T(8,128)S(1)} %get-tuple-element.21), channel_id=1, source_target_pairs={{0,12},{4,8},{8,4},{12,0},{16,28},{20,24},{24,20},{28,16},{1,13},{... | collective-permute-start | bytes 24584 | tf_op jit(solution)/shard_map/ppermute | solution.py:534
  6.3 3.9 %collective-permute-start.4 = (f32[16,128]{1,0:T(8,128)S(1)}, f32[16,128]{1,0:T(8,128)S(1)}, u32[]{:S(2)}, u32[]{:S(2)}) collective-permute-start(f32[16,128]{1,0:T(8,128)S(1)} %get-tuple-element.22), channel_id=1, source_target_pairs={{0,20},{4,16},{8,28},{12,24},{16,4},{20,0},{24,12},{28,8},{1,21},{... | collective-permute-start | bytes 24584 | tf_op jit(solution)/shard_map/ppermute | solution.py:534
  7.1 3.1 %collective-permute-start.3 = (f32[16,128]{1,0:T(8,128)S(1)}, f32[16,128]{1,0:T(8,128)S(1)}, u32[]{:S(2)}, u32[]{:S(2)}) collective-permute-start(f32[16,128]{1,0:T(8,128)S(1)} %get-tuple-element.22), channel_id=1, source_target_pairs={{0,4},{4,0},{8,12},{12,8},{16,20},{20,16},{24,28},{28,24},{1,5},{5... | collective-permute-start | bytes 24584 | tf_op jit(solution)/shard_map/ppermute | solution.py:534
  10.7 4.1 %collective-permute-start.5 = (s32[72,256]{1,0:T(8,128)S(1)}, s32[72,256]{1,0:T(8,128)S(1)}, u32[]{:S(2)}, u32[]{:S(2)}) collective-permute-start(s32[72,256]{1,0:T(8,128)S(1)} %get-tuple-element.26), channel_id=1, source_target_pairs={{0,1},{1,0},{2,3},{3,2},{4,5},{5,4},{6,7},{7,6},{8,9},{9,8},{10,11... | collective-permute-start | bytes 221192 | tf_op jit(solution)/shard_map/ppermute | solution.py:550
  12.1 3.8 %collective-permute-start.6 = (s32[72,256]{1,0:T(8,128)S(1)}, s32[72,256]{1,0:T(8,128)S(1)}, u32[]{:S(2)}, u32[]{:S(2)}) collective-permute-start(s32[72,256]{1,0:T(8,128)S(1)} %get-tuple-element.26), channel_id=1, source_target_pairs={{0,4},{1,2},{2,1},{3,7},{4,0},{5,6},{6,5},{7,3},{8,12},{9,10},{10,... | collective-permute-start | bytes 221192 | tf_op jit(solution)/shard_map/ppermute | solution.py:555
  16.8 2.7 %collective-permute-start.7 = (s16[4,64,128]{2,1,0:T(8,128)(2,1)S(1)}, s16[4,64,128]{2,1,0:T(8,128)(2,1)S(1)}, u32[]{:S(2)}, u32[]{:S(2)}) collective-permute-start(s16[4,64,128]{2,1,0:T(8,128)(2,1)S(1)} %get-tuple-element.28), channel_id=1, source_target_pairs={{0,4},{4,0},{8,12},{12,8},{1,5},{5,1},{9,13},{13,9},{2,6},{6,2},{1... | collective-permute-start | bytes 196616 | tf_op jit(solution)/shard_map/ppermute | solution.py:528
  17.8 3.7 %collective-permute-start.8 = (s16[4,64,128]{2,1,0:T(8,128)(2,1)S(1)}, s16[4,64,128]{2,1,0:T(8,128)(2,1)S(1)}, u32[]{:S(2)}, u32[]{:S(2)}) collective-permute-start(s16[4,64,128]{2,1,0:T(8,128)(2,1)S(1)} %get-tuple-element.28), channel_id=1, source_target_pairs={{0,8},{4,12},{8,0},{12,4},{1,9},{5,13},{9,1},{13,5},{2,10},{6,14},... | collective-permute-start | bytes 196616 | tf_op jit(solution)/shard_map/ppermute | solution.py:528
  18.9 4.0 %collective-permute-start.9 = (s16[4,64,128]{2,1,0:T(8,128)(2,1)S(1)}, s16[4,64,128]{2,1,0:T(8,128)(2,1)S(1)}, u32[]{:S(2)}, u32[]{:S(2)}) collective-permute-start(s16[4,64,128]{2,1,0:T(8,128)(2,1)S(1)} %get-tuple-element.28), channel_id=1, source_target_pairs={{0,16},{4,8},{8,4},{12,28},{16,0},{20,24},{24,20},{28,12},{1,17},{... | collective-permute-start | bytes 196616 | tf_op jit(solution)/shard_map/ppermute | solution.py:564

commit v6 on v5

--- a/solution.py
+++ b/solution.py
@@ -138,12 +138,13 @@
                 copy.wait()
             if x:
                 masks.wait()
-                for p in range(x - 1):
-                    finish(p, at_plane[p])
+                finish(x - half, at_plane[x - half])
         right = jnp.concatenate(
             [f_vmem[:, x, 16 * t : 16 * t + 16, :].reshape(depth, LANES) for t in range(tiles)],
             axis=1,
         )
+        if x == size_x - 1:
+            finish(x - 2, at_plane[x - 2])
         got = jnp.dot(w_big[...], right, preferred_element_type=jnp.float32)
         for a in range(3):
             at = x + 2 - a
@@ -151,7 +152,7 @@
                 first = (3 * a + c) * ROWS
                 part = got[first : first + ROWS, :]
                 acc[at, c] = part if a == 0 or x == 0 else acc[at, c] + part
-    for p in range(half - 1, len(at_plane)):
+    for p in range(size_x - 2, len(at_plane)):
         finish(p, at_plane[p])
     m_ref[len(folds) * size_y :, :] = functools.reduce(jnp.add, folds)
 
@@ -381,56 +382,65 @@
     valid = jnp.where(low, index > 0, index < last)
     count, half = LANES // 8, LANES // 16
     out = out_ref if even else work
-
     own, got = zm_ref[LANES : LANES + 8, :], unpack_ends(got_ref)
-    mine = jnp.where(low, own[0:2], own[2:4]) + jnp.where(valid, jnp.where(low, got[6:8], got[4:6]), 0.0)
-    theirs = jnp.where(low, got[2:4] + own[4:6], got[0:2] + own[6:8])
-    ends = border_minima(cost_of(jnp.concatenate([mine, theirs, mine, theirs], axis=0)), size_x, size_y, partner)
+    lanes = [slice(k * LANES, (k + 1) * LANES) for k in range(zm_ref.shape[1] // LANES)]
     source[0 : LANES // 2, :], source[LANES // 2 :, :] = unpack_rows(got_ref[0 : LANES // 2, :])
 
-    squares = table.at[pl.ds(jnp.where(low, -Z_FLOOR, 1 - LANES - Z_FLOOR), LANES)]
-    lanes = [slice(k * LANES, (k + 1) * LANES) for k in range(zm_ref.shape[1] // LANES)]
-    rows = [jnp.broadcast_to(ends[0:1, cols], (8, LANES)) for cols in lanes]
-    for b in range(count):
-        for row, cols in zip(rows, lanes):
+    def minima(mine, theirs):
+        ends = cost_of(jnp.concatenate([mine, theirs, mine, theirs], axis=0))
+        return border_minima(ends, size_x, size_y, partner)
+
+    def add_ends(ends, start, places):
+        for b in range(count):
             span = slice(8 * b, 8 * b + 8)
-            out[span, cols] = jnp.minimum(acc_ref[span, cols], row + squares[8 * b])
-
-    def slanted(accs, blocks, offset, tiles, reach):
-        for j in tiles:
+            for cols in lanes:
+                best = start[span, cols]
+                for i, place in enumerate(places):
+                    row = jnp.broadcast_to(ends[2 * i : 2 * i + 1, cols], (8, LANES))
+                    best = jnp.minimum(best, row + table[8 * b - place - Z_FLOOR])
+                out[span, cols] = best
+
+    def slanted(accs, blocks, offset, skip, reach):
+        for j in blocks:
             tile = tiles_of(source, j)
             for r in range(8):
                 q = 8 * j + r
                 rows = [jnp.broadcast_to(t[r : r + 1, :], (8, LANES)) for t in tile]
                 for i, b in enumerate(blocks):
-                    if reach(b, q):
+                    if reach(b, q) and q != skip:
                         square = table[8 * b - q + offset - Z_FLOOR]
                         accs[i] = [jnp.minimum(v, row + square) for v, row in zip(accs[i], rows)]
         return accs
 
+    def far(offset, skip, reach, more):
+        source[skip : skip + 1, :] = jnp.full((1, zm_ref.shape[1]), HUGE, jnp.float32)
+        for first in (0, half):
+            blocks = range(first, first + half)
+            accs = slanted(load_blocks(acc_ref, blocks), blocks, offset, skip, reach)
+            if more(first):
+                read = functools.partial(tiles_of, source)
+                accs = sweep(accs, blocks, read, table, offset - 7 - Z_FLOOR, *more(first))
+            save_blocks(out, blocks, accs)
+
     @pl.when(valid & low)
     def _():
-        source[LANES - 1 : LANES, :] = ends[2:3]
-        for first in (0, half):
-            blocks = range(first, first + half)
-            accs = load_blocks(out, blocks)
-            accs = slanted(accs, blocks, LANES, blocks, lambda b, q: 8 * b < q)
-            if blocks[-1] + 1 < count:
-                read = functools.partial(tiles_of, source)
-                accs = sweep(accs, blocks, read, table, LANES - 7 - Z_FLOOR, blocks[-1] + 1, count)
-            save_blocks(out, blocks, accs)
+        ends = minima(own[0:2] + got[6:8], got[2:4] + own[4:6])
+        far(LANES, LANES - 1, lambda b, q: 8 * b < q, lambda first: None if first else (half, count))
+        add_ends(ends, out, (0, -1))
 
     @pl.when(valid & jnp.logical_not(low))
     def _():
-        source[0:1, :] = ends[2:3]
-        for first in (0, half):
-            blocks = range(first, first + half)
-            accs = load_blocks(out, blocks)
-            accs = slanted(accs, blocks, -LANES, blocks, lambda b, q: q < 8 * b + 7)
-            if first:
-                read = functools.partial(tiles_of, source)
-                accs = sweep(accs, blocks, read, table, -LANES - 7 - Z_FLOOR, 0, first)
-            save_blocks(out, blocks, accs)
+        ends = minima(own[2:4] + got[4:6], got[0:2] + own[6:8])
+        far(-LANES, 0, lambda b, q: q < 8 * b + 7, lambda first: (0, first) if first else None)
+        add_ends(ends, out, (LANES - 1, LANES))
+
+    @pl.when(jnp.logical_not(valid) & low)
+    def _():
+        add_ends(minima(own[0:2], own[0:2]), acc_ref, (0,))
+
+    @pl.when(jnp.logical_not(valid) & jnp.logical_not(low))
+    def _():
+        add_ends(minima(own[2:4], own[2:4]), acc_ref, (LANES - 1,))
 
     if not even:
         per = LANES // size_y
@@ -640,7 +650,7 @@
 def shards(features, conv_weight, mask):
     _, size_x, size_y, size_z = features.shape
     gx, gy = lax.axis_size("gx"), lax.axis_size("gy")
-    assert size_z == LANES and size_y % 16 == 0 and LANES % size_y == 0 and gy == 4
+    assert size_x == 4 and size_z == LANES and size_y % 16 == 0 and LANES % size_y == 0 and gy == 4
     brick = (size_x, size_y, LANES)
     lines = size_x * size_y
     partner = gx == 2

time: 24.4 us -> 24.3 us (level)
  no operation moved by 1% of the time
where the time goes in v6:
time: 24.3 us; the launch traced here: 24.1 us
  Pallas kernels  9.38 us (39%)
  starting transfers between devices  8.1 us (33%)
  waiting for transfers between devices  5.9 us (24%)
  between operations  0.71 us (3%)
    pallas_call x9, Pallas kernels, run(): pl.pallas_call(kernel, out_shape=shapes, in_specs=in_specs or [VMEM] * le...  9.38 us
    ppermute x5, starting transfers between devices, swap_xy(): return lax.ppermute(value, ('gx', 'gy'), pairs)  4.09 us
    ppermute x5, waiting for transfers between devices, swap_xy(): return lax.ppermute(value, ('gx', 'gy'), pairs)  3.13 us
    ppermute x2, starting transfers between devices, swap(): return lax.ppermute(value, axis, [(i, i ^ hop) for i in range(n)])  2.01 us
    ppermute x1, starting transfers between devices, z_swaps(): even = lax.ppermute(value, 'gz', [(i, i ^ 1) for i in range(n)])  1.36 us
    ppermute x1, waiting for transfers between devices, z_swaps(): even = lax.ppermute(value, 'gz', [(i, i ^ 1) for i in range(n)])  1.13 us
    ppermute x2, waiting for transfers between devices, swap(): return lax.ppermute(value, axis, [(i, i ^ hop) for i in range(n)])  0.65 us
    ppermute x1, starting transfers between devices, corner_swap(): return lax.ppermute(value, ('gx', 'gy'), pairs)  0.63 us
  transfers between devices with their start and end apart: 10, of which 5 were waited for; matrix products, arithmetic and copies ran while one was open for 0% of the time, Pallas kernels for 18%

profile of v6, /device:TPU:19, one launch (start us, length us, event | category | flops | bytes accessed | tf_op | source)
XLA Modules:
  0.0 24.1 jit_solution(2139728688688984508)
XLA Ops:
  0.6 2.4 %shard_map.50 = (f32[4,64,128]{2,1,0:T(8,128)S(1)}, f32[328,128]{1,0:T(8,128)S(1)}, f32[16,128]{1,0:T(8,128)S(1)}, f32[16,128]{1,0:T(8,128)S(1)}) custom-call(bf16[32,4,64,128]{3,2,1,0:T(8,128)(2,1)} %f_hbm.1, bf16[27,32]{1,0:T(8,128)(2,1)} %w_hbm.1, s32[4,64,128]{2,1,0:T(8,128)} %mask_hbm.1), custom_call_target="tpu_custom_call" | custom-call | tf_op jit(solution)/shard_map/pallas_call | solution.py:23
  3.0 0.3 %collective-permute-start = (f32[328,128]{1,0:T(8,128)S(1)}, f32[328,128]{1,0:T(8,128)S(1)}, u32[]{:S(2)}, u32[]{:S(2)}) collective-permute-start(f32[328,128]{1,0:T(8,128)S(1)} %get-tuple-element.20.own_ref), channel_id=1, source_target_pairs={{0,16},{4,20},{8,24},{12,28},{16,0},{20,4},{24,8},{28,12},{1,17},{... | collective-permute-start | bytes 503816 | tf_op jit(solution)/shard_map/ppermute | solution.py:544
  3.3 3.0 %collective-permute-start.2 = (f32[16,128]{1,0:T(8,128)S(1)}, f32[16,128]{1,0:T(8,128)S(1)}, u32[]{:S(2)}, u32[]{:S(2)}) collective-permute-start(f32[16,128]{1,0:T(8,128)S(1)} %get-tuple-element.21), channel_id=1, source_target_pairs={{0,28},{4,24},{8,20},{12,16},{16,12},{20,8},{24,4},{28,0},{1,29},{... | collective-permute-start | bytes 24584 | tf_op jit(solution)/shard_map/ppermute | solution.py:544
  6.3 0.0 collective-permute-start.1
  6.3 0.8 %collective-permute-start.4 = (f32[16,128]{1,0:T(8,128)S(1)}, f32[16,128]{1,0:T(8,128)S(1)}, u32[]{:S(2)}, u32[]{:S(2)}) collective-permute-start(f32[16,128]{1,0:T(8,128)S(1)} %get-tuple-element.22), channel_id=1, source_target_pairs={{0,20},{4,16},{8,28},{12,24},{16,4},{20,0},{24,12},{28,8},{1,21},{... | collective-permute-start | bytes 24584 | tf_op jit(solution)/shard_map/ppermute | solution.py:544
  7.1 0.0 collective-permute-start.3
  7.1 3.1 %collective-permute-done.2.xcross_ref = f32[16,128]{1,0:T(8,128)S(1)} collective-permute-done((f32[16,128]{1,0:T(8,128)S(1)}, f32[16,128]{1,0:T(8,128)S(1)}, u32[]{:S(2)}, u32[]{:S(2)}) %collective-permute-start.2) | collective-permute-done | bytes 8224 | tf_op jit(solution)/shard_map/ppermute | solution.py:544
  10.2 0.0 collective-permute-done.1.cross_ref
  10.2 0.0 collective-permute-done.4.xchip_ref
  10.2 0.0 collective-permute-done.3.chip_ref
  10.2 0.0 collective-permute-done.far_ref
  10.2 0.5 %shard_map.51 = (f32[4,64,128]{2,1,0:T(8,128)S(1)}, f32[136,256]{1,0:T(8,128)S(1)}, s32[72,256]{1,0:T(8,128)S(1)}) custom-call(f32[4,64,128]{2,1,0:T(8,128)S(1)} %get-tuple-element.19.s_ref, f32[328,128]{1,0:T(8,128)S(1)} %get-tuple-element.20.own_ref, f32[328,128]{1,0:T(8,128)S(1)} %collective-permute-done.far_ref, ...), custom_call_target="tpu_custom_call" | custom-call | tf_op jit(solution)/shard_map/pallas_call | solution.py:23
  10.7 1.4 %collective-permute-start.5 = (s32[72,256]{1,0:T(8,128)S(1)}, s32[72,256]{1,0:T(8,128)S(1)}, u32[]{:S(2)}, u32[]{:S(2)}) collective-permute-start(s32[72,256]{1,0:T(8,128)S(1)} %get-tuple-element.26), channel_id=1, source_target_pairs={{0,1},{1,0},{2,3},{3,2},{4,5},{5,4},{6,7},{7,6},{8,9},{9,8},{10,11... | collective-permute-start | bytes 221192 | tf_op jit(solution)/shard_map/ppermute | solution.py:560
  12.1 0.0 collective-permute-start.6
  12.1 1.6 %shard_map.52 = (f32[128,256]{1,0:T(8,128)S(1)}, f32[262,8,128]{2,1,0:T(8,128)S(1)}, f32[120,8,128]{2,1,0:T(8,128)S(1)}, f32[120,8,128]{2,1,0:T(8,128)S(1)}, f32...) custom-call(f32[136,256]{1,0:T(8,128)S(1)} %get-tuple-element.23.zm_ref), custom_call_target="tpu_custom_call" | custom-call | tf_op jit(solution)/shard_map/pallas_call | solution.py:23
  13.7 1.1 %collective-permute-done.5.got_ref.even_ref = s32[72,256]{1,0:T(8,128)S(1)} collective-permute-done((s32[72,256]{1,0:T(8,128)S(1)}, s32[72,256]{1,0:T(8,128)S(1)}, u32[]{:S(2)}, u32[]{:S(2)}) %collective-permute-start.5) | collective-permute-done | bytes 73760 | tf_op jit(solution)/shard_map/ppermute | solution.py:560
  14.8 0.7 %shard_map.53.acc_ref = f32[128,256]{1,0:T(8,128)S(1)} custom-call(f32[128,256]{1,0:T(8,128)S(1)} %get-tuple-element.24.acc_ref, f32[262,8,128]{2,1,0:T(8,128)S(1)} %get-tuple-element.25.table, f32[136,256]{1,0:T(8,128)S(1)} %get-tuple-element.23.zm_ref, s32[72,256]{1,0:T(8,128)S(1)} %collective-permute-done.5.got_ref.even_ref), custom_call_target="tpu_custom_call" | custom-call | tf_op jit(solution)/shard_map/pallas_call | solution.py:23
  15.5 0.4 %collective-permute-done.6.got_ref.odd_ref = s32[72,256]{1,0:T(8,128)S(1)} collective-permute-done((s32[72,256]{1,0:T(8,128)S(1)}, s32[72,256]{1,0:T(8,128)S(1)}, u32[]{:S(2)}, u32[]{:S(2)}) %collective-permute-start.6) | collective-permute-done | bytes 73760 | tf_op jit(solution)/shard_map/ppermute | solution.py:565
  15.9 0.8 %shard_map.54 = (f32[4,64,128]{2,1,0:T(8,128)S(1)}, s16[4,64,128]{2,1,0:T(8,128)(2,1)S(1)}) custom-call(f32[128,256]{1,0:T(8,128)S(1)} %shard_map.53.acc_ref, f32[262,8,128]{2,1,0:T(8,128)S(1)} %get-tuple-element.25.table, f32[136,256]{1,0:T(8,128)S(1)} %get-tuple-element.23.zm_ref, s32[72,256]{1,0:T(8,128)S(1)} %collective-permute-done.6.got_ref.odd_ref), custom_call_target="tpu_custom_call" | custom-call | tf_op jit(solution)/shard_map/pallas_call | solution.py:23
  16.7 0.9 %collective-permute-start.7 = (s16[4,64,128]{2,1,0:T(8,128)(2,1)S(1)}, s16[4,64,128]{2,1,0:T(8,128)(2,1)S(1)}, u32[]{:S(2)}, u32[]{:S(2)}) collective-permute-start(s16[4,64,128]{2,1,0:T(8,128)(2,1)S(1)} %get-tuple-element.28), channel_id=1, source_target_pairs={{0,4},{4,0},{8,12},{12,8},{1,5},{5,1},{9,13},{13,9},{2,6},{6,2},{1... | collective-permute-start | bytes 196616 | tf_op jit(solution)/shard_map/ppermute | solution.py:538
  17.7 1.1 %collective-permute-start.8 = (s16[4,64,128]{2,1,0:T(8,128)(2,1)S(1)}, s16[4,64,128]{2,1,0:T(8,128)(2,1)S(1)}, u32[]{:S(2)}, u32[]{:S(2)}) collective-permute-start(s16[4,64,128]{2,1,0:T(8,128)(2,1)S(1)} %get-tuple-element.28), channel_id=1, source_target_pairs={{0,8},{4,12},{8,0},{12,4},{1,9},{5,13},{9,1},{13,5},{2,10},{6,14},... | collective-permute-start | bytes 196616 | tf_op jit(solution)/shard_map/ppermute | solution.py:538
  18.8 0.6 %collective-permute-start.9 = (s16[4,64,128]{2,1,0:T(8,128)(2,1)S(1)}, s16[4,64,128]{2,1,0:T(8,128)(2,1)S(1)}, u32[]{:S(2)}, u32[]{:S(2)}) collective-permute-start(s16[4,64,128]{2,1,0:T(8,128)(2,1)S(1)} %get-tuple-element.28), channel_id=1, source_target_pairs={{0,16},{4,8},{8,4},{12,28},{16,0},{20,24},{24,20},{28,12},{1,17},{... | collective-permute-start | bytes 196616 | tf_op jit(solution)/shard_map/ppermute | solution.py:574
  19.4 0.0 collective-permute-done.7.code_ref
  19.4 1.3 %shard_map.55.start_ref = f32[4,64,128]{2,1,0:T(8,128)S(1)} custom-call(f32[4,64,128]{2,1,0:T(8,128)S(1)} %get-tuple-element.27.own_ref, s16[4,64,128]{2,1,0:T(8,128)(2,1)S(1)} %collective-permute-done.7.code_ref, f32[120,8,128]{2,1,0:T(8,128)S(1)} %get-tuple-element.29.table_0, f32[120,8,128]{2,1,0:T(8,128)S(1)} %get-tuple-element.30.table_1), custom_call_target="tpu_custom_call" | custom-call | tf_op jit(solution)/shard_map/pallas_call | solution.py:23
  20.7 0.6 %collective-permute-done.8.code_ref = s16[4,64,128]{2,1,0:T(8,128)(2,1)S(1)} collective-permute-done((s16[4,64,128]{2,1,0:T(8,128)(2,1)S(1)}, s16[4,64,128]{2,1,0:T(8,128)(2,1)S(1)}, u32[]{:S(2)}, u32[]{:S(2)}) %collective-permute-start.8) | collective-permute-done | bytes 65568 | tf_op jit(solution)/shard_map/ppermute | solution.py:538
  21.4 0.7 %shard_map.56._.start_ref = f32[4,64,128]{2,1,0:T(8,128)S(1)} custom-call(f32[4,64,128]{2,1,0:T(8,128)S(1)} %shard_map.55.start_ref, s16[4,64,128]{2,1,0:T(8,128)(2,1)S(1)} %collective-permute-done.8.code_ref, f32[120,8,128]{2,1,0:T(8,128)S(1)} %get-tuple-element.31.table), custom_call_target="tpu_custom_call" | custom-call | tf_op jit(solution)/shard_map/pallas_call | solution.py:23
  22.0 0.1 shard_map.57.score_ref
  22.2 0.6 %collective-permute-done.9.code_ref = s16[4,64,128]{2,1,0:T(8,128)(2,1)S(1)} collective-permute-done((s16[4,64,128]{2,1,0:T(8,128)(2,1)S(1)}, s16[4,64,128]{2,1,0:T(8,128)(2,1)S(1)}, u32[]{:S(2)}, u32[]{:S(2)}) %collective-permute-start.9) | collective-permute-done | bytes 65568 | tf_op jit(solution)/shard_map/ppermute | solution.py:574
  22.7 1.3 %shard_map.58 = (f32[4,64,128]{2,1,0:T(8,128)}, f32[4,64,128]{2,1,0:T(8,128)}) custom-call(f32[4,64,128]{2,1,0:T(8,128)S(1)} %shard_map.56._.start_ref, s16[4,64,128]{2,1,0:T(8,128)(2,1)S(1)} %collective-permute-done.9.code_ref, f32[120,8,128]{2,1,0:T(8,128)S(1)} %get-tuple-element.32.table, f32[4,64,128]{2,1,0:T(8,128)S(1)} %shard_map.57.score_ref), custom_call_target="tpu_custom_call" | custom-call | tf_op jit(solution)/shard_map/pallas_call | solution.py:23
Async XLA Ops:
  3.0 7.2 %collective-permute-start = (f32[328,128]{1,0:T(8,128)S(1)}, f32[328,128]{1,0:T(8,128)S(1)}, u32[]{:S(2)}, u32[]{:S(2)}) collective-permute-start(f32[328,128]{1,0:T(8,128)S(1)} %get-tuple-element.20.own_ref), channel_id=1, source_target_pairs={{0,16},{4,20},{8,24},{12,28},{16,0},{20,4},{24,8},{28,12},{1,17},{... | collective-permute-start | bytes 503816 | tf_op jit(solution)/shard_map/ppermute | solution.py:544
  3.3 6.9 %collective-permute-start.2 = (f32[16,128]{1,0:T(8,128)S(1)}, f32[16,128]{1,0:T(8,128)S(1)}, u32[]{:S(2)}, u32[]{:S(2)}) collective-permute-start(f32[16,128]{1,0:T(8,128)S(1)} %get-tuple-element.21), channel_id=1, source_target_pairs={{0,28},{4,24},{8,20},{12,16},{16,12},{20,8},{24,4},{28,0},{1,29},{... | collective-permute-start | bytes 24584 | tf_op jit(solution)/shard_map/ppermute | solution.py:544
  6.3 3.9 %collective-permute-start.1 = (f32[16,128]{1,0:T(8,128)S(1)}, f32[16,128]{1,0:T(8,128)S(1)}, u32[]{:S(2)}, u32[]{:S(2)}) collective-permute-start(f32[16,128]{1,0:T(8,128)S(1)} %get-tuple-element.21), channel_id=1, source_target_pairs={{0,12},{4,8},{8,4},{12,0},{16,28},{20,24},{24,20},{28,16},{1,13},{... | collective-permute-start | bytes 24584 | tf_op jit(solution)/shard_map/ppermute | solution.py:544
  6.3 3.9 %collective-permute-start.4 = (f32[16,128]{1,0:T(8,128)S(1)}, f32[16,128]{1,0:T(8,128)S(1)}, u32[]{:S(2)}, u32[]{:S(2)}) collective-permute-start(f32[16,128]{1,0:T(8,128)S(1)} %get-tuple-element.22), channel_id=1, source_target_pairs={{0,20},{4,16},{8,28},{12,24},{16,4},{20,0},{24,12},{28,8},{1,21},{... | collective-permute-start | bytes 24584 | tf_op jit(solution)/shard_map/ppermute | solution.py:544
  7.1 3.1 %collective-permute-start.3 = (f32[16,128]{1,0:T(8,128)S(1)}, f32[16,128]{1,0:T(8,128)S(1)}, u32[]{:S(2)}, u32[]{:S(2)}) collective-permute-start(f32[16,128]{1,0:T(8,128)S(1)} %get-tuple-element.22), channel_id=1, source_target_pairs={{0,4},{4,0},{8,12},{12,8},{16,20},{20,16},{24,28},{28,24},{1,5},{5... | collective-permute-start | bytes 24584 | tf_op jit(solution)/shard_map/ppermute | solution.py:544
  10.7 4.1 %collective-permute-start.5 = (s32[72,256]{1,0:T(8,128)S(1)}, s32[72,256]{1,0:T(8,128)S(1)}, u32[]{:S(2)}, u32[]{:S(2)}) collective-permute-start(s32[72,256]{1,0:T(8,128)S(1)} %get-tuple-element.26), channel_id=1, source_target_pairs={{0,1},{1,0},{2,3},{3,2},{4,5},{5,4},{6,7},{7,6},{8,9},{9,8},{10,11... | collective-permute-start | bytes 221192 | tf_op jit(solution)/shard_map/ppermute | solution.py:560
  12.1 3.8 %collective-permute-start.6 = (s32[72,256]{1,0:T(8,128)S(1)}, s32[72,256]{1,0:T(8,128)S(1)}, u32[]{:S(2)}, u32[]{:S(2)}) collective-permute-start(s32[72,256]{1,0:T(8,128)S(1)} %get-tuple-element.26), channel_id=1, source_target_pairs={{0,4},{1,2},{2,1},{3,7},{4,0},{5,6},{6,5},{7,3},{8,12},{9,10},{10,... | collective-permute-start | bytes 221192 | tf_op jit(solution)/shard_map/ppermute | solution.py:565
  16.7 2.7 %collective-permute-start.7 = (s16[4,64,128]{2,1,0:T(8,128)(2,1)S(1)}, s16[4,64,128]{2,1,0:T(8,128)(2,1)S(1)}, u32[]{:S(2)}, u32[]{:S(2)}) collective-permute-start(s16[4,64,128]{2,1,0:T(8,128)(2,1)S(1)} %get-tuple-element.28), channel_id=1, source_target_pairs={{0,4},{4,0},{8,12},{12,8},{1,5},{5,1},{9,13},{13,9},{2,6},{6,2},{1... | collective-permute-start | bytes 196616 | tf_op jit(solution)/shard_map/ppermute | solution.py:538
  17.7 3.7 %collective-permute-start.8 = (s16[4,64,128]{2,1,0:T(8,128)(2,1)S(1)}, s16[4,64,128]{2,1,0:T(8,128)(2,1)S(1)}, u32[]{:S(2)}, u32[]{:S(2)}) collective-permute-start(s16[4,64,128]{2,1,0:T(8,128)(2,1)S(1)} %get-tuple-element.28), channel_id=1, source_target_pairs={{0,8},{4,12},{8,0},{12,4},{1,9},{5,13},{9,1},{13,5},{2,10},{6,14},... | collective-permute-start | bytes 196616 | tf_op jit(solution)/shard_map/ppermute | solution.py:538
  18.8 4.0 %collective-permute-start.9 = (s16[4,64,128]{2,1,0:T(8,128)(2,1)S(1)}, s16[4,64,128]{2,1,0:T(8,128)(2,1)S(1)}, u32[]{:S(2)}, u32[]{:S(2)}) collective-permute-start(s16[4,64,128]{2,1,0:T(8,128)(2,1)S(1)} %get-tuple-element.28), channel_id=1, source_target_pairs={{0,16},{4,8},{8,4},{12,28},{16,0},{20,24},{24,20},{28,12},{1,17},{... | collective-permute-start | bytes 196616 | tf_op jit(solution)/shard_map/ppermute | solution.py:574

commit v7 on v6

--- a/solution.py
+++ b/solution.py
@@ -332,10 +332,8 @@
         table[d - (1 - size_y)] = v * v
 
 
-def z_own_kernel(size_y, zm_ref, out_ref, table, *y_tables):
+def z_own_kernel(zm_ref, out_ref, table):
     count, half = LANES // 8, LANES // 16
-    for hop, y_one in enumerate(y_tables):
-        y_table("gy", hop, size_y, y_one)
     s = row_of((8, LANES)).astype(jnp.float32)
     for d in range(Z_FLOOR, LANES):
         v = s + float(d)
@@ -494,7 +492,9 @@
                 out_ref[x, 8 * b : 8 * b + 8, :] = v if scale == 1.0 else v * scale
 
 
-def y_near_kernel(own_ref, code_ref, table_0, table_1, out_ref, block):
+def y_near_kernel(own_ref, code_ref, out_ref, table_2, table_3, block, table_0, table_1):
+    for hop, table in enumerate((table_0, table_1, table_2, table_3)):
+        y_table("gy", hop, own_ref.shape[1], table)
     block[...] = decode(code_ref[...])
     y_sweep((own_ref, block), (table_0, table_1), None, out_ref, 1.0)
 
@@ -660,8 +660,7 @@
 
     even, odd = z_swaps(words)
     tables = (2 * size_y - 8, 8, LANES)
-    own = functools.partial(z_own_kernel, size_y)
-    best, table, *kept = call(own, [(LANES, lines), (LANES - Z_FLOOR, 8, LANES)] + [tables] * 4)(zm)
+    best, table = call(z_own_kernel, [(LANES, lines), (LANES - Z_FLOOR, 8, LANES)])(zm)
     work = [pltpu.VMEM((LANES, lines), jnp.float32)] * 2
     coded = jax.ShapeDtypeStruct(brick, jnp.int16)
     for first, got, shapes in ((True, even, [(LANES, lines)]), (False, odd, [brick, coded])):
@@ -674,11 +673,12 @@
     code = code[0]
     chip, across, corner = swap(code, "gy", 1), swap(code, "gy", 2), corner_swap(code)
     block = [pltpu.VMEM(brick, jnp.float32)]
-    (near,) = call(y_near_kernel, [brick], block)(best, chip, kept[0], kept[1])
-    (near,) = call(y_across_kernel, [brick], block)(near, across, kept[2])
+    scratch = [*block, *[pltpu.VMEM(tables, jnp.float32)] * 2]
+    near, table_2, table_3 = call(y_near_kernel, [brick, tables, tables], scratch)(best, chip)
+    (near,) = call(y_across_kernel, [brick], block)(near, across, table_2)
     (score,) = call(score_kernel, [brick])(score, even, odd, near)
     last = [*block, *block, pltpu.SemaphoreType.DMA((3,))]
-    depth, score = call(y_last_kernel, [brick, brick], last, out_spec=HBM)(near, corner, kept[3], score)
+    depth, score = call(y_last_kernel, [brick, brick], last, out_spec=HBM)(near, corner, table_3, score)
     return score, depth
 
 

time: 24.3 us -> 24.3 us (level)
  no operation moved by 1% of the time
where the time goes in v7:
time: 24.3 us; the launch traced here: 24.1 us
  Pallas kernels  9.42 us (39%)
  starting transfers between devices  8.1 us (33%)
  waiting for transfers between devices  5.88 us (24%)
  between operations  0.7 us (3%)
    pallas_call x9, Pallas kernels, run(): pl.pallas_call(kernel, out_shape=shapes, in_specs=in_specs or [VMEM] * le...  9.42 us
    ppermute x5, starting transfers between devices, swap_xy(): return lax.ppermute(value, ('gx', 'gy'), pairs)  4.09 us
    ppermute x5, waiting for transfers between devices, swap_xy(): return lax.ppermute(value, ('gx', 'gy'), pairs)  3.13 us
    ppermute x2, starting transfers between devices, swap(): return lax.ppermute(value, axis, [(i, i ^ hop) for i in range(n)])  2.01 us
    ppermute x1, starting transfers between devices, z_swaps(): even = lax.ppermute(value, 'gz', [(i, i ^ 1) for i in range(n)])  1.36 us
    ppermute x1, waiting for transfers between devices, z_swaps(): even = lax.ppermute(value, 'gz', [(i, i ^ 1) for i in range(n)])  1.26 us
    ppermute x1, starting transfers between devices, corner_swap(): return lax.ppermute(value, ('gx', 'gy'), pairs)  0.63 us
    ppermute x1, waiting for transfers between devices, corner_swap(): return lax.ppermute(value, ('gx', 'gy'), pairs)  0.59 us
  transfers between devices with their start and end apart: 10, of which 5 were waited for; matrix products, arithmetic and copies ran while one was open for 0% of the time, Pallas kernels for 18%

profile of v7, /device:TPU:19, one launch (start us, length us, event | category | flops | bytes accessed | tf_op | source)
XLA Modules:
  0.0 24.1 jit_solution(5678043123561345326)
XLA Ops:
  0.6 2.4 %shard_map.50 = (f32[4,64,128]{2,1,0:T(8,128)S(1)}, f32[328,128]{1,0:T(8,128)S(1)}, f32[16,128]{1,0:T(8,128)S(1)}, f32[16,128]{1,0:T(8,128)S(1)}) custom-call(bf16[32,4,64,128]{3,2,1,0:T(8,128)(2,1)} %f_hbm.1, bf16[27,32]{1,0:T(8,128)(2,1)} %w_hbm.1, s32[4,64,128]{2,1,0:T(8,128)} %mask_hbm.1), custom_call_target="tpu_custom_call" | custom-call | tf_op jit(solution)/shard_map/pallas_call | solution.py:23
  3.0 0.3 %collective-permute-start = (f32[328,128]{1,0:T(8,128)S(1)}, f32[328,128]{1,0:T(8,128)S(1)}, u32[]{:S(2)}, u32[]{:S(2)}) collective-permute-start(f32[328,128]{1,0:T(8,128)S(1)} %get-tuple-element.19.own_ref), channel_id=1, source_target_pairs={{0,16},{4,20},{8,24},{12,28},{16,0},{20,4},{24,8},{28,12},{1,17},{... | collective-permute-start | bytes 503816 | tf_op jit(solution)/shard_map/ppermute | solution.py:544
  3.3 3.0 %collective-permute-start.2 = (f32[16,128]{1,0:T(8,128)S(1)}, f32[16,128]{1,0:T(8,128)S(1)}, u32[]{:S(2)}, u32[]{:S(2)}) collective-permute-start(f32[16,128]{1,0:T(8,128)S(1)} %get-tuple-element.20), channel_id=1, source_target_pairs={{0,28},{4,24},{8,20},{12,16},{16,12},{20,8},{24,4},{28,0},{1,29},{... | collective-permute-start | bytes 24584 | tf_op jit(solution)/shard_map/ppermute | solution.py:544
  6.3 0.0 collective-permute-start.1
  6.3 0.8 %collective-permute-start.4 = (f32[16,128]{1,0:T(8,128)S(1)}, f32[16,128]{1,0:T(8,128)S(1)}, u32[]{:S(2)}, u32[]{:S(2)}) collective-permute-start(f32[16,128]{1,0:T(8,128)S(1)} %get-tuple-element.21), channel_id=1, source_target_pairs={{0,20},{4,16},{8,28},{12,24},{16,4},{20,0},{24,12},{28,8},{1,21},{... | collective-permute-start | bytes 24584 | tf_op jit(solution)/shard_map/ppermute | solution.py:544
  7.1 0.0 collective-permute-start.3
  7.1 3.1 %collective-permute-done.2.xcross_ref = f32[16,128]{1,0:T(8,128)S(1)} collective-permute-done((f32[16,128]{1,0:T(8,128)S(1)}, f32[16,128]{1,0:T(8,128)S(1)}, u32[]{:S(2)}, u32[]{:S(2)}) %collective-permute-start.2) | collective-permute-done | bytes 8224 | tf_op jit(solution)/shard_map/ppermute | solution.py:544
  10.2 0.0 collective-permute-done.1.cross_ref
  10.2 0.0 collective-permute-done.4.xchip_ref
  10.2 0.0 collective-permute-done.3.chip_ref
  10.2 0.0 collective-permute-done.far_ref
  10.2 0.5 %shard_map.51 = (f32[4,64,128]{2,1,0:T(8,128)S(1)}, f32[136,256]{1,0:T(8,128)S(1)}, s32[72,256]{1,0:T(8,128)S(1)}) custom-call(f32[4,64,128]{2,1,0:T(8,128)S(1)} %get-tuple-element.18.s_ref, f32[328,128]{1,0:T(8,128)S(1)} %get-tuple-element.19.own_ref, f32[328,128]{1,0:T(8,128)S(1)} %collective-permute-done.far_ref, ...), custom_call_target="tpu_custom_call" | custom-call | tf_op jit(solution)/shard_map/pallas_call | solution.py:23
  10.7 1.4 %collective-permute-start.5 = (s32[72,256]{1,0:T(8,128)S(1)}, s32[72,256]{1,0:T(8,128)S(1)}, u32[]{:S(2)}, u32[]{:S(2)}) collective-permute-start(s32[72,256]{1,0:T(8,128)S(1)} %get-tuple-element.25), channel_id=1, source_target_pairs={{0,1},{1,0},{2,3},{3,2},{4,5},{5,4},{6,7},{7,6},{8,9},{9,8},{10,11... | collective-permute-start | bytes 221192 | tf_op jit(solution)/shard_map/ppermute | solution.py:560
  12.1 0.0 collective-permute-start.6
  12.1 1.4 %shard_map.52 = (f32[128,256]{1,0:T(8,128)S(1)}, f32[262,8,128]{2,1,0:T(8,128)S(1)}) custom-call(f32[136,256]{1,0:T(8,128)S(1)} %get-tuple-element.22.zm_ref), custom_call_target="tpu_custom_call" | custom-call | tf_op jit(solution)/shard_map/pallas_call | solution.py:23
  13.5 1.3 %collective-permute-done.5.got_ref.even_ref = s32[72,256]{1,0:T(8,128)S(1)} collective-permute-done((s32[72,256]{1,0:T(8,128)S(1)}, s32[72,256]{1,0:T(8,128)S(1)}, u32[]{:S(2)}, u32[]{:S(2)}) %collective-permute-start.5) | collective-permute-done | bytes 73760 | tf_op jit(solution)/shard_map/ppermute | solution.py:560
  14.8 0.7 %shard_map.53.acc_ref = f32[128,256]{1,0:T(8,128)S(1)} custom-call(f32[128,256]{1,0:T(8,128)S(1)} %get-tuple-element.23.acc_ref, f32[262,8,128]{2,1,0:T(8,128)S(1)} %get-tuple-element.24.table, f32[136,256]{1,0:T(8,128)S(1)} %get-tuple-element.22.zm_ref, s32[72,256]{1,0:T(8,128)S(1)} %collective-permute-done.5.got_ref.even_ref), custom_call_target="tpu_custom_call" | custom-call | tf_op jit(solution)/shard_map/pallas_call | solution.py:23
  15.5 0.4 %collective-permute-done.6.got_ref.odd_ref = s32[72,256]{1,0:T(8,128)S(1)} collective-permute-done((s32[72,256]{1,0:T(8,128)S(1)}, s32[72,256]{1,0:T(8,128)S(1)}, u32[]{:S(2)}, u32[]{:S(2)}) %collective-permute-start.6) | collective-permute-done | bytes 73760 | tf_op jit(solution)/shard_map/ppermute | solution.py:565
  15.9 0.8 %shard_map.54 = (f32[4,64,128]{2,1,0:T(8,128)S(1)}, s16[4,64,128]{2,1,0:T(8,128)(2,1)S(1)}) custom-call(f32[128,256]{1,0:T(8,128)S(1)} %shard_map.53.acc_ref, f32[262,8,128]{2,1,0:T(8,128)S(1)} %get-tuple-element.24.table, f32[136,256]{1,0:T(8,128)S(1)} %get-tuple-element.22.zm_ref, s32[72,256]{1,0:T(8,128)S(1)} %collective-permute-done.6.got_ref.odd_ref), custom_call_target="tpu_custom_call" | custom-call | tf_op jit(solution)/shard_map/pallas_call | solution.py:23
  16.8 0.9 %collective-permute-start.7 = (s16[4,64,128]{2,1,0:T(8,128)(2,1)S(1)}, s16[4,64,128]{2,1,0:T(8,128)(2,1)S(1)}, u32[]{:S(2)}, u32[]{:S(2)}) collective-permute-start(s16[4,64,128]{2,1,0:T(8,128)(2,1)S(1)} %get-tuple-element.27), channel_id=1, source_target_pairs={{0,4},{4,0},{8,12},{12,8},{1,5},{5,1},{9,13},{13,9},{2,6},{6,2},{1... | collective-permute-start | bytes 196616 | tf_op jit(solution)/shard_map/ppermute | solution.py:538
  17.7 1.1 %collective-permute-start.8 = (s16[4,64,128]{2,1,0:T(8,128)(2,1)S(1)}, s16[4,64,128]{2,1,0:T(8,128)(2,1)S(1)}, u32[]{:S(2)}, u32[]{:S(2)}) collective-permute-start(s16[4,64,128]{2,1,0:T(8,128)(2,1)S(1)} %get-tuple-element.27), channel_id=1, source_target_pairs={{0,8},{4,12},{8,0},{12,4},{1,9},{5,13},{9,1},{13,5},{2,10},{6,14},... | collective-permute-start | bytes 196616 | tf_op jit(solution)/shard_map/ppermute | solution.py:538
  18.8 0.6 %collective-permute-start.9 = (s16[4,64,128]{2,1,0:T(8,128)(2,1)S(1)}, s16[4,64,128]{2,1,0:T(8,128)(2,1)S(1)}, u32[]{:S(2)}, u32[]{:S(2)}) collective-permute-start(s16[4,64,128]{2,1,0:T(8,128)(2,1)S(1)} %get-tuple-element.27), channel_id=1, source_target_pairs={{0,16},{4,8},{8,4},{12,28},{16,0},{20,24},{24,20},{28,12},{1,17},{... | collective-permute-start | bytes 196616 | tf_op jit(solution)/shard_map/ppermute | solution.py:574
  19.4 0.0 collective-permute-done.7.code_ref
  19.4 1.4 %shard_map.55 = (f32[4,64,128]{2,1,0:T(8,128)S(1)}, f32[120,8,128]{2,1,0:T(8,128)S(1)}, f32[120,8,128]{2,1,0:T(8,128)S(1)}) custom-call(f32[4,64,128]{2,1,0:T(8,128)S(1)} %get-tuple-element.26.own_ref, s16[4,64,128]{2,1,0:T(8,128)(2,1)S(1)} %collective-permute-done.7.code_ref), custom_call_target="tpu_custom_call" | custom-call | tf_op jit(solution)/shard_map/pallas_call | solution.py:23
  20.9 0.5 %collective-permute-done.8.code_ref = s16[4,64,128]{2,1,0:T(8,128)(2,1)S(1)} collective-permute-done((s16[4,64,128]{2,1,0:T(8,128)(2,1)S(1)}, s16[4,64,128]{2,1,0:T(8,128)(2,1)S(1)}, u32[]{:S(2)}, u32[]{:S(2)}) %collective-permute-start.8) | collective-permute-done | bytes 65568 | tf_op jit(solution)/shard_map/ppermute | solution.py:538
  21.4 0.7 %shard_map.56._.start_ref = f32[4,64,128]{2,1,0:T(8,128)S(1)} custom-call(f32[4,64,128]{2,1,0:T(8,128)S(1)} %get-tuple-element.28.start_ref, s16[4,64,128]{2,1,0:T(8,128)(2,1)S(1)} %collective-permute-done.8.code_ref, f32[120,8,128]{2,1,0:T(8,128)S(1)} %get-tuple-element.29.table), custom_call_target="tpu_custom_call" | custom-call | tf_op jit(solution)/shard_map/pallas_call | solution.py:23
  22.0 0.1 shard_map.57.score_ref
  22.2 0.6 %collective-permute-done.9.code_ref = s16[4,64,128]{2,1,0:T(8,128)(2,1)S(1)} collective-permute-done((s16[4,64,128]{2,1,0:T(8,128)(2,1)S(1)}, s16[4,64,128]{2,1,0:T(8,128)(2,1)S(1)}, u32[]{:S(2)}, u32[]{:S(2)}) %collective-permute-start.9) | collective-permute-done | bytes 65568 | tf_op jit(solution)/shard_map/ppermute | solution.py:574
  22.8 1.3 %shard_map.58 = (f32[4,64,128]{2,1,0:T(8,128)}, f32[4,64,128]{2,1,0:T(8,128)}) custom-call(f32[4,64,128]{2,1,0:T(8,128)S(1)} %shard_map.56._.start_ref, s16[4,64,128]{2,1,0:T(8,128)(2,1)S(1)} %collective-permute-done.9.code_ref, f32[120,8,128]{2,1,0:T(8,128)S(1)} %get-tuple-element.30.table, f32[4,64,128]{2,1,0:T(8,128)S(1)} %shard_map.57.score_ref), custom_call_target="tpu_custom_call" | custom-call | tf_op jit(solution)/shard_map/pallas_call | solution.py:23
Async XLA Ops:
  3.0 7.2 %collective-permute-start = (f32[328,128]{1,0:T(8,128)S(1)}, f32[328,128]{1,0:T(8,128)S(1)}, u32[]{:S(2)}, u32[]{:S(2)}) collective-permute-start(f32[328,128]{1,0:T(8,128)S(1)} %get-tuple-element.19.own_ref), channel_id=1, source_target_pairs={{0,16},{4,20},{8,24},{12,28},{16,0},{20,4},{24,8},{28,12},{1,17},{... | collective-permute-start | bytes 503816 | tf_op jit(solution)/shard_map/ppermute | solution.py:544
  3.3 6.9 %collective-permute-start.2 = (f32[16,128]{1,0:T(8,128)S(1)}, f32[16,128]{1,0:T(8,128)S(1)}, u32[]{:S(2)}, u32[]{:S(2)}) collective-permute-start(f32[16,128]{1,0:T(8,128)S(1)} %get-tuple-element.20), channel_id=1, source_target_pairs={{0,28},{4,24},{8,20},{12,16},{16,12},{20,8},{24,4},{28,0},{1,29},{... | collective-permute-start | bytes 24584 | tf_op jit(solution)/shard_map/ppermute | solution.py:544
  6.3 3.9 %collective-permute-start.1 = (f32[16,128]{1,0:T(8,128)S(1)}, f32[16,128]{1,0:T(8,128)S(1)}, u32[]{:S(2)}, u32[]{:S(2)}) collective-permute-start(f32[16,128]{1,0:T(8,128)S(1)} %get-tuple-element.20), channel_id=1, source_target_pairs={{0,12},{4,8},{8,4},{12,0},{16,28},{20,24},{24,20},{28,16},{1,13},{... | collective-permute-start | bytes 24584 | tf_op jit(solution)/shard_map/ppermute | solution.py:544
  6.3 3.9 %collective-permute-start.4 = (f32[16,128]{1,0:T(8,128)S(1)}, f32[16,128]{1,0:T(8,128)S(1)}, u32[]{:S(2)}, u32[]{:S(2)}) collective-permute-start(f32[16,128]{1,0:T(8,128)S(1)} %get-tuple-element.21), channel_id=1, source_target_pairs={{0,20},{4,16},{8,28},{12,24},{16,4},{20,0},{24,12},{28,8},{1,21},{... | collective-permute-start | bytes 24584 | tf_op jit(solution)/shard_map/ppermute | solution.py:544
  7.1 3.1 %collective-permute-start.3 = (f32[16,128]{1,0:T(8,128)S(1)}, f32[16,128]{1,0:T(8,128)S(1)}, u32[]{:S(2)}, u32[]{:S(2)}) collective-permute-start(f32[16,128]{1,0:T(8,128)S(1)} %get-tuple-element.21), channel_id=1, source_target_pairs={{0,4},{4,0},{8,12},{12,8},{16,20},{20,16},{24,28},{28,24},{1,5},{5... | collective-permute-start | bytes 24584 | tf_op jit(solution)/shard_map/ppermute | solution.py:544
  10.7 4.1 %collective-permute-start.5 = (s32[72,256]{1,0:T(8,128)S(1)}, s32[72,256]{1,0:T(8,128)S(1)}, u32[]{:S(2)}, u32[]{:S(2)}) collective-permute-start(s32[72,256]{1,0:T(8,128)S(1)} %get-tuple-element.25), channel_id=1, source_target_pairs={{0,1},{1,0},{2,3},{3,2},{4,5},{5,4},{6,7},{7,6},{8,9},{9,8},{10,11... | collective-permute-start | bytes 221192 | tf_op jit(solution)/shard_map/ppermute | solution.py:560
  12.1 3.8 %collective-permute-start.6 = (s32[72,256]{1,0:T(8,128)S(1)}, s32[72,256]{1,0:T(8,128)S(1)}, u32[]{:S(2)}, u32[]{:S(2)}) collective-permute-start(s32[72,256]{1,0:T(8,128)S(1)} %get-tuple-element.25), channel_id=1, source_target_pairs={{0,4},{1,2},{2,1},{3,7},{4,0},{5,6},{6,5},{7,3},{8,12},{9,10},{10,... | collective-permute-start | bytes 221192 | tf_op jit(solution)/shard_map/ppermute | solution.py:565
  16.8 2.7 %collective-permute-start.7 = (s16[4,64,128]{2,1,0:T(8,128)(2,1)S(1)}, s16[4,64,128]{2,1,0:T(8,128)(2,1)S(1)}, u32[]{:S(2)}, u32[]{:S(2)}) collective-permute-start(s16[4,64,128]{2,1,0:T(8,128)(2,1)S(1)} %get-tuple-element.27), channel_id=1, source_target_pairs={{0,4},{4,0},{8,12},{12,8},{1,5},{5,1},{9,13},{13,9},{2,6},{6,2},{1... | collective-permute-start | bytes 196616 | tf_op jit(solution)/shard_map/ppermute | solution.py:538
  17.7 3.7 %collective-permute-start.8 = (s16[4,64,128]{2,1,0:T(8,128)(2,1)S(1)}, s16[4,64,128]{2,1,0:T(8,128)(2,1)S(1)}, u32[]{:S(2)}, u32[]{:S(2)}) collective-permute-start(s16[4,64,128]{2,1,0:T(8,128)(2,1)S(1)} %get-tuple-element.27), channel_id=1, source_target_pairs={{0,8},{4,12},{8,0},{12,4},{1,9},{5,13},{9,1},{13,5},{2,10},{6,14},... | collective-permute-start | bytes 196616 | tf_op jit(solution)/shard_map/ppermute | solution.py:538
  18.8 4.0 %collective-permute-start.9 = (s16[4,64,128]{2,1,0:T(8,128)(2,1)S(1)}, s16[4,64,128]{2,1,0:T(8,128)(2,1)S(1)}, u32[]{:S(2)}, u32[]{:S(2)}) collective-permute-start(s16[4,64,128]{2,1,0:T(8,128)(2,1)S(1)} %get-tuple-element.27), channel_id=1, source_target_pairs={{0,16},{4,8},{8,4},{12,28},{16,0},{20,24},{24,20},{28,12},{1,17},{... | collective-permute-start | bytes 196616 | tf_op jit(solution)/shard_map/ppermute | solution.py:574

commit v8 on v6

--- a/solution.py
+++ b/solution.py
@@ -163,13 +163,13 @@
 
 
 def encode(value):
-    code = jnp.round(jnp.log(value + 1.0) * (CODES / LN2)) - 32768.0
-    return jnp.clip(code, -32768.0, 32767.0).astype(jnp.int32)
+    code = jnp.round(jnp.log(value + 1.0) * (CODES / LN2) - 32768.0)
+    return jnp.minimum(code, 32767.0).astype(jnp.int32)
 
 
 def decode(code):
-    level = code.astype(jnp.int32).astype(jnp.float32) + 32768.0
-    return jnp.exp(level * (LN2 / CODES)) - 1.0
+    level = code.astype(jnp.int32).astype(jnp.float32)
+    return jnp.exp(level * (LN2 / CODES) + 32768.0 * (LN2 / CODES)) - 1.0
 
 
 def pack_z(rows, ends):

time: 24.3 us -> 24.3 us (level)
  no operation moved by 1% of the time
where the time goes in v8:
time: 24.3 us; the launch traced here: 24.1 us
  Pallas kernels  9.38 us (39%)
  starting transfers between devices  8.1 us (33%)
  waiting for transfers between devices  5.89 us (24%)
  between operations  0.7 us (3%)
    pallas_call x9, Pallas kernels, run(): pl.pallas_call(kernel, out_shape=shapes, in_specs=in_specs or [VMEM] * le...  9.38 us
    ppermute x5, starting transfers between devices, swap_xy(): return lax.ppermute(value, ('gx', 'gy'), pairs)  4.09 us
    ppermute x5, waiting for transfers between devices, swap_xy(): return lax.ppermute(value, ('gx', 'gy'), pairs)  3.13 us
    ppermute x2, starting transfers between devices, swap(): return lax.ppermute(value, axis, [(i, i ^ hop) for i in range(n)])  2.01 us
    ppermute x1, starting transfers between devices, z_swaps(): even = lax.ppermute(value, 'gz', [(i, i ^ 1) for i in range(n)])  1.36 us
    ppermute x1, waiting for transfers between devices, z_swaps(): even = lax.ppermute(value, 'gz', [(i, i ^ 1) for i in range(n)])  1.13 us
    ppermute x2, waiting for transfers between devices, swap(): return lax.ppermute(value, axis, [(i, i ^ hop) for i in range(n)])  0.64 us
    ppermute x1, starting transfers between devices, corner_swap(): return lax.ppermute(value, ('gx', 'gy'), pairs)  0.63 us
  transfers between devices with their start and end apart: 10, of which 5 were waited for; matrix products, arithmetic and copies ran while one was open for 0% of the time, Pallas kernels for 18%

profile of v8, /device:TPU:19, one launch (start us, length us, event | category | flops | bytes accessed | tf_op | source)
XLA Modules:
  0.0 24.1 jit_solution(17972681942261050298)
XLA Ops:
  0.6 2.4 %shard_map.50 = (f32[4,64,128]{2,1,0:T(8,128)S(1)}, f32[328,128]{1,0:T(8,128)S(1)}, f32[16,128]{1,0:T(8,128)S(1)}, f32[16,128]{1,0:T(8,128)S(1)}) custom-call(bf16[32,4,64,128]{3,2,1,0:T(8,128)(2,1)} %f_hbm.1, bf16[27,32]{1,0:T(8,128)(2,1)} %w_hbm.1, s32[4,64,128]{2,1,0:T(8,128)} %mask_hbm.1), custom_call_target="tpu_custom_call" | custom-call | tf_op jit(solution)/shard_map/pallas_call | solution.py:23
  3.0 0.3 %collective-permute-start = (f32[328,128]{1,0:T(8,128)S(1)}, f32[328,128]{1,0:T(8,128)S(1)}, u32[]{:S(2)}, u32[]{:S(2)}) collective-permute-start(f32[328,128]{1,0:T(8,128)S(1)} %get-tuple-element.20.own_ref), channel_id=1, source_target_pairs={{0,16},{4,20},{8,24},{12,28},{16,0},{20,4},{24,8},{28,12},{1,17},{... | collective-permute-start | bytes 503816 | tf_op jit(solution)/shard_map/ppermute | solution.py:544
  3.3 3.0 %collective-permute-start.2 = (f32[16,128]{1,0:T(8,128)S(1)}, f32[16,128]{1,0:T(8,128)S(1)}, u32[]{:S(2)}, u32[]{:S(2)}) collective-permute-start(f32[16,128]{1,0:T(8,128)S(1)} %get-tuple-element.21), channel_id=1, source_target_pairs={{0,28},{4,24},{8,20},{12,16},{16,12},{20,8},{24,4},{28,0},{1,29},{... | collective-permute-start | bytes 24584 | tf_op jit(solution)/shard_map/ppermute | solution.py:544
  6.3 0.0 collective-permute-start.1
  6.3 0.8 %collective-permute-start.4 = (f32[16,128]{1,0:T(8,128)S(1)}, f32[16,128]{1,0:T(8,128)S(1)}, u32[]{:S(2)}, u32[]{:S(2)}) collective-permute-start(f32[16,128]{1,0:T(8,128)S(1)} %get-tuple-element.22), channel_id=1, source_target_pairs={{0,20},{4,16},{8,28},{12,24},{16,4},{20,0},{24,12},{28,8},{1,21},{... | collective-permute-start | bytes 24584 | tf_op jit(solution)/shard_map/ppermute | solution.py:544
  7.1 0.0 collective-permute-start.3
  7.1 3.1 %collective-permute-done.2.xcross_ref = f32[16,128]{1,0:T(8,128)S(1)} collective-permute-done((f32[16,128]{1,0:T(8,128)S(1)}, f32[16,128]{1,0:T(8,128)S(1)}, u32[]{:S(2)}, u32[]{:S(2)}) %collective-permute-start.2) | collective-permute-done | bytes 8224 | tf_op jit(solution)/shard_map/ppermute | solution.py:544
  10.2 0.0 collective-permute-done.1.cross_ref
  10.2 0.0 collective-permute-done.4.xchip_ref
  10.2 0.0 collective-permute-done.3.chip_ref
  10.2 0.0 collective-permute-done.far_ref
  10.2 0.5 %shard_map.51 = (f32[4,64,128]{2,1,0:T(8,128)S(1)}, f32[136,256]{1,0:T(8,128)S(1)}, s32[72,256]{1,0:T(8,128)S(1)}) custom-call(f32[4,64,128]{2,1,0:T(8,128)S(1)} %get-tuple-element.19.s_ref, f32[328,128]{1,0:T(8,128)S(1)} %get-tuple-element.20.own_ref, f32[328,128]{1,0:T(8,128)S(1)} %collective-permute-done.far_ref, ...), custom_call_target="tpu_custom_call" | custom-call | tf_op jit(solution)/shard_map/pallas_call | solution.py:23
  10.7 1.4 %collective-permute-start.5 = (s32[72,256]{1,0:T(8,128)S(1)}, s32[72,256]{1,0:T(8,128)S(1)}, u32[]{:S(2)}, u32[]{:S(2)}) collective-permute-start(s32[72,256]{1,0:T(8,128)S(1)} %get-tuple-element.26), channel_id=1, source_target_pairs={{0,1},{1,0},{2,3},{3,2},{4,5},{5,4},{6,7},{7,6},{8,9},{9,8},{10,11... | collective-permute-start | bytes 221192 | tf_op jit(solution)/shard_map/ppermute | solution.py:560
  12.1 0.0 collective-permute-start.6
  12.1 1.6 %shard_map.52 = (f32[128,256]{1,0:T(8,128)S(1)}, f32[262,8,128]{2,1,0:T(8,128)S(1)}, f32[120,8,128]{2,1,0:T(8,128)S(1)}, f32[120,8,128]{2,1,0:T(8,128)S(1)}, f32...) custom-call(f32[136,256]{1,0:T(8,128)S(1)} %get-tuple-element.23.zm_ref), custom_call_target="tpu_custom_call" | custom-call | tf_op jit(solution)/shard_map/pallas_call | solution.py:23
  13.6 1.1 %collective-permute-done.5.got_ref.even_ref = s32[72,256]{1,0:T(8,128)S(1)} collective-permute-done((s32[72,256]{1,0:T(8,128)S(1)}, s32[72,256]{1,0:T(8,128)S(1)}, u32[]{:S(2)}, u32[]{:S(2)}) %collective-permute-start.5) | collective-permute-done | bytes 73760 | tf_op jit(solution)/shard_map/ppermute | solution.py:560
  14.8 0.7 %shard_map.53.acc_ref = f32[128,256]{1,0:T(8,128)S(1)} custom-call(f32[128,256]{1,0:T(8,128)S(1)} %get-tuple-element.24.acc_ref, f32[262,8,128]{2,1,0:T(8,128)S(1)} %get-tuple-element.25.table, f32[136,256]{1,0:T(8,128)S(1)} %get-tuple-element.23.zm_ref, s32[72,256]{1,0:T(8,128)S(1)} %collective-permute-done.5.got_ref.even_ref), custom_call_target="tpu_custom_call" | custom-call | tf_op jit(solution)/shard_map/pallas_call | solution.py:23
  15.5 0.4 %collective-permute-done.6.got_ref.odd_ref = s32[72,256]{1,0:T(8,128)S(1)} collective-permute-done((s32[72,256]{1,0:T(8,128)S(1)}, s32[72,256]{1,0:T(8,128)S(1)}, u32[]{:S(2)}, u32[]{:S(2)}) %collective-permute-start.6) | collective-permute-done | bytes 73760 | tf_op jit(solution)/shard_map/ppermute | solution.py:565
  15.9 0.8 %shard_map.54 = (f32[4,64,128]{2,1,0:T(8,128)S(1)}, s16[4,64,128]{2,1,0:T(8,128)(2,1)S(1)}) custom-call(f32[128,256]{1,0:T(8,128)S(1)} %shard_map.53.acc_ref, f32[262,8,128]{2,1,0:T(8,128)S(1)} %get-tuple-element.25.table, f32[136,256]{1,0:T(8,128)S(1)} %get-tuple-element.23.zm_ref, s32[72,256]{1,0:T(8,128)S(1)} %collective-permute-done.6.got_ref.odd_ref), custom_call_target="tpu_custom_call" | custom-call | tf_op jit(solution)/shard_map/pallas_call | solution.py:23
  16.7 0.9 %collective-permute-start.7 = (s16[4,64,128]{2,1,0:T(8,128)(2,1)S(1)}, s16[4,64,128]{2,1,0:T(8,128)(2,1)S(1)}, u32[]{:S(2)}, u32[]{:S(2)}) collective-permute-start(s16[4,64,128]{2,1,0:T(8,128)(2,1)S(1)} %get-tuple-element.28), channel_id=1, source_target_pairs={{0,4},{4,0},{8,12},{12,8},{1,5},{5,1},{9,13},{13,9},{2,6},{6,2},{1... | collective-permute-start | bytes 196616 | tf_op jit(solution)/shard_map/ppermute | solution.py:538
  17.7 1.1 %collective-permute-start.8 = (s16[4,64,128]{2,1,0:T(8,128)(2,1)S(1)}, s16[4,64,128]{2,1,0:T(8,128)(2,1)S(1)}, u32[]{:S(2)}, u32[]{:S(2)}) collective-permute-start(s16[4,64,128]{2,1,0:T(8,128)(2,1)S(1)} %get-tuple-element.28), channel_id=1, source_target_pairs={{0,8},{4,12},{8,0},{12,4},{1,9},{5,13},{9,1},{13,5},{2,10},{6,14},... | collective-permute-start | bytes 196616 | tf_op jit(solution)/shard_map/ppermute | solution.py:538
  18.8 0.6 %collective-permute-start.9 = (s16[4,64,128]{2,1,0:T(8,128)(2,1)S(1)}, s16[4,64,128]{2,1,0:T(8,128)(2,1)S(1)}, u32[]{:S(2)}, u32[]{:S(2)}) collective-permute-start(s16[4,64,128]{2,1,0:T(8,128)(2,1)S(1)} %get-tuple-element.28), channel_id=1, source_target_pairs={{0,16},{4,8},{8,4},{12,28},{16,0},{20,24},{24,20},{28,12},{1,17},{... | collective-permute-start | bytes 196616 | tf_op jit(solution)/shard_map/ppermute | solution.py:574
  19.4 0.0 collective-permute-done.7.code_ref
  19.4 1.3 %shard_map.55.start_ref = f32[4,64,128]{2,1,0:T(8,128)S(1)} custom-call(f32[4,64,128]{2,1,0:T(8,128)S(1)} %get-tuple-element.27.own_ref, s16[4,64,128]{2,1,0:T(8,128)(2,1)S(1)} %collective-permute-done.7.code_ref, f32[120,8,128]{2,1,0:T(8,128)S(1)} %get-tuple-element.29.table_0, f32[120,8,128]{2,1,0:T(8,128)S(1)} %get-tuple-element.30.table_1), custom_call_target="tpu_custom_call" | custom-call | tf_op jit(solution)/shard_map/pallas_call | solution.py:23
  20.7 0.6 %collective-permute-done.8.code_ref = s16[4,64,128]{2,1,0:T(8,128)(2,1)S(1)} collective-permute-done((s16[4,64,128]{2,1,0:T(8,128)(2,1)S(1)}, s16[4,64,128]{2,1,0:T(8,128)(2,1)S(1)}, u32[]{:S(2)}, u32[]{:S(2)}) %collective-permute-start.8) | collective-permute-done | bytes 65568 | tf_op jit(solution)/shard_map/ppermute | solution.py:538
  21.3 0.7 %shard_map.56._.start_ref = f32[4,64,128]{2,1,0:T(8,128)S(1)} custom-call(f32[4,64,128]{2,1,0:T(8,128)S(1)} %shard_map.55.start_ref, s16[4,64,128]{2,1,0:T(8,128)(2,1)S(1)} %collective-permute-done.8.code_ref, f32[120,8,128]{2,1,0:T(8,128)S(1)} %get-tuple-element.31.table), custom_call_target="tpu_custom_call" | custom-call | tf_op jit(solution)/shard_map/pallas_call | solution.py:23
  22.0 0.1 shard_map.57.score_ref
  22.1 0.6 %collective-permute-done.9.code_ref = s16[4,64,128]{2,1,0:T(8,128)(2,1)S(1)} collective-permute-done((s16[4,64,128]{2,1,0:T(8,128)(2,1)S(1)}, s16[4,64,128]{2,1,0:T(8,128)(2,1)S(1)}, u32[]{:S(2)}, u32[]{:S(2)}) %collective-permute-start.9) | collective-permute-done | bytes 65568 | tf_op jit(solution)/shard_map/ppermute | solution.py:574
  22.7 1.3 %shard_map.58 = (f32[4,64,128]{2,1,0:T(8,128)}, f32[4,64,128]{2,1,0:T(8,128)}) custom-call(f32[4,64,128]{2,1,0:T(8,128)S(1)} %shard_map.56._.start_ref, s16[4,64,128]{2,1,0:T(8,128)(2,1)S(1)} %collective-permute-done.9.code_ref, f32[120,8,128]{2,1,0:T(8,128)S(1)} %get-tuple-element.32.table, f32[4,64,128]{2,1,0:T(8,128)S(1)} %shard_map.57.score_ref), custom_call_target="tpu_custom_call" | custom-call | tf_op jit(solution)/shard_map/pallas_call | solution.py:23
Async XLA Ops:
  3.0 7.2 %collective-permute-start = (f32[328,128]{1,0:T(8,128)S(1)}, f32[328,128]{1,0:T(8,128)S(1)}, u32[]{:S(2)}, u32[]{:S(2)}) collective-permute-start(f32[328,128]{1,0:T(8,128)S(1)} %get-tuple-element.20.own_ref), channel_id=1, source_target_pairs={{0,16},{4,20},{8,24},{12,28},{16,0},{20,4},{24,8},{28,12},{1,17},{... | collective-permute-start | bytes 503816 | tf_op jit(solution)/shard_map/ppermute | solution.py:544
  3.3 6.9 %collective-permute-start.2 = (f32[16,128]{1,0:T(8,128)S(1)}, f32[16,128]{1,0:T(8,128)S(1)}, u32[]{:S(2)}, u32[]{:S(2)}) collective-permute-start(f32[16,128]{1,0:T(8,128)S(1)} %get-tuple-element.21), channel_id=1, source_target_pairs={{0,28},{4,24},{8,20},{12,16},{16,12},{20,8},{24,4},{28,0},{1,29},{... | collective-permute-start | bytes 24584 | tf_op jit(solution)/shard_map/ppermute | solution.py:544
  6.3 3.9 %collective-permute-start.1 = (f32[16,128]{1,0:T(8,128)S(1)}, f32[16,128]{1,0:T(8,128)S(1)}, u32[]{:S(2)}, u32[]{:S(2)}) collective-permute-start(f32[16,128]{1,0:T(8,128)S(1)} %get-tuple-element.21), channel_id=1, source_target_pairs={{0,12},{4,8},{8,4},{12,0},{16,28},{20,24},{24,20},{28,16},{1,13},{... | collective-permute-start | bytes 24584 | tf_op jit(solution)/shard_map/ppermute | solution.py:544
  6.3 3.9 %collective-permute-start.4 = (f32[16,128]{1,0:T(8,128)S(1)}, f32[16,128]{1,0:T(8,128)S(1)}, u32[]{:S(2)}, u32[]{:S(2)}) collective-permute-start(f32[16,128]{1,0:T(8,128)S(1)} %get-tuple-element.22), channel_id=1, source_target_pairs={{0,20},{4,16},{8,28},{12,24},{16,4},{20,0},{24,12},{28,8},{1,21},{... | collective-permute-start | bytes 24584 | tf_op jit(solution)/shard_map/ppermute | solution.py:544
  7.1 3.1 %collective-permute-start.3 = (f32[16,128]{1,0:T(8,128)S(1)}, f32[16,128]{1,0:T(8,128)S(1)}, u32[]{:S(2)}, u32[]{:S(2)}) collective-permute-start(f32[16,128]{1,0:T(8,128)S(1)} %get-tuple-element.22), channel_id=1, source_target_pairs={{0,4},{4,0},{8,12},{12,8},{16,20},{20,16},{24,28},{28,24},{1,5},{5... | collective-permute-start | bytes 24584 | tf_op jit(solution)/shard_map/ppermute | solution.py:544
  10.7 4.1 %collective-permute-start.5 = (s32[72,256]{1,0:T(8,128)S(1)}, s32[72,256]{1,0:T(8,128)S(1)}, u32[]{:S(2)}, u32[]{:S(2)}) collective-permute-start(s32[72,256]{1,0:T(8,128)S(1)} %get-tuple-element.26), channel_id=1, source_target_pairs={{0,1},{1,0},{2,3},{3,2},{4,5},{5,4},{6,7},{7,6},{8,9},{9,8},{10,11... | collective-permute-start | bytes 221192 | tf_op jit(solution)/shard_map/ppermute | solution.py:560
  12.1 3.8 %collective-permute-start.6 = (s32[72,256]{1,0:T(8,128)S(1)}, s32[72,256]{1,0:T(8,128)S(1)}, u32[]{:S(2)}, u32[]{:S(2)}) collective-permute-start(s32[72,256]{1,0:T(8,128)S(1)} %get-tuple-element.26), channel_id=1, source_target_pairs={{0,4},{1,2},{2,1},{3,7},{4,0},{5,6},{6,5},{7,3},{8,12},{9,10},{10,... | collective-permute-start | bytes 221192 | tf_op jit(solution)/shard_map/ppermute | solution.py:565
  16.7 2.7 %collective-permute-start.7 = (s16[4,64,128]{2,1,0:T(8,128)(2,1)S(1)}, s16[4,64,128]{2,1,0:T(8,128)(2,1)S(1)}, u32[]{:S(2)}, u32[]{:S(2)}) collective-permute-start(s16[4,64,128]{2,1,0:T(8,128)(2,1)S(1)} %get-tuple-element.28), channel_id=1, source_target_pairs={{0,4},{4,0},{8,12},{12,8},{1,5},{5,1},{9,13},{13,9},{2,6},{6,2},{1... | collective-permute-start | bytes 196616 | tf_op jit(solution)/shard_map/ppermute | solution.py:538
  17.7 3.7 %collective-permute-start.8 = (s16[4,64,128]{2,1,0:T(8,128)(2,1)S(1)}, s16[4,64,128]{2,1,0:T(8,128)(2,1)S(1)}, u32[]{:S(2)}, u32[]{:S(2)}) collective-permute-start(s16[4,64,128]{2,1,0:T(8,128)(2,1)S(1)} %get-tuple-element.28), channel_id=1, source_target_pairs={{0,8},{4,12},{8,0},{12,4},{1,9},{5,13},{9,1},{13,5},{2,10},{6,14},... | collective-permute-start | bytes 196616 | tf_op jit(solution)/shard_map/ppermute | solution.py:538
  18.8 4.0 %collective-permute-start.9 = (s16[4,64,128]{2,1,0:T(8,128)(2,1)S(1)}, s16[4,64,128]{2,1,0:T(8,128)(2,1)S(1)}, u32[]{:S(2)}, u32[]{:S(2)}) collective-permute-start(s16[4,64,128]{2,1,0:T(8,128)(2,1)S(1)} %get-tuple-element.28), channel_id=1, source_target_pairs={{0,16},{4,8},{8,4},{12,28},{16,0},{20,24},{24,20},{28,12},{1,17},{... | collective-permute-start | bytes 196616 | tf_op jit(solution)/shard_map/ppermute | solution.py:574
